TPU v7x, 32 devices: a whole 2x2x4 slice. The times are simulated.
32 devices in a mesh: dp: 32 (over z, y, x, core).
Axes of the slice: x: 2, y: 2, z: 4, core: 2. Of those that a mesh axis runs over, the one named last changes fastest.
Arguments:
- images: bfloat16 [512, 14, 14, 384], P('dp'), may hold values from -6 to 6
- mix_weight: float32 [512], P('dp'), may hold values from 0.5 to 1
- partner: int32 [512], P('dp'), may hold values from 0 to 511, as said below
- keep_mask: int32 [512], P('dp'), may hold values 0 or 1
- cotangent: bfloat16 [512, 7, 7, 768], P('dp'), may hold values from -6 to 6
- weight_in: float32 [1536, 384], P('dp')
- weight_out: float32 [1536, 384], P('dp')
- weight_down: float32 [1536, 768], P('dp'), may hold values from -0.15625 to 0.15625
- small_params: float32 [23808], P('dp')
- first_in: float32 [1536, 384], P('dp'), may hold values from -0.0009765625 to 0.0009765625
- second_in: float32 [1536, 384], P('dp'), may hold values from 4.196208e-10 to 1.6784832e-09
- first_out: float32 [1536, 384], P('dp'), may hold values from -0.0009765625 to 0.0009765625
- second_out: float32 [1536, 384], P('dp'), may hold values from 4.196208e-10 to 1.6784832e-09
- first_down: float32 [1536, 768], P('dp'), may hold values from -0.0009765625 to 0.0009765625
- second_down: float32 [1536, 768], P('dp'), may hold values from 4.196208e-10 to 1.6784832e-09
- first_small: float32 [23808], P('dp'), may hold values from -0.0009765625 to 0.0009765625
- second_small: float32 [23808], P('dp'), may hold values from 4.196208e-10 to 1.6784832e-09
Outputs:
- output: bfloat16 [512, 7, 7, 768], P('dp')
- images_grad: float32 [512, 14, 14, 384], P('dp')
- grad_norm: float32 [], replicated
- new_first_in: float32 [1536, 384], P('dp')
- new_second_in: float32 [1536, 384], P('dp')
- new_weight_in: float32 [1536, 384], P('dp')
- new_first_out: float32 [1536, 384], P('dp')
- new_second_out: float32 [1536, 384], P('dp')
- new_weight_out: float32 [1536, 384], P('dp')
- new_first_down: float32 [1536, 768], P('dp')
- new_second_down: float32 [1536, 768], P('dp')
- new_weight_down: float32 [1536, 768], P('dp')
- new_first_small: float32 [23808], P('dp')
- new_second_small: float32 [23808], P('dp')
- new_small_params: float32 [23808], P('dp')
Inputs may be any that keep to these rules, and one draw needn't show every extreme that they name: The partner of each image lies in the same aligned block of 16 images (one device's), and within each block the partners are a permutation of its images.
All inputs are finite; a program needn't handle non-finite values. No bound on the sum of `keep_mask` on one device may be relied on, other than what follows from the above.
Results may differ from a plain program's by a relative error of at most 0.0089.
Values may be sent and summed in bfloat16 or wider, within the bound.
No kernel may reach another device: no remote copies, remote signals or barrier semaphores. Data moves between devices by JAX's collectives and lax.ppermute only.
A program may use at most 192 MiB of HBM per device.

v0:
```python
import functools
import jax
import jax.numpy as jnp
import numpy as np
from jax import lax
from jax.experimental import pallas as pl
from jax.experimental.pallas import tpu as pltpu
from jax.sharding import PartitionSpec as P

STEP = 10
DROP_RATE = 0.2
RATE_MATRIX = 0.05
RATE_VECTOR = 0.3
LAYER_DECAY = 0.8
BETA_ONE = 0.9
BETA_TWO = 0.999
ADAM_EPS = 1e-08
WEIGHT_DECAY = 0.05
CLIP_NORM = 1.0
D = 384
FF = 1536
LN_EPS = 1e-06
F32 = jnp.float32
BF16 = jnp.bfloat16
VMEM = pl.BlockSpec(memory_space=pltpu.VMEM)
SMEM = pl.BlockSpec(memory_space=pltpu.SMEM)
HBM = pl.BlockSpec(memory_space=pltpu.HBM)
ANY = pl.BlockSpec(memory_space=pl.ANY)
ROWS = (((0,), (0,)), ((), ()))
COLS = (((1,), (1,)), ((), ()))
DEPTH_BIAS, GAIN_ONE, BIAS_ONE, HIDDEN_BIAS, OUT_BIAS, LAYER_SCALE, GAIN_TWO, BIAS_TWO, DOWN_BIAS = 49, 50, 51, 52, 56, 57, 58, 59, 60
SQUARES = 62
HALF_PIECES = 16


def near(shape, dtype):
    return jax.ShapeDtypeStruct(shape, dtype)


def far(shape, dtype):
    return pltpu.HBM(shape, dtype)


def held(x):
    return pltpu.with_memory_space_constraint(x, pltpu.HBM)


def dma(src, dst, sem):
    return pltpu.make_async_copy(src, dst, sem)


def start(copies):
    for copy in copies:
        copy.start()


def wait(copies):
    for copy in copies:
        copy.wait()


class Far:
    def __init__(self, array):
        self.array = array


def kernel_call(body, out, specs, scratch, args, after, us, mib, aliases=None):
    specs = specs + [HBM if isinstance(x, Far) else ANY for x in after]
    args = tuple(args) + tuple(x.array if isinstance(x, Far) else x for x in after)
    args = [held(x) if spec is HBM else x for spec, x in zip(specs, args)]
    return pl.pallas_call(
        body,
        out_shape=tuple(out),
        in_specs=specs,
        out_specs=tuple(HBM if isinstance(x, type(far((8, 128), F32))) else VMEM for x in out),
        scratch_shapes=scratch,
        input_output_aliases=aliases or {},
        cost_estimate=pl.CostEstimate(flops=int(us * 1e9), bytes_accessed=0, transcendentals=0),
        compiler_params=pltpu.CompilerParams(vmem_limit_bytes=mib << 20),
    )(*args)


def norm_of(v):
    c = v - jnp.mean(v, axis=-1, keepdims=True)
    inv = lax.rsqrt(jnp.mean(c * c, axis=-1, keepdims=True) + LN_EPS)
    return c * inv, inv


def norm_back(back, unit, inv, gain):
    scaled = back * gain
    m1 = jnp.mean(scaled, axis=-1, keepdims=True)
    m2 = jnp.mean(scaled * unit, axis=-1, keepdims=True)
    return inv * (scaled - m1 - unit * m2)


def tile_of(k, imgs):
    groups = imgs // 8
    return pl.ds(pl.multiple_of(k % groups * 8, 8), 8), pl.ds(pl.multiple_of(k // groups * 128, 128), 128)


def tiles(h, imgs, tile):
    count = imgs // 8 * (D // 128)
    if isinstance(h, int):
        return lax.fori_loop(0, count, tile, 0)
    for k in range(count):
        tile(k, 0)
    return 0


def every_row(begin, end, side, do):
    for h in range(begin, min(end, 3)):
        do(h, range(3 - h, 7))
    low, high = max(begin, 3), min(end, side - 3)
    if low < high:
        lax.fori_loop(low, high, lambda h, _: do(h, range(7)), 0)
    for h in range(max(begin, side - 3), end):
        do(h, range(side + 3 - h))


def conv_rows(src, sums, taps, h, kys, t, lanes, side, base):
    pairs = side // 2

    def one(ky, acc):
        u, v, w = list(acc[:pairs]), list(acc[pairs : 2 * pairs + 1]), list(acc[2 * pairs + 1 :])
        row = h + ky - 3
        for out, shift, first, count, read in (
            (u, 0, 4, 3, lambda i: src[row, 2 * i, t, lanes]),
            (v, -1, 0, 4, lambda i: src[row, 2 * i + 1, t, lanes]),
            (w, 0, 7, 4, lambda i: sums[row, i, t, lanes]),
        ):
            x = [read(i) for i in range(pairs)]
            for j in range(count):
                tap = taps[ky * 11 + first + j, :, lanes]
                for k in range(len(out)):
                    i = k + shift - 1 + j
                    if 0 <= i < pairs:
                        out[k] = out[k] + x[i] * tap
        return tuple(u + v + w)

    acc = (jnp.zeros((8, 128), F32),) * (3 * pairs + 1)
    for ky in kys:
        acc = one(ky, acc)
    u, v, w = acc[:pairs], acc[pairs : 2 * pairs + 1], acc[2 * pairs + 1 :]
    out = []
    for k in range(pairs):
        out.append(base[2 * k] + (u[k] + v[k]))
        out.append(base[2 * k + 1] + (w[k] - (u[k] + v[k + 1])))
    return out


def fill_taps(small_ref, taps, flip):
    for ky in range(7):
        rows = []
        for kx in range(7):
            k = 48 - (ky * 7 + kx) if flip else ky * 7 + kx
            rows.append(small_ref[k : k + 1, :])
        rows = rows[0::2] + rows[1::2] + [rows[2 * j] + rows[2 * j + 1] for j in range(3)] + [rows[6]]
        for k, value in enumerate(rows):
            taps[ky * 11 + k] = jnp.broadcast_to(value, (8, D))


def add_columns(src, sums, row):
    pairs = sums.shape[1]
    sums[row] = jnp.stack([src[row, 2 * i] + src[row, 2 * i + 1] for i in range(pairs)])


def spread(scalars_ref, rows_ref):
    for i in range(rows_ref.shape[0]):
        rows_ref[i : i + 1, :] = jnp.full((1, rows_ref.shape[1]), scalars_ref[i], F32)


def select(row_ref, sel_ref):
    imgs, wide = row_ref.shape
    lane = lax.broadcasted_iota(jnp.int32, (imgs, wide), 1)
    for w in range(wide // imgs):
        sel_ref[w * imgs : (w + 1) * imgs, :] = (lane == row_ref[...] + w * imgs).astype(F32).astype(BF16)


def conv_kernel(begin, end, fresh, *refs):
    if fresh:
        small_hbm, img_hbm, partner_ref, weight_ref = refs[:4]
        mixed_hbm, unit_hbm, inv_hbm, norm_hbm, token_ref, small_ref, mixed_ref, taps, conv_ref, unit_ref, inv_ref, norm_ref, sem, pair_sums, img_ref, mix_ref, row_ref, sel_ref = refs[-18:]
    else:
        small_hbm, mixed_hbm = refs[:2]
        unit_hbm, inv_hbm, norm_hbm, token_ref, small_ref, mixed_ref, taps, conv_ref, unit_ref, inv_ref, norm_ref, sem, pair_sums = refs[-13:]
    side, _, imgs, _ = mixed_ref.shape
    low = max(begin - 3, 0)
    high = side if fresh else min(end + 3, side)
    rows = end - begin
    load = dma(small_hbm, small_ref, sem.at[4, 0])
    load.start()
    token_ref[...] = jnp.zeros(token_ref.shape, F32)

    def enter(h):
        if fresh:
            return dma(img_hbm.at[h], img_ref.at[h], sem.at[3, h])
        return dma(mixed_hbm.at[h], mixed_ref.at[h], sem.at[3, h])

    def store(h):
        return dma(mixed_ref.at[h], mixed_hbm.at[h], sem.at[5, h])

    for h in range(low, high):
        enter(h).start()
    if fresh:
        spread(weight_ref, mix_ref)
        for i in range(imgs):
            row_ref[i : i + 1, :] = jnp.full((1, row_ref.shape[1]), lax.rem(partner_ref[i], imgs), jnp.int32)
        select(row_ref, sel_ref)
    load.wait()
    fill_taps(small_ref, taps, False)
    if fresh:
        mix = mix_ref[...][None]
        rest = 1.0 - mix

        def blend(h, _):
            enter(h).wait()
            x = img_ref[h].reshape(side * imgs, D)
            other = jnp.dot(sel_ref[...], x, preferred_element_type=F32).reshape(side, imgs, D)
            mixed_ref[h] = mix * x.reshape(side, imgs, D).astype(F32) + rest * other
            add_columns(mixed_ref, pair_sums, h)
            store(h).start()
            return 0

        lax.fori_loop(0, side, blend, 0)
    else:
        for h in range(low, min(begin + 3, high)):
            enter(h).wait()
            add_columns(mixed_ref, pair_sums, h)

    def conv(h, kys):
        r = h - begin
        if not fresh:

            @pl.when(h + 3 < high)
            def _():
                enter(h + 3).wait()
                add_columns(mixed_ref, pair_sums, h + 3)

        def tile(k, _):
            at, lanes = tile_of(k, imgs)
            base = jnp.broadcast_to(small_ref[DEPTH_BIAS : DEPTH_BIAS + 1, lanes], (8, 128))
            acc = conv_rows(mixed_ref, pair_sums, taps, h, kys, at, lanes, side, [base] * side)
            for w in range(side):
                conv_ref[r, w, at, lanes] = acc[w]
            return 0

        return tiles(h, imgs, tile)

    every_row(begin, end, side, conv)
    gain = small_ref[GAIN_ONE : GAIN_ONE + 1, :][None]
    bias = small_ref[BIAS_ONE : BIAS_ONE + 1, :][None]

    def leave(r):
        return (
            dma(unit_ref.at[r], unit_hbm.at[r + begin], sem.at[0, r]),
            dma(inv_ref.at[r], inv_hbm.at[r + begin], sem.at[1, r]),
            dma(norm_ref.at[r], norm_hbm.at[r + begin], sem.at[2, r]),
        )

    def norm(r):
        unit, inv = norm_of(conv_ref[r])
        unit_ref[r] = unit.astype(BF16)
        inv_ref[r] = inv
        norm_ref[r] = (unit * gain + bias).astype(BF16)
        start(leave(r))

    def two(i, _):
        norm(2 * i)
        norm(2 * i + 1)
        return 0

    lax.fori_loop(0, rows // 2, two, 0)
    if rows % 2:
        norm(rows - 1)
    for r in range(rows):
        wait(leave(r))
    if fresh:
        for h in range(side):
            store(h).wait()


def conv_forward(small, inputs, begin, end, so_far=(), after=()):
    fresh = not so_far
    full = inputs[0].shape
    side = full[0]
    thin = full[:3] + (1,)
    rows = end - begin
    out = [far(full, BF16), far(thin, F32), far(full, BF16), near((8, 128), F32)]
    scratch = [
        pltpu.VMEM(small.shape, F32),
        pltpu.VMEM(full, F32),
        pltpu.VMEM((77, 8, D), F32),
        pltpu.VMEM((rows,) + full[1:], F32),
        pltpu.VMEM((rows,) + full[1:], BF16),
        pltpu.VMEM((rows,) + thin[1:], F32),
        pltpu.VMEM((rows,) + full[1:], BF16),
        pltpu.SemaphoreType.DMA((6, side)),
        pltpu.VMEM((side, side // 2) + full[2:], F32),
    ]
    specs = [HBM] * 2
    if fresh:
        out = [far(full, F32)] + out
        wide = side * full[2]
        scratch += [pltpu.VMEM(full, BF16), pltpu.VMEM((full[2], D), F32), pltpu.VMEM((full[2], wide), jnp.int32), pltpu.VMEM((wide, wide), BF16)]
        specs = [HBM] * 2 + [SMEM] * 2
    return kernel_call(
        functools.partial(conv_kernel, begin, end, fresh),
        out,
        specs + [HBM] * len(so_far),
        scratch,
        (small,) + tuple(inputs) + tuple(so_far),
        after,
        21 * rows / side + 3 * fresh,
        36,
        {2 + k: k for k in range(len(so_far))},
    )


def home(me, order, j, chips):
    if order is None:
        return j % HALF_PIECES if chips else j
    device = me
    for k, bit in enumerate(order):
        device = device ^ (((j >> k) & 1) * bit)
    return device >> 1 if chips else device


def keep_rows(mask_ref, keep_ref):
    for i in range(keep_ref.shape[0]):
        keep_ref[i : i + 1, :] = jnp.full((1, D), mask_ref[i], jnp.int32).astype(F32) / (1.0 - DROP_RATE)


def assembly(me, order, chips, first, src_hbm, whole_ref, sem):
    deep = src_hbm.shape[0] // HALF_PIECES

    def copy(j, _):
        to = pl.ds(pl.multiple_of(home(me, order, first + j, chips) * deep, 16), deep)
        dma(src_hbm.at[pl.ds(pl.multiple_of(j * deep, 16), deep), :], whole_ref.at[to, :], sem).start()
        return 0

    lax.fori_loop(0, HALF_PIECES, copy, 0)
    return dma(src_hbm, whole_ref.at[pl.ds(0, src_hbm.shape[0]), :], sem)


def deal(me, order, chips, first, out_ref, read):
    deep = out_ref.shape[0] // HALF_PIECES

    def move(j, _):
        begin = pl.multiple_of(home(me, order, first + j, chips) * deep, 16)
        to = pl.ds(pl.multiple_of(j * deep, 16), deep)
        for g in range(out_ref.shape[1] // 128):
            out_ref[to, g * 128 : (g + 1) * 128] = read(pl.ds(begin, deep), g).astype(BF16)
        return 0

    lax.fori_loop(0, HALF_PIECES, move, 0)


def even_first(rows, deep):
    blocks = [rows[d * deep // D][:, d * deep % D : d * deep % D + deep] for d in range(FF // deep)]
    return jnp.concatenate(blocks[0::2] + blocks[1::2], axis=1)


def even_last(even, odd, k, deep):
    per = D // deep
    blocks = []
    for d in range(per * k, per * k + per):
        source = odd if d % 2 else even
        blocks.append(source[:, d // 2 * deep : d // 2 * deep + deep])
    return jnp.concatenate(blocks, axis=1)


def block_kernel(block, masks, me_ref, norm_hbm, mixed_hbm, pnear_hbm, pfar_hbm, wnear_hbm, wfar_hbm, dy_hbm, small_hbm, mask_ref, *rest):
    act_hbm, dg_hbm, gnear_ref, gfar_ref, gdb_ref, out_ref, bb_hbm, sums_ref, res_hbm = rest[-32:-23]
    pair_ref, small_ref, keep_ref, norm_ref, mixed_ref, act_ref, dg_ref, branch_ref, unit_ref, inv_ref, out2_ref = rest[-23:-12]
    wd_ref, dy_ref, bb_ref, res_ref, acc, wide, wk, isem, osem, wsem, bsem, rsem = rest[-12:]
    rows = norm_hbm.shape[0]
    steps = rows // block
    imgs = keep_ref.shape[0]
    shape = (block // imgs, imgs, D)
    half = dy_hbm.shape[0]

    def spot(i):
        return pl.ds(pl.multiple_of(i * block, block), block)

    def enter(i):
        s = i % 2
        return (
            dma(norm_hbm.at[spot(i), :], norm_ref.at[s], isem.at[0, s]),
            dma(mixed_hbm.at[spot(i), :], mixed_ref.at[s], isem.at[1, s]),
        )

    def leave(i):
        s = i % 2
        pairs = ((act_ref, act_hbm), (dg_ref, dg_hbm))
        return [dma(a.at[s], b.at[spot(i), :], osem.at[k, s]) for k, (a, b) in enumerate(pairs)]

    me = me_ref[0]
    p_masks, w_masks, d_masks = masks
    load = dma(small_hbm, small_ref, wsem.at[0])
    start(enter(0))
    load.start()
    half_rows = FF // 2
    mine = 0 if p_masks is None else me % 2
    pair_in = []
    for src, first, which in ((pnear_hbm, 0, mine), (pfar_hbm, HALF_PIECES, 1 - mine)):
        to = pair_ref.at[pl.ds(pl.multiple_of(which * half_rows, half_rows), half_rows), :]
        pair_in.append(assembly(me, p_masks, True, first, src, to, wsem.at[1]))
    dy_in = dma(dy_hbm, dy_ref, wsem.at[3])
    wait(pair_in)
    down_in = [
        assembly(me, w_masks, False, first, src, wd_ref, wsem.at[2]) for first, src in ((0, wnear_hbm), (HALF_PIECES, wfar_hbm))
    ]
    dy_in.start()
    load.wait()
    keep_rows(mask_ref, keep_ref)
    keep = keep_ref[...][None]
    scale = keep * small_ref[LAYER_SCALE : LAYER_SCALE + 1, :][None]
    gain = small_ref[GAIN_TWO : GAIN_TWO + 1, :][None]
    bias = small_ref[BIAS_TWO : BIAS_TWO + 1, :][None]
    bias_rows = [small_ref[HIDDEN_BIAS + k : HIDDEN_BIAS + k + 1, :] for k in range(FF // D)]
    hidden_bias = jnp.concatenate(bias_rows, axis=1) if p_masks is None else even_first(bias_rows, FF >> len(p_masks))
    chunk = FF // 2

    def body(i, _):
        s = i % 2

        @pl.when(i + 1 < steps)
        def _():
            start(enter(i + 1))

        @pl.when(i >= 2)
        def _():
            wait(leave(i - 2))

        wait(enter(i))
        x = norm_ref[s]
        branch = jnp.broadcast_to(small_ref[OUT_BIAS : OUT_BIAS + 1, :], (block, D))

        def hidden(j):
            cols = slice(j * chunk, (j + 1) * chunk)
            return lax.dot_general(x, pair_ref[cols, :D], COLS, preferred_element_type=F32) + hidden_bias[:, cols]

        pre = hidden(0)
        for j in range(FF // chunk):
            after = hidden(j + 1) if j + 1 < FF // chunk else None
            cols = slice(j * chunk, (j + 1) * chunk)
            phi = 0.5 + 0.5 * lax.erf(pre * 0.7071067811865476)
            bell = jnp.exp2(pre * pre * -0.7213475204444817) * 0.3989422804014327
            act = (pre * phi).astype(BF16)
            act_ref[s, :, cols] = act
            dg_ref[s, :, cols] = (phi + pre * bell).astype(BF16)
            branch = branch + jnp.dot(act, pair_ref[cols, D:], preferred_element_type=F32)
            pre = after
        start(leave(i))
        split = branch_ref.shape[1:]
        branch_ref[i] = branch.astype(BF16).reshape(split)
        unit, inv = norm_of(mixed_ref[s].reshape(shape) + scale * branch.reshape(shape))
        unit_ref[i] = unit.astype(BF16).reshape(split)
        inv_ref[i] = inv.reshape(split[:-1] + (1,))
        out2_ref[i] = (unit * gain + bias).astype(BF16).reshape(split)
        return 0

    lax.fori_loop(0, steps, body, 0)

    wait(down_in)
    for g in range(6):
        wide[g] = wd_ref[:, pl.ds(g * 128, 128)].astype(F32)
        for k in range(4):
            wk[k, :, pl.ds(g * 128, 128)] = wide[g, pl.ds(k, D, stride=4), :].astype(BF16)
    sums_ref[...] = jnp.zeros(sums_ref.shape, F32)
    rows = half * half * imgs
    shape = (half * half, imgs, D)
    for k in range(2):
        acc[:, k * D : (k + 1) * D] = jnp.broadcast_to(small_ref[DOWN_BIAS + k : DOWN_BIAS + k + 1, :], (rows, D))
    dy_in.wait()
    gdb_ref[...] = jnp.sum(dy_ref[...].astype(F32).reshape(half * half, imgs, 2 * D), axis=0)

    def give(k):
        pairs = ((bb_ref, bb_hbm), (res_ref, res_hbm))
        return [dma(a.at[k], b.at[:, k // 2, :, k % 2], rsem.at[j, k]) for j, (a, b) in enumerate(pairs)]

    def quarter(k):
        dy = dy_ref[...].reshape(rows, 2 * D)
        x = out2_ref[:, k // 2, :, k % 2].reshape(rows, D)
        back = lax.dot_general(dy, wk[k], COLS, preferred_element_type=F32).reshape(shape)
        acc[...] += jnp.dot(x, wk[k], preferred_element_type=F32)
        gd = lax.dot_general(x, dy, ROWS, preferred_element_type=F32)
        for g in range(6):
            wide[g, pl.ds(k, D, stride=4), :] = gd[:, g * 128 : (g + 1) * 128]
        unit = unit_ref[:, k // 2, :, k % 2].reshape(shape).astype(F32)
        sums_ref[0] += jnp.sum(back * unit, axis=0)
        sums_ref[1] += jnp.sum(back, axis=0)
        res = norm_back(back, unit, inv_ref[:, k // 2, :, k % 2].reshape(half * half, imgs, 1), gain)
        res_ref[k] = res.astype(BF16).reshape(half, half, imgs, D)
        sums_ref[2] += jnp.sum(res * keep * branch_ref[:, k // 2, :, k % 2].reshape(shape).astype(F32), axis=0)
        bb = (res * scale).astype(BF16)
        bb_ref[k] = bb.reshape(half, half, imgs, D)
        start(give(k))
        sums_ref[3] += jnp.sum(bb.astype(F32), axis=0)

    def half_of(a, _):
        quarter(2 * a)
        quarter(2 * a + 1)
        return 0

    lax.fori_loop(0, 2, half_of, 0)
    out_ref[...] = acc[...].astype(BF16).reshape(out_ref.shape)
    deal(me, d_masks, False, 0, gnear_ref, lambda at, g: wide[g, at, :])
    deal(me, d_masks, False, HALF_PIECES, gfar_ref, lambda at, g: wide[g, at, :])
    for k in range(4):
        wait(give(k))
    for i in range(max(steps - 2, 0), steps):
        wait(leave(i))


def block_both(masks, me, norm, mixed, pair, down, dy, small, mask, after=(), block=448):
    rows = norm.shape[0]
    half, _, imgs, _ = dy.shape
    area = half * half * imgs
    six = (half, 2, half, 2, imgs)
    two = lambda width, dtype: pltpu.VMEM((2, block, width), dtype)
    whole = lambda width, dtype: pltpu.VMEM(six + (width,), dtype)
    part = pltpu.VMEM((4, half, half, imgs, D), BF16)
    return kernel_call(
        functools.partial(block_kernel, block, masks),
        [far((rows, FF), BF16)] * 2
        + [near((2 * D, 2 * D), BF16)] * 2
        + [near((imgs, 2 * D), F32), near((half, half, imgs, 2 * D), BF16)]
        + [far(six + (D,), BF16), near((4, imgs, D), F32), far(six + (D,), BF16)],
        [SMEM] + [HBM] * 2 + [ANY, HBM] * 2 + [HBM] * 2 + [SMEM],
        [pltpu.VMEM((FF, 2 * D), BF16), pltpu.VMEM(small.shape, F32), pltpu.VMEM((imgs, D), F32)]
        + [two(D, BF16), two(D, F32), two(FF, BF16), two(FF, BF16)]
        + [whole(D, BF16), whole(D, BF16), whole(1, F32), whole(D, BF16)]
        + [pltpu.VMEM((4 * D, 2 * D), BF16), pltpu.VMEM(dy.shape, BF16), part, part]
        + [pltpu.VMEM((area, 2 * D), F32), pltpu.VMEM((6, 4 * D, 128), F32), pltpu.VMEM((4, D, 2 * D), BF16)]
        + [pltpu.SemaphoreType.DMA((2, 2)), pltpu.SemaphoreType.DMA((2, 2)), pltpu.SemaphoreType.DMA((4,))]
        + [pltpu.SemaphoreType.DMA((1,)), pltpu.SemaphoreType.DMA((2, 4))],
        (me, norm, mixed, *pair, *down, dy, small, mask),
        after,
        34,
        58,
    )


def pair_grad_kernel(block, first, masks, me_ref, bb_hbm, act_hbm, dg_hbm, norm_hbm, pair_hbm, *rest):
    g_ref, hb_ref, p_hbm, pair_ref, acc, bb_ref, act_ref, dg_ref, norm_ref, p_ref, sem, osem, wsem = rest[-13:]
    rows = bb_hbm.shape[0]
    imgs = hb_ref.shape[0]
    steps = rows // block
    wide = FF // 2
    me = me_ref[0]
    which = 0 if masks is None else me % 2
    which = 1 - which if first else which
    lanes = pl.ds(pl.multiple_of(which * wide, wide), wide)

    def spot(i):
        return pl.ds(pl.multiple_of(i * block, block), block)

    def enter(i):
        s = i % 2
        return (
            dma(bb_hbm.at[spot(i), :], bb_ref.at[s], sem.at[0, s]),
            dma(dg_hbm.at[spot(i), lanes], dg_ref.at[s], sem.at[1, s]),
            dma(act_hbm.at[spot(i), lanes], act_ref.at[s], sem.at[2, s]),
            dma(norm_hbm.at[spot(i), :], norm_ref.at[s], sem.at[3, s]),
        )

    def leave(i):
        return dma(p_ref.at[i % 2], p_hbm.at[spot(i), :], osem.at[i % 2])

    pair_in = [assembly(me, masks, True, first, pair_hbm, pair_ref, wsem.at[0])]
    start(enter(0))
    hb_ref[...] = jnp.zeros(hb_ref.shape, F32)
    acc[...] = jnp.zeros(acc.shape, F32)
    wait(pair_in)

    def body(i, _):
        s = i % 2

        @pl.when(i + 1 < steps)
        def _():
            start(enter(i + 1))

        @pl.when(i >= 2)
        def _():
            leave(i - 2).wait()

        wait(enter(i))
        b = bb_ref[s]
        back = lax.dot_general(b, pair_ref[:, D:], COLS, preferred_element_type=F32)
        acc[:, D:] += lax.dot_general(act_ref[s], b, ROWS, preferred_element_type=F32)
        p = (back * dg_ref[s].astype(F32)).astype(BF16)
        p_ref[s] = p
        hb_ref[...] += jnp.sum(p.astype(F32).reshape(block // imgs, imgs, wide), axis=0)
        acc[:, :D] += lax.dot_general(p, norm_ref[s], ROWS, preferred_element_type=F32)
        leave(i).start()
        return 0

    lax.fori_loop(0, steps, body, 0)
    deal(me, masks, True, first, g_ref, lambda at, g: acc[at, pl.ds(g * 128, 128)])
    for i in range(max(steps - 2, 0), steps):
        leave(i).wait()


def pair_grad(first, masks, me, bb, act, dg, norm, pair, imgs, after=(), block=448):
    rows = bb.shape[0]
    wide = FF // 2
    two = lambda width: pltpu.VMEM((2, block, width), BF16)
    return kernel_call(
        functools.partial(pair_grad_kernel, block, first, masks),
        [near((wide, 2 * D), BF16), near((imgs, wide), F32), far((rows, wide), BF16)],
        [SMEM] + [HBM] * 5,
        [pltpu.VMEM((wide, 2 * D), BF16), pltpu.VMEM((wide, 2 * D), F32)]
        + [two(D), two(wide), two(wide), two(D), two(wide)]
        + [pltpu.SemaphoreType.DMA((4, 2)), pltpu.SemaphoreType.DMA((2,)), pltpu.SemaphoreType.DMA((1,))],
        (me, bb, act, dg, norm, pair),
        after,
        13,
        28,
    )


def back_one_kernel(block, masks, me_ref, pnear_hbm, pfar_hbm, unit_hbm, inv_hbm, near_hbm, far_hbm, small_hbm, *rest):
    conv_hbm, sums_ref, near_ref, far_ref, small_ref, pnear_ref, pfar_ref, unit_ref, inv_ref, conv_ref, sem, wsem = rest[-12:]
    rows = pnear_hbm.shape[0]
    imgs = sums_ref.shape[1]
    steps = rows // block
    shape = (block // imgs, imgs, D)

    def spot(i):
        return pl.ds(pl.multiple_of(i * block, block), block)

    def enter(i):
        s = i % 2
        pairs = ((pnear_hbm, pnear_ref), (pfar_hbm, pfar_ref), (unit_hbm, unit_ref), (inv_hbm, inv_ref))
        return [dma(a.at[spot(i), :], b.at[s], sem.at[k, s]) for k, (a, b) in enumerate(pairs)]

    def leave(i):
        return dma(conv_ref.at[i % 2], conv_hbm.at[spot(i), :], sem.at[4, i % 2])

    load = dma(small_hbm, small_ref, wsem.at[0])
    left = pl.ds(0, D)
    pair_in = [
        assembly(me_ref[0], masks, True, first, src.at[:, left], dst, wsem.at[1])
        for first, src, dst in ((0, near_hbm, near_ref), (HALF_PIECES, far_hbm, far_ref))
    ]
    start(enter(0))
    load.start()
    sums_ref[...] = jnp.zeros(sums_ref.shape, F32)
    wait(pair_in)
    load.wait()
    gain = small_ref[GAIN_ONE : GAIN_ONE + 1, :][None]

    def body(i, _):
        s = i % 2

        @pl.when(i + 1 < steps)
        def _():
            start(enter(i + 1))

        @pl.when(i >= 2)
        def _():
            leave(i - 2).wait()

        wait(enter(i))
        back = jnp.dot(pnear_ref[s], near_ref[...], preferred_element_type=F32)
        back = (back + jnp.dot(pfar_ref[s], far_ref[...], preferred_element_type=F32)).reshape(shape)
        unit = unit_ref[s].reshape(shape).astype(F32)
        sums_ref[0] += jnp.sum(back * unit, axis=0)
        sums_ref[1] += jnp.sum(back, axis=0)
        out = norm_back(back, unit, inv_ref[s].reshape(shape[:2] + (1,)), gain)
        sums_ref[2] += jnp.sum(out, axis=0)
        conv_ref[s] = out.astype(BF16).reshape(block, D)
        leave(i).start()
        return 0

    lax.fori_loop(0, steps, body, 0)
    for i in range(max(steps - 2, 0), steps):
        leave(i).wait()


def back_one(masks, me, p, unit, inv, pair, small, imgs, after=(), block=784):
    rows = unit.shape[0]
    wide = FF // 2
    two = lambda width, dtype: pltpu.VMEM((2, block, width), dtype)
    return kernel_call(
        functools.partial(back_one_kernel, block, masks),
        [far((rows, D), BF16), near((3, imgs, D), F32)],
        [SMEM] + [HBM] * 7,
        [pltpu.VMEM((wide, D), BF16)] * 2
        + [pltpu.VMEM(small.shape, F32)]
        + [two(wide, BF16), two(wide, BF16), two(D, BF16), two(1, F32), two(D, BF16)]
        + [pltpu.SemaphoreType.DMA((5, 2)), pltpu.SemaphoreType.DMA((2,))],
        (me, *p, unit, inv, *pair, small),
        after,
        11,
        32,
    )


def taps_kernel(groups, conv_hbm, mixed_hbm, *rest):
    g_ref, conv_ref, mixed_ref, sums, even, odd, last, sem = rest[-8:]
    side, _, imgs, _ = conv_hbm.shape
    pairs = side // 2

    def enter(k):
        lanes = pl.ds(pl.multiple_of((k + groups[0]) * 128, 128), 128)
        return (
            dma(mixed_hbm.at[:, :, :, lanes], mixed_ref.at[k], sem.at[0, k]),
            dma(conv_hbm.at[:, :, :, lanes], conv_ref.at[k], sem.at[1, k]),
        )

    for k in range(len(groups)):
        start(enter(k))
    def group(k, _):
        wait(enter(k))

        def prepare(h, _):
            x = [mixed_ref[k, h, w] for w in range(side)]
            d = [conv_ref[k, h, w].astype(F32) for w in range(side)]
            for i in range(pairs):
                sums[h, i] = x[2 * i] + x[2 * i + 1]
                last[h, i] = d[2 * i + 1]
                even[h, i] = d[2 * i] - d[2 * i + 1]
                odd[h, i + 1] = (d[2 * i + 2] if i + 1 < pairs else jnp.zeros_like(d[0])) - d[2 * i + 1]
            odd[h, 0] = d[0]
            return 0

        lax.fori_loop(0, side, prepare, 0)
        for ky in range(7):
            first = max(3 - ky, 0)
            count = min(side, side + 3 - ky) - first

            def row(h, acc):
                acc = list(acc)
                for t in range(imgs // 8):
                    at = pl.ds(t * 8, 8)
                    for begin, shift, taps, length, read_x, read_d in (
                        (4, 0, 3, pairs, lambda i: mixed_ref[k, h + ky - 3, 2 * i, at], lambda i: even[h, i, at]),
                        (0, -1, 4, pairs + 1, lambda i: mixed_ref[k, h + ky - 3, 2 * i + 1, at], lambda i: odd[h, i, at]),
                        (7, 0, 4, pairs, lambda i: sums[h + ky - 3, i, at], lambda i: last[h, i, at]),
                    ):
                        x = [read_x(i) for i in range(pairs)]
                        for a in range(length):
                            d = read_d(a)
                            for j in range(taps):
                                i = a + shift - 1 + j
                                if 0 <= i < pairs:
                                    acc[begin + j] = acc[begin + j] + x[i] * d
                return tuple(acc)

            acc = lax.fori_loop(
                0, count // 2, lambda r, acc: row(first + 2 * r + 1, row(first + 2 * r, acc)), (jnp.zeros((8, 128), F32),) * 11
            )
            if count % 2:
                acc = row(first + count - 1, acc)
            even_taps = [acc[j] + acc[7 + j] for j in range(4)]
            odd_taps = [acc[4 + j] + acc[7 + j] for j in range(3)]
            for kx in range(7):
                value = odd_taps[kx // 2] if kx % 2 else even_taps[kx // 2]
                g_ref[ky * 7 + kx, :, pl.ds(pl.multiple_of(k * 128, 128), 128)] = value
        return 0

    lax.fori_loop(0, len(groups), group, 0)


def taps_grad(conv, mixed, groups, after=()):
    side, _, imgs, _ = conv.shape
    lanes = lambda dtype: pltpu.VMEM((len(groups),) + conv.shape[:3] + (128,), dtype)
    part = lambda columns: pltpu.VMEM((side, columns, imgs, 128), F32)
    return kernel_call(
        functools.partial(taps_kernel, groups),
        [near((49, 8, 128 * len(groups)), F32)],
        [HBM] * 2,
        [lanes(BF16), lanes(F32), part(side // 2), part(side // 2), part(side // 2 + 1), part(side // 2), pltpu.SemaphoreType.DMA((2, len(groups)))],
        (conv, mixed),
        after,
        4.7 * len(groups),
        28,
    )[0]


def images_kernel(begin, end, conv_hbm, small_hbm, partner_ref, weight_ref, res_hbm, *rest):
    g_hbm, token_ref, small_ref, raw_ref, conv_ref, taps, res_ref, out_ref, mix_ref, row_ref, sel_ref, rest_ref, sem, csem, pair_sums = rest[-15:]
    side, _, imgs, _ = conv_hbm.shape
    low = max(begin - 3, 0)
    high = min(end + 3, side)
    load = dma(small_hbm, small_ref, csem.at[side])
    load.start()
    token_ref[...] = jnp.zeros(token_ref.shape, F32)

    def bring(h):
        return dma(conv_hbm.at[h], raw_ref.at[h], csem.at[h])

    def widen(h):
        bring(h).wait()
        conv_ref[h] = raw_ref[h].astype(F32)
        add_columns(conv_ref, pair_sums, h)

    def enter(h):
        return dma(res_hbm.at[h], res_ref.at[h % 2], sem.at[0, h % 2])

    def leave(h):
        return dma(out_ref.at[h - begin], g_hbm.at[h], sem.at[1, 0])

    for h in range(low, high):
        bring(h).start()
        if h == min(begin + 3, high - 1):
            enter(begin).start()
    spread(weight_ref, mix_ref)
    for i in range(imgs):
        row_ref[pl.ds(lax.rem(partner_ref[i], imgs), 1), :] = jnp.full((1, row_ref.shape[1]), i, jnp.int32)
    select(row_ref, sel_ref)
    load.wait()
    fill_taps(small_ref, taps, True)
    mix = mix_ref[...][None]
    others = 1.0 - mix
    for h in range(low, min(begin + 3, high)):
        widen(h)

    def row(h, kys):
        s = h % 2

        @pl.when(h + 1 < end)
        def _():
            enter(h + 1).start()

        @pl.when(h + 3 < high)
        def _():
            widen(h + 3)

        enter(h).wait()
        rest_ref[...] = res_ref[s].astype(F32)
        def tile(k, _):
            at, lanes = tile_of(k, imgs)
            base = [rest_ref[w, at, lanes] for w in range(side)]
            acc = conv_rows(conv_ref, pair_sums, taps, h, kys, at, lanes, side, base)
            for w in range(side):
                out_ref[h - begin, w, at, lanes] = acc[w]
            return 0

        return tiles(h, imgs, tile)

    every_row(begin, end, side, row)
    def unmix(r):
        v = out_ref[r]
        part = (others * v).reshape(side * imgs, D)
        upper = part.astype(BF16)
        lower = (part - upper.astype(F32)).astype(BF16)
        back = jnp.dot(sel_ref[...], upper, preferred_element_type=F32)
        back = back + jnp.dot(sel_ref[...], lower, preferred_element_type=F32)
        out_ref[r] = mix * v + back.reshape(side, imgs, D)
        leave(begin + r).start()

    for r in range(end - begin):
        unmix(r)
    for h in range(begin, end):
        leave(h).wait()


def images_back(conv, small, partner, weight, res, begin, end, so_far=(), after=()):
    side, _, imgs, _ = conv.shape
    return kernel_call(
        functools.partial(images_kernel, begin, end),
        [far(conv.shape, F32), near((8, 128), F32)],
        [HBM, HBM, SMEM, SMEM, HBM] + [HBM] * len(so_far),
        [
            pltpu.VMEM(small.shape, F32),
            pltpu.VMEM(conv.shape, BF16),
            pltpu.VMEM(conv.shape, F32),
            pltpu.VMEM((77, 8, D), F32),
            pltpu.VMEM((2, side, imgs, D), BF16),
            pltpu.VMEM((end - begin, side, imgs, D), F32),
            pltpu.VMEM((imgs, D), F32),
            pltpu.VMEM((imgs, side * imgs), jnp.int32),
            pltpu.VMEM((side * imgs, side * imgs), BF16),
            pltpu.VMEM((side, imgs, D), F32),
            pltpu.SemaphoreType.DMA((2, 2)),
            pltpu.SemaphoreType.DMA((side + 1,)),
            pltpu.VMEM((side, side // 2, imgs, D), F32),
        ],
        (conv, small, partner, weight, res) + tuple(so_far),
        after,
        22 * (end - begin) / side,
        28,
        {5: 0} if so_far else {},
    )


def ready_kernel(in_hbm, out_hbm, down_hbm, *rest):
    pair_ref, low_ref, in_ref, out_ref, down_ref, sem = rest[-6:]
    pairs = ((in_hbm, in_ref), (out_hbm, out_ref), (down_hbm, down_ref))
    copies = [dma(a, b, sem.at[k]) for k, (a, b) in enumerate(pairs)]
    start(copies)
    wait(copies)
    pair_ref[0, :, :D] = in_ref[...].astype(BF16)
    pair_ref[0, :, D:] = out_ref[...].astype(BF16)
    low_ref[0] = down_ref[...].astype(BF16)


def ready(weight_in, weight_out, weight_down, after=()):
    deep = weight_in.shape[0]
    return kernel_call(
        ready_kernel,
        [near((1, deep, 2 * D), BF16)] * 2,
        [HBM] * 3,
        [pltpu.VMEM(x.shape, F32) for x in (weight_in, weight_out, weight_down)] + [pltpu.SemaphoreType.DMA((3,))],
        (weight_in, weight_out, weight_down),
        after,
        0.5,
        8,
    )


def join_kernel(first_ref, second_ref, *rest):
    out_ref = rest[-1]
    k = first_ref.shape[0]
    out_ref[:k] = first_ref[...]
    out_ref[k:] = second_ref[...]


def join(first, second, after=()):
    return kernel_call(
        join_kernel,
        [near((2 * first.shape[0],) + first.shape[1:], first.dtype)],
        [VMEM] * 2,
        [],
        (first, second),
        after,
        0.5,
        8,
    )[0]


def fold_kernel(count, *refs):
    ins, (stay_ref, leave_ref) = refs[: 2 * count], refs[-2:]
    k = stay_ref.shape[0] // count
    for i in range(count):
        keep_ref, come_ref = ins[2 * i], ins[2 * i + 1]
        stay_ref[i * k : (i + 1) * k] = keep_ref[:k].astype(F32) + come_ref[:k].astype(F32)
        leave_ref[i * k : (i + 1) * k] = (keep_ref[k:].astype(F32) + come_ref[k:].astype(F32)).astype(BF16)


def fold(*arrays, after=()):
    slots, deep, wide = arrays[0].shape
    count = len(arrays) // 2
    return kernel_call(
        functools.partial(fold_kernel, count),
        [near((count * slots // 2, deep, wide), F32), near((count * slots // 2, deep, wide), BF16)],
        [VMEM] * len(arrays),
        [],
        arrays,
        after,
        0.5,
        12,
    )


def small_kernel(hops, me_ref, gk_ref, sums1_ref, sums2_ref, near_ref, far_ref, db_ref, keep_ref, come_ref, sum_ref, send_ref, total):
    grads = keep_ref[...] + come_ref[...].astype(F32)
    sum_ref[...] = grads
    rows = lambda x: jnp.sum(x, axis=0, keepdims=True)
    for t in range(49):
        total[t : t + 1, :] = rows(gk_ref[t])
    for row, value in (
        (DEPTH_BIAS, sums1_ref[2]),
        (GAIN_ONE, sums1_ref[0]),
        (BIAS_ONE, sums1_ref[1]),
        (OUT_BIAS, sums2_ref[3]),
        (LAYER_SCALE, sums2_ref[2]),
        (GAIN_TWO, sums2_ref[0]),
        (BIAS_TWO, sums2_ref[1]),
    ):
        total[row : row + 1, :] = rows(value)
    mine, other = rows(near_ref[...]), rows(far_ref[...])
    if hops:
        odd_device = (me_ref[0] % 2).astype(F32)
        even = mine * (1.0 - odd_device) + other * odd_device
        odd = other * (1.0 - odd_device) + mine * odd_device
    for k in range(4):
        if hops:
            value = even_last(even, odd, k, FF // hops)
        else:
            value = (mine, other)[k // 2][:, k % 2 * D : k % 2 * D + D]
        total[HIDDEN_BIAS + k : HIDDEN_BIAS + k + 1, :] = value
    for k in range(2):
        total[DOWN_BIAS + k : DOWN_BIAS + k + 1, :] = rows(db_ref[:, k * D : (k + 1) * D])
    square = jnp.full((1, D), jnp.sum(grads * grads), F32)
    upper = square.astype(BF16).astype(F32)
    total[SQUARES : SQUARES + 1, :] = upper
    total[SQUARES + 1 : SQUARES + 2, :] = square - upper
    send_ref[...] = total[...].astype(BF16)


def small_total(hops, me, gk, sums1, sums2, near_hb, far_hb, db, keep, come):
    return kernel_call(
        functools.partial(small_kernel, hops),
        [near(keep.shape, F32), near((SQUARES + 2, D), BF16)],
        [SMEM] + [VMEM] * 8,
        [pltpu.VMEM((SQUARES + 2, D), F32)],
        (me, gk, sums1, sums2, near_hb, far_hb, db, keep, come),
        (),
        1,
        8,
    )


def meet_kernel(*refs):
    arrays, out_ref = refs[:-1], refs[-1]
    sums = [x[...].astype(F32) for x in arrays]
    while len(sums) > 1:
        sums = [a + b for a, b in zip(sums[::2], sums[1::2])]
    total = sums[0]
    square = total[SQUARES : SQUARES + 1] + total[SQUARES + 1 : SQUARES + 2]
    upper = square.astype(BF16).astype(F32)
    out_ref[...] = total.astype(out_ref.dtype)
    out_ref[SQUARES : SQUARES + 2, :] = jnp.concatenate([upper, square - upper], axis=0).astype(out_ref.dtype)


def meet(arrays, dtype):
    return kernel_call(meet_kernel, [near(arrays[0].shape, dtype)], [VMEM] * len(arrays), [], arrays, (), 0.3, 8)[0]


def adam(weight, first, second, grad, rate, decay):
    first = BETA_ONE * first + (1.0 - BETA_ONE) * grad
    second = BETA_TWO * second + (1.0 - BETA_TWO) * grad * grad
    first_hat = first / (1.0 - BETA_ONE**STEP)
    second_hat = second / (1.0 - BETA_TWO**STEP)
    weight = weight - rate * (first_hat / (jnp.sqrt(second_hat) + ADAM_EPS) + decay * weight)
    return first, second, weight


def adam_kernel(total_ref, grads_ref, *refs):
    ins, outs = refs[:9], refs[9:18]
    norm_ref = refs[18]
    gs = total_ref[:SQUARES]
    norm = jnp.sqrt(jnp.sum(gs * gs) + jnp.sum(total_ref[SQUARES : SQUARES + 2, 0:1]))
    norm_ref[0, 0] = norm
    factor = CLIP_NORM / jnp.maximum(norm, CLIP_NORM)
    grads = (grads_ref[0, :, :D], grads_ref[0, :, D:], grads_ref[1])
    rates = (LAYER_DECAY * RATE_MATRIX, LAYER_DECAY * RATE_MATRIX, RATE_MATRIX)
    for k in range(3):
        new = adam(ins[3 * k][...], ins[3 * k + 1][...], ins[3 * k + 2][...], grads[k] * factor, rates[k], WEIGHT_DECAY)
        for out_ref, value in zip(outs[3 * k : 3 * k + 3], new):
            out_ref[...] = value


def adam_all(total, grads, states):
    return pl.pallas_call(
        adam_kernel,
        out_shape=tuple(near(x.shape, F32) for x in states) + (near((1, 1), F32),),
        in_specs=[VMEM] * 11,
        out_specs=(VMEM,) * 9 + (SMEM,),
        cost_estimate=pl.CostEstimate(flops=int(2e9), bytes_accessed=0, transcendentals=0),
        compiler_params=pltpu.CompilerParams(vmem_limit_bytes=12 << 20),
    )(total, grads, *states)


def swap(x, bit, n):
    return lax.ppermute(x, "dp", [(i, i ^ bit) for i in range(n)])


def is_set(bit):
    return (lax.axis_index("dp") & bit) != 0


def gather_natural(shard, n, order, gates=None):
    have = shard
    met = []
    for hop, bit in enumerate(order):
        if gates and hop in gates:
            have, _ = lax.optimization_barrier((have, gates[hop]))
        other = swap(have, bit, n)
        axis = sum(1 for b in met if b > bit)
        mine = is_set(bit)
        have = jnp.stack([jnp.where(mine, other, have), jnp.where(mine, have, other)], axis=axis)
        met.append(bit)
    return have.reshape((n,) + shard.shape)


def local(n, images, mix_weight, partner, keep_mask, cotangent, weight_in, weight_out, weight_down, small_params,
          first_in, second_in, first_out, second_out, first_down, second_down, first_small, second_small):
    imgs, side = images.shape[:2]
    half = side // 2
    pixels = side * side * imgs
    me = lax.axis_index("dp")
    bits = [1 << k for k in range(n.bit_length() - 1)]
    deep = FF // n
    by_hops = n == 32

    pair, down = ready(weight_in, weight_out, weight_down)
    mine = me[None].astype(jnp.int32)
    p_masks = w_masks = d_masks = None
    if by_hops:
        p_order = [16, 8, 4, 2, 1]
        w_order = [16, 8, 2, 4, 1]
        d_order = [16, 2, 8, 4, 1]
        p_masks, w_masks, d_masks = p_order, w_order, d_order

    img = images.transpose(1, 2, 0, 3)
    dy = cotangent.transpose(1, 2, 0, 3)
    flat = lambda a: a.reshape(pixels, a.shape[-1])
    square = lambda a: a.reshape(side, side, imgs, a.shape[-1])

    cut = [0, 3, 10, side]
    gates = None
    if by_hops:
        gates = {0: pair}
        pair = join(pair, swap(pair, p_order[0], n))
        gates[2] = pair
        down = join(down, swap(down, w_order[0], n))
        pair = join(pair, swap(pair, p_order[1], n))
        gates[4] = pair
    small = gather_natural(small_params.astype(BF16), n, bits[1:] + bits[:1], gates).reshape(-1, D).astype(F32)
    if by_hops:
        down = join(down, swap(down, w_order[1], n))
    mixed, *made, token = conv_forward(small, (img, partner, mix_weight), cut[0], cut[1])
    for part in (1, 2):
        if by_hops:
            pair = join(pair, swap(pair, p_order[part + 1], n), (token,))
            down = join(down, swap(down, w_order[part + 1], n), (token,))
        *made, token = conv_forward(small, (mixed,), cut[part], cut[part + 1], tuple(made), (pair, down))
    unit1, inv1, norm1 = made
    if by_hops:
        pair = (pair, swap(pair, p_order[4], n))
        down = (down, swap(down, w_order[4], n))
    else:
        pair, down = (lax.all_gather(x[0], "dp", axis=0, tiled=True).reshape(2, FF // 2, 2 * D) for x in (pair, down))
    pair = tuple(x.reshape(FF // 2, 2 * D) for x in pair)
    down = tuple(x.reshape(FF // 2, 2 * D) for x in down)
    act, dg, d_near, d_far, gdb, out, bb, sums2, res = block_both(
        (p_masks, w_masks, d_masks), mine, flat(norm1), flat(mixed), pair, down, dy, small, keep_mask
    )
    shards = (n // 2, deep, 2 * D)
    if by_hops:
        d_keep = d_near.reshape(shards)
        d_come = swap(d_far.reshape(shards), d_order[4], n)
    grads_of = lambda which, after: pair_grad(
        16 * which, p_masks, mine, flat(bb), act, dg, flat(norm1), pair[which], imgs, after
    )
    p_far, far_hb, far_p = grads_of(1, ())
    if by_hops:
        d_keep, d_send = fold(d_keep, d_come, after=(far_hb,))
        d_come = swap(d_send, d_order[3], n)
        p_come = swap(p_far.reshape(shards), p_order[4], n)
    p_near, near_hb, near_p = grads_of(0, (d_send,) if by_hops else (far_hb,))
    p_gate = ()
    if by_hops:
        p_keep, p_send = fold(p_near.reshape(shards), p_come, after=(near_hb,))
        p_come = swap(p_send, p_order[3], n)
        d_keep, d_send = fold(d_keep, d_come, after=(near_hb,))
        d_come = swap(d_send, d_order[2], n)
        p_gate = (p_send, d_send)
    back_conv, sums1 = back_one(p_masks, mine, (near_p, far_p), flat(unit1), flat(inv1), pair, small, imgs, p_gate)
    back_conv = square(back_conv)
    res = square(res)
    back = functools.partial(images_back, back_conv, small, partner, mix_weight, res)
    if by_hops:
        p_keep, p_send = fold(p_keep, p_come, after=(sums1,))
        p_come = swap(p_send, p_order[2], n)
        d_keep, d_send = fold(d_keep, d_come, after=(sums1,))
        d_come = swap(d_send, d_order[1], n)
        grad, token = back(0, half, (), (p_send, d_send))
        p_keep, p_send = fold(p_keep, p_come, after=(token,))
        p_come = swap(p_send, p_order[1], n)
        grad, token = back(half, side, (grad,), (p_send,))
        keep, send = fold(p_keep, p_come, d_keep, d_come, after=(token,))
        come = swap(send, p_order[0], n)
        gk = taps_grad(back_conv, mixed, (0, 1, 2), (send,))
    else:
        grad, _ = back(0, side)
        gk = taps_grad(back_conv, mixed, (0, 1, 2))
        keep = jnp.stack(
            [
                lax.psum_scatter(jnp.concatenate(x).astype(F32), "dp", scatter_dimension=0, tiled=True)
                for x in ((p_near, p_far), (d_near, d_far))
            ]
        )
        come = jnp.zeros(keep.shape, BF16)

    grads, total = small_total(n if by_hops else 0, mine, gk, sums1, sums2, near_hb, far_hb, gdb, keep, come)
    rounds = [bits[k : k + 2] for k in range(1, len(bits), 2)] + [bits[:1]]
    for step, pair_bits in enumerate(rounds):
        others = [pair_bits[0], pair_bits[-1], sum(pair_bits)] if len(pair_bits) == 2 else pair_bits
        arrays = (total,) + tuple(swap(total, other, n) for other in others)
        total = meet(arrays, F32 if step == len(rounds) - 1 else BF16)
    states = (weight_in, first_in, second_in, weight_out, first_out, second_out, weight_down, first_down, second_down)
    *news, norm = adam_all(total, grads, states)
    grad_norm = norm[0, 0]
    factor = CLIP_NORM / jnp.maximum(grad_norm, CLIP_NORM)
    shard_len = small_params.shape[0]
    gs = lax.dynamic_slice_in_dim(total[:SQUARES].reshape(-1), me * shard_len, shard_len)
    position = me * shard_len + jnp.arange(shard_len, dtype=jnp.int32)
    small_rate = jnp.where(position < 54 * D + FF, LAYER_DECAY * RATE_VECTOR, RATE_VECTOR)
    small_decay = jnp.where(position < 49 * D, WEIGHT_DECAY, 0.0)
    new_small = adam(small_params, first_small, second_small, gs * factor, small_rate, small_decay)
    return (
        out.transpose(2, 0, 1, 3),
        grad.transpose(2, 0, 1, 3),
        grad_norm,
        *news,
        *new_small,
    )


def solution(mesh):
    four = P("dp", None, None, None)
    two = P("dp", None)
    one = P("dp")
    return jax.shard_map(
        functools.partial(local, mesh.shape["dp"]),
        mesh=mesh,
        in_specs=(four, one, one, one, four, two, two, two, one) + (two,) * 6 + (one,) * 2,
        out_specs=(four, four, P()) + (two,) * 9 + (one,) * 3,
        check_vma=False,
    )
```

profile of v0, /device:TPU:0, one launch (start us, length us, event | category | flops | bytes accessed | tf_op | source)
XLA Modules:
  0.0 198.0 jit_solution(17943179542158110090)
XLA Ops:
  1.3 1.0 shard_map.280
  2.4 3.0 %collective-permute-start = (bf16[744]{0:T(1024)(128)(2,1)S(1)}, bf16[744]{0:T(1024)(128)(2,1)S(1)}, u32[]{:S(2)}, u32[]{:S(2)}) collective-permute-start(bf16[744]{0:T(1024)(128)(2,1)S(1)} %convert_element_type.8), channel_id=1, source_target_pairs={{0,2},{1,3},{2,0},{3,1},{4,6},{5,7},{6,4},{7,5},{8,10},{9,11},{10,... | collective-permute-start | bytes 4472 | tf_op jit(solution)/shard_map/ppermute | solution.py:1060
  5.4 1.6 collective-permute-done
  7.0 2.1 %collective-permute-start.1 = (bf16[2,744]{1,0:T(2,128)(2,1)S(1)}, bf16[2,744]{1,0:T(2,128)(2,1)S(1)}, u32[]{:S(2)}, u32[]{:S(2)}) collective-permute-start(bf16[2,744]{1,0:T(2,128)(2,1)S(1)} %pad_maximum_fusion.3), channel_id=1, source_target_pairs={{0,4},{1,5},{2,6},{3,7},{4,0},{5,1},{6,2},{7,3},{8,12},{9,13},{10,... | collective-permute-start | bytes 8936 | tf_op jit(solution)/shard_map/ppermute | solution.py:1060
  9.1 2.6 %collective-permute-start.2 = (bf16[1,48,768]{2,1,0:T(8,128)(2,1)S(1)}, bf16[1,48,768]{2,1,0:T(8,128)(2,1)S(1)}, u32[]{:S(2)}, u32[]{:S(2)}) collective-permute-start(bf16[1,48,768]{2,1,0:T(8,128)(2,1)S(1)} %get-tuple-element.79.first_ref), channel_id=1, source_target_pairs={{0,16},{1,17},{2,18},{3,19},{4,20},{5,21},{6,22},{7,23},{8,24},{9,... | collective-permute-start | bytes 221192 | tf_op jit(solution)/shard_map/ppermute | solution.py:1060
  11.7 2.6 %collective-permute-done.2.second_ref = bf16[1,48,768]{2,1,0:T(8,128)(2,1)S(1)} collective-permute-done((bf16[1,48,768]{2,1,0:T(8,128)(2,1)S(1)}, bf16[1,48,768]{2,1,0:T(8,128)(2,1)S(1)}, u32[]{:S(2)}, u32[]{:S(2)}) %collective-permute-start.2) | collective-permute-done | bytes 73760 | tf_op jit(solution)/shard_map/ppermute | solution.py:1060
  14.4 1.6 collective-permute-start.3
  16.0 3.3 %collective-permute-start.8 = (bf16[1,48,768]{2,1,0:T(8,128)(2,1)S(1)}, bf16[1,48,768]{2,1,0:T(8,128)(2,1)S(1)}, u32[]{:S(2)}, u32[]{:S(2)}) collective-permute-start(bf16[1,48,768]{2,1,0:T(8,128)(2,1)S(1)} %get-tuple-element.88.first_ref), channel_id=1, source_target_pairs={{0,16},{1,17},{2,18},{3,19},{4,20},{5,21},{6,22},{7,23},{8,24},{9,... | collective-permute-start | bytes 221192 | tf_op jit(solution)/shard_map/ppermute | solution.py:1060
  19.4 1.6 collective-permute-start.4
  21.0 1.2 collective-permute-done.8.second_ref
  22.2 0.9 collective-permute-start.9
  23.1 1.0 collective-permute-done.4
  24.3 0.8 collective-permute-done.5.second_ref
  25.7 1.8 collective-permute-done.9.second_ref
  27.4 1.6 collective-permute-start.10
  29.2 0.8 reshape.99.refs_0_.small_hbm
  30.0 9.1 %shard_map.283 = (f32[14,14,16,384]{3,2,1,0:T(8,128)}, bf16[14,14,16,384]{3,2,1,0:T(8,128)(2,1)}, f32[14,14,16,1]{3,2,1,0:T(8,128)}, bf16[14,14,16,384]{3,2,1,0:T(8,128)(2,1)}, f32[8,128]{1,0:T(8,128)S(1)}) custom-call(f32[62,384]{1,0:T(8,128)} %reshape.99.refs_0_.small_hbm, bf16[14,14,16,384]{3,2,1,0:T(8,128)(2,1)} %bitcast.46, s32[16]{0:T(128)S(1)} %copy-done.12, ...), custom_call_target="tpu_custom_call" | custom-call | flops 7500000256 | tf_op jit(solution)/shard_map/pallas_call | solution.py:71
  40.4 10.9 %shard_map.288 = (bf16[14,14,16,384]{3,2,1,0:T(8,128)(2,1)}, f32[14,14,16,1]{3,2,1,0:T(8,128)}, bf16[14,14,16,384]{3,2,1,0:T(8,128)(2,1)}, f32[8,128]{1,0:T(8,128)S(1)}) custom-call(f32[62,384]{1,0:T(8,128)} %reshape.99.refs_0_.small_hbm, ...), custom_call_target="tpu_custom_call", output_to_operand_aliasing={{0}: (2, {}), {1}: (3, {}), {2}: (4, {})} | custom-call | flops 10499999744 | tf_op jit(solution)/shard_map/pallas_call | solution.py:71
  51.3 1.7 collective-permute-done.12.second_ref
  53.2 1.2 collective-permute-done.11.second_ref
  54.6 8.0 %shard_map.291 = (bf16[14,14,16,384]{3,2,1,0:T(8,128)(2,1)}, f32[14,14,16,1]{3,2,1,0:T(8,128)}, bf16[14,14,16,384]{3,2,1,0:T(8,128)(2,1)}, f32[8,128]{1,0:T(8,128)}) custom-call(f32[62,384]{1,0:T(8,128)} %reshape.99.refs_0_.small_hbm, ...), custom_call_target="tpu_custom_call", output_to_operand_aliasing={{0}: (2, {}), {1}: (3, {}), {2}: (4, {})} | custom-call | flops 6000000000 | tf_op jit(solution)/shard_map/pallas_call | solution.py:71
  62.6 1.1 copy-done.20
  64.0 33.0 %shard_map.292 = (bf16[3136,1536]{1,0:T(8,128)(2,1)}, bf16[3136,1536]{1,0:T(8,128)(2,1)}, bf16[768,768]{1,0:T(8,128)(2,1)}, bf16[768,768]{1,0:T(8,128)(2,1)}, f3...) custom-call(s32[1]{0:T(128)} %bitcast.me_ref, ...), custom_call_target="tpu_custom_call" | custom-call | flops 33999998976 | tf_op jit(solution)/shard_map/pallas_call | solution.py:71
  97.2 12.7 %shard_map.293 = (bf16[768,768]{1,0:T(8,128)(2,1)S(1)}, f32[16,768]{1,0:T(8,128)S(1)}, bf16[3136,768]{1,0:T(8,128)(2,1)}) custom-call(s32[1]{0:T(128)} %bitcast.me_ref, bf16[3136,384]{1,0:T(8,128)(2,1)} %bitcast.60, bf16[3136,1536]{1,0:T(8,128)(2,1)} %get-tuple-element.96.act_hbm, bf16[3136,1536]{1,0:T(8,128)(2,1)} %get-tuple-element.97.dg_hbm, ...), custom_call_target="tpu_custom_call" | custom-call | flops 12999999488 | tf_op jit(solution)/shard_map/pallas_call | solution.py:71
  111.1 12.6 %shard_map.295 = (bf16[768,768]{1,0:T(8,128)(2,1)S(1)}, f32[16,768]{1,0:T(8,128)S(1)}, bf16[3136,768]{1,0:T(8,128)(2,1)}) custom-call(s32[1]{0:T(128)} %bitcast.me_ref, bf16[3136,384]{1,0:T(8,128)(2,1)} %bitcast.61, bf16[3136,1536]{1,0:T(8,128)(2,1)} %get-tuple-element.96.act_hbm, bf16[3136,1536]{1,0:T(8,128)(2,1)} %get-tuple-element.97.dg_hbm, ...), custom_call_target="tpu_custom_call" | custom-call | flops 12999999488 | tf_op jit(solution)/shard_map/pallas_call | solution.py:71
  124.0 1.1 collective-permute-start.18
  125.1 0.9 collective-permute-done.17.refs_1_
  126.1 1.2 collective-permute-start.19
  127.3 11.0 %shard_map.298 = (bf16[3136,384]{1,0:T(8,128)(2,1)}, f32[3,16,384]{2,1,0:T(8,128)S(1)}) custom-call(s32[1]{0:T(128)} %bitcast.me_ref, bf16[3136,768]{1,0:T(8,128)(2,1)} %get-tuple-element.102.pnear_hbm, bf16[3136,768]{1,0:T(8,128)(2,1)} %get-tuple-element.103.pfar_hbm, bf16[3136,384]{1,0:T(8,128)(2,1)} %bitcast.62, f32[3136,1]{1,0:T(8,128)} %bitcast.66, ...), custom_call_target="tpu_custom_call" | custom-call | flops 11000000512 | tf_op jit(solution)/shard_map/pallas_call | solution.py:71
  138.3 1.1 collective-permute-done.18.refs_1_
  139.4 1.4 collective-permute-start.20
  140.9 1.1 collective-permute-start.22
  142.0 10.3 %shard_map.301 = (f32[14,14,16,384]{3,2,1,0:T(8,128)}, f32[8,128]{1,0:T(8,128)S(1)}) custom-call(bf16[14,14,16,384]{3,2,1,0:T(8,128)(2,1)} %bitcast.57, f32[62,384]{1,0:T(8,128)} %reshape.99.refs_0_.small_hbm, s32[16]{0:T(128)S(1)} %copy-done.12, f32[16]{0:T(128)S(1)} %copy-done.13, bf16[14,14,16,384]{3,2,1,0:T(8,128)(2,1)} %bitcast.55, ...), custom_call_target="tpu_custom_call" | custom-call | flops 11000000512 | tf_op jit(solution)/shard_map/pallas_call | solution.py:71
  152.4 1.2 collective-permute-start.21
  153.6 10.0 %shard_map.303 = (f32[14,14,16,384]{3,2,1,0:T(8,128)}, f32[8,128]{1,0:T(8,128)S(1)}) custom-call(bf16[14,14,16,384]{3,2,1,0:T(8,128)(2,1)} %bitcast.58, f32[62,384]{1,0:T(8,128)} %reshape.99.refs_0_.small_hbm, s32[16]{0:T(128)S(1)} %copy-done.12, f32[16]{0:T(128)S(1)} %copy-done.13, ...), custom_call_target="tpu_custom_call", output_to_operand_aliasing={{0}: (5, {})} | custom-call | flops 11000000512 | tf_op jit(solution)/shard_map/pallas_call | solution.py:71
  163.7 1.6 collective-permute-start.23
  165.3 13.0 %shard_map.305.gk_ref = f32[49,8,384]{2,1,0:T(8,128)S(1)} custom-call(bf16[14,14,16,384]{3,2,1,0:T(8,128)(2,1)} %bitcast.59, f32[14,14,16,384]{3,2,1,0:T(8,128)} %get-tuple-element.83.refs_1_.mixed_hbm, bf16[2,48,768]{2,1,0:T(8,128)(2,1)S(1)} %get-tuple-element.127.rest_0_), custom_call_target="tpu_custom_call" | custom-call | flops 14099999744 | tf_op jit(solution)/shard_map/pallas_call | solution.py:71
  178.7 1.1 collective-permute-start.24
  180.5 1.8 collective-permute-start.26
  182.9 1.0 collective-permute-done.25.refs_2_
  183.9 1.6 collective-permute-done.26.refs_3_
  185.5 1.3 collective-permute-start.27
  186.8 1.1 collective-permute-start.28
  187.9 2.0 %collective-permute-start.29 = (bf16[64,384]{1,0:T(8,128)(2,1)S(1)}, bf16[64,384]{1,0:T(8,128)(2,1)S(1)}, u32[]{:S(2)}, u32[]{:S(2)}) collective-permute-start(bf16[64,384]{1,0:T(8,128)(2,1)S(1)} %shard_map.307.refs_0_), channel_id=1, source_target_pairs={{0,24},{1,25},{2,26},{3,27},{4,28},{5,29},{6,30},{7,31},{8,16},{9,... | collective-permute-start | bytes 147464 | tf_op jit(solution)/shard_map/ppermute | solution.py:1060
  190.0 2.4 %collective-permute-done.28.refs_2_ = bf16[64,384]{1,0:T(8,128)(2,1)S(1)} collective-permute-done((bf16[64,384]{1,0:T(8,128)(2,1)S(1)}, bf16[64,384]{1,0:T(8,128)(2,1)S(1)}, u32[]{:S(2)}, u32[]{:S(2)}) %collective-permute-start.28) | collective-permute-done | bytes 49184 | tf_op jit(solution)/shard_map/ppermute | solution.py:1060
  192.3 1.5 collective-permute-done.29.refs_3_
  193.9 1.2 collective-permute-done.30.refs_1_
  195.3 1.3 shard_map.310
  (104 shorter events, 8.5 us)
Async XLA Ops:
  2.4 4.6 %collective-permute-start = (bf16[744]{0:T(1024)(128)(2,1)S(1)}, bf16[744]{0:T(1024)(128)(2,1)S(1)}, u32[]{:S(2)}, u32[]{:S(2)}) collective-permute-start(bf16[744]{0:T(1024)(128)(2,1)S(1)} %convert_element_type.8), channel_id=1, source_target_pairs={{0,2},{1,3},{2,0},{3,1},{4,6},{5,7},{6,4},{7,5},{8,10},{9,11},{10,... | collective-permute-start | bytes 4472 | tf_op jit(solution)/shard_map/ppermute | solution.py:1060
  7.0 4.7 %collective-permute-start.1 = (bf16[2,744]{1,0:T(2,128)(2,1)S(1)}, bf16[2,744]{1,0:T(2,128)(2,1)S(1)}, u32[]{:S(2)}, u32[]{:S(2)}) collective-permute-start(bf16[2,744]{1,0:T(2,128)(2,1)S(1)} %pad_maximum_fusion.3), channel_id=1, source_target_pairs={{0,4},{1,5},{2,6},{3,7},{4,0},{5,1},{6,2},{7,3},{8,12},{9,13},{10,... | collective-permute-start | bytes 8936 | tf_op jit(solution)/shard_map/ppermute | solution.py:1060
  9.1 5.3 %collective-permute-start.2 = (bf16[1,48,768]{2,1,0:T(8,128)(2,1)S(1)}, bf16[1,48,768]{2,1,0:T(8,128)(2,1)S(1)}, u32[]{:S(2)}, u32[]{:S(2)}) collective-permute-start(bf16[1,48,768]{2,1,0:T(8,128)(2,1)S(1)} %get-tuple-element.79.first_ref), channel_id=1, source_target_pairs={{0,16},{1,17},{2,18},{3,19},{4,20},{5,21},{6,22},{7,23},{8,24},{9,... | collective-permute-start | bytes 221192 | tf_op jit(solution)/shard_map/ppermute | solution.py:1060
  14.4 5.0 %collective-permute-start.3 = (bf16[2,2,744]{2,1,0:T(2,128)(2,1)S(1)}, bf16[2,2,744]{2,1,0:T(2,128)(2,1)S(1)}, u32[]{:S(2)}, u32[]{:S(2)}) collective-permute-start(bf16[2,2,744]{2,1,0:T(2,128)(2,1)S(1)} %pad_maximum_fusion.2), channel_id=1, source_target_pairs={{0,8},{1,9},{2,10},{3,11},{4,12},{5,13},{6,14},{7,15},{8,0},{9,1},... | collective-permute-start | bytes 17864 | tf_op jit(solution)/shard_map/ppermute | solution.py:1060
  16.0 6.2 %collective-permute-start.8 = (bf16[1,48,768]{2,1,0:T(8,128)(2,1)S(1)}, bf16[1,48,768]{2,1,0:T(8,128)(2,1)S(1)}, u32[]{:S(2)}, u32[]{:S(2)}) collective-permute-start(bf16[1,48,768]{2,1,0:T(8,128)(2,1)S(1)} %get-tuple-element.88.first_ref), channel_id=1, source_target_pairs={{0,16},{1,17},{2,18},{3,19},{4,20},{5,21},{6,22},{7,23},{8,24},{9,... | collective-permute-start | bytes 221192 | tf_op jit(solution)/shard_map/ppermute | solution.py:1060
  19.3 5.8 %collective-permute-start.5 = (bf16[2,48,768]{2,1,0:T(8,128)(2,1)S(1)}, bf16[2,48,768]{2,1,0:T(8,128)(2,1)S(1)}, u32[]{:S(2)}, u32[]{:S(2)}) collective-permute-start(bf16[2,48,768]{2,1,0:T(8,128)(2,1)S(1)} %shard_map.281.first_ref), channel_id=1, source_target_pairs={{0,8},{1,9},{2,10},{3,11},{4,12},{5,13},{6,14},{7,15},{8,0},{9,1},... | collective-permute-start | bytes 442376 | tf_op jit(solution)/shard_map/ppermute | solution.py:1060
  19.4 4.8 %collective-permute-start.4 = (bf16[2,2,2,744]{3,2,1,0:T(2,128)(2,1)S(1)}, bf16[2,2,2,744]{3,2,1,0:T(2,128)(2,1)S(1)}, u32[]{:S(2)}, u32[]{:S(2)}) collective-permute-start(bf16[2,2,2,744]{3,2,1,0:T(2,128)(2,1)S(1)} %pad_maximum_fusion.1), channel_id=1, source_target_pairs={{0,16},{1,17},{2,18},{3,19},{4,20},{5,21},{6,22},{7,23},{8,24},{9,... | collective-permute-start | bytes 35720 | tf_op jit(solution)/shard_map/ppermute | solution.py:1060
  22.2 7.8 %copy-start.12 = (s32[16]{0:T(128)S(1)}, s32[16]{0:T(128)}, u32[]{:S(2)}) copy-start(s32[16]{0:T(128)} %partner_ref.3) | copy-start | bytes 196
  22.2 7.8 %copy-start.13 = (f32[16]{0:T(128)S(1)}, f32[16]{0:T(128)}, u32[]{:S(2)}) copy-start(f32[16]{0:T(128)} %weight_ref.3) | copy-start | bytes 196
  22.2 5.2 %collective-permute-start.9 = (bf16[2,48,768]{2,1,0:T(8,128)(2,1)S(1)}, bf16[2,48,768]{2,1,0:T(8,128)(2,1)S(1)}, u32[]{:S(2)}, u32[]{:S(2)}) collective-permute-start(bf16[2,48,768]{2,1,0:T(8,128)(2,1)S(1)} %shard_map.285.first_ref), channel_id=1, source_target_pairs={{0,8},{1,9},{2,10},{3,11},{4,12},{5,13},{6,14},{7,15},{8,0},{9,1},... | collective-permute-start | bytes 442376 | tf_op jit(solution)/shard_map/ppermute | solution.py:1060
  25.1 14.7 %collective-permute-start.7 = (bf16[4,48,768]{2,1,0:T(8,128)(2,1)S(1)}, bf16[4,48,768]{2,1,0:T(8,128)(2,1)S(1)}, u32[]{:S(2)}, u32[]{:S(2)}) collective-permute-start(bf16[4,48,768]{2,1,0:T(8,128)(2,1)S(1)} %shard_map.282.first_ref), channel_id=1, source_target_pairs={{0,4},{1,5},{2,6},{3,7},{4,0},{5,1},{6,2},{7,3},{8,12},{9,13},{10,... | collective-permute-start | bytes 884744 | tf_op jit(solution)/shard_map/ppermute | solution.py:1060
  25.7 3.3 %collective-permute-start.6 = (bf16[2,2,2,2,744]{4,3,2,1,0:T(2,128)(2,1)S(1)}, bf16[2,2,2,2,744]{4,3,2,1,0:T(2,128)(2,1)S(1)}, u32[]{:S(2)}, u32[]{:S(2)}) collective-permute-start(bf16[2,2,2,2,744]{4,3,2,1,0:T(2,128)(2,1)S(1)} %pad_maximum_fusion), channel_id=1, source_target_pairs={{0,1},{1,0},{2,3},{3,2},{4,5},{5,4},{6,7},{7,6},{8,9},{9,8},{10,11... | collective-permute-start | bytes 71432 | tf_op jit(solution)/shard_map/ppermute | solution.py:1060
  27.4 11.7 %collective-permute-start.10 = (bf16[4,48,768]{2,1,0:T(8,128)(2,1)S(1)}, bf16[4,48,768]{2,1,0:T(8,128)(2,1)S(1)}, u32[]{:S(2)}, u32[]{:S(2)}) collective-permute-start(bf16[4,48,768]{2,1,0:T(8,128)(2,1)S(1)} %shard_map.286.first_ref), channel_id=1, source_target_pairs={{0,2},{1,3},{2,0},{3,1},{4,6},{5,7},{6,4},{7,5},{8,10},{9,11},{10,... | collective-permute-start | bytes 884744 | tf_op jit(solution)/shard_map/ppermute | solution.py:1060
  39.2 13.8 %collective-permute-start.12 = (bf16[8,48,768]{2,1,0:T(8,128)(2,1)S(1)}, bf16[8,48,768]{2,1,0:T(8,128)(2,1)S(1)}, u32[]{:S(2)}, u32[]{:S(2)}) collective-permute-start(bf16[8,48,768]{2,1,0:T(8,128)(2,1)S(1)} %shard_map.287.refs_6_.first_ref), channel_id=1, source_target_pairs={{0,4},{1,5},{2,6},{3,7},{4,0},{5,1},{6,2},{7,3},{8,12},{9,13},{10,... | collective-permute-start | bytes 1769480 | tf_op jit(solution)/shard_map/ppermute | solution.py:1060
  39.8 14.5 %collective-permute-start.11 = (bf16[8,48,768]{2,1,0:T(8,128)(2,1)S(1)}, bf16[8,48,768]{2,1,0:T(8,128)(2,1)S(1)}, u32[]{:S(2)}, u32[]{:S(2)}) collective-permute-start(bf16[8,48,768]{2,1,0:T(8,128)(2,1)S(1)} %shard_map.284.refs_5_.first_ref), channel_id=1, source_target_pairs={{0,2},{1,3},{2,0},{3,1},{4,6},{5,7},{6,4},{7,5},{8,10},{9,11},{10,... | collective-permute-start | bytes 1769480 | tf_op jit(solution)/shard_map/ppermute | solution.py:1060
  53.1 9.4 %copy-start.1 = (bf16[16,48,768]{2,1,0:T(8,128)(2,1)}, bf16[16,48,768]{2,1,0:T(8,128)(2,1)S(1)}, u32[]{:S(2)}) copy-start(bf16[16,48,768]{2,1,0:T(8,128)(2,1)S(1)} %shard_map.290.refs_6_) | copy-start | bytes 3538948
  53.1 9.4 %collective-permute-start.14 = (bf16[16,48,768]{2,1,0:T(8,128)(2,1)S(1)}, bf16[16,48,768]{2,1,0:T(8,128)(2,1)S(1)}, u32[]{:S(2)}, u32[]{:S(2)}) collective-permute-start(bf16[16,48,768]{2,1,0:T(8,128)(2,1)S(1)} %shard_map.290.refs_6_), channel_id=1, source_target_pairs={{0,1},{1,0},{2,3},{3,2},{4,5},{5,4},{6,7},{7,6},{8,9},{9,8},{10,11... | collective-permute-start | bytes 3538952 | tf_op jit(solution)/shard_map/ppermute | solution.py:1060
  54.5 8.1 %copy-start = (bf16[16,48,768]{2,1,0:T(8,128)(2,1)}, bf16[16,48,768]{2,1,0:T(8,128)(2,1)S(1)}, u32[]{:S(2)}) copy-start(bf16[16,48,768]{2,1,0:T(8,128)(2,1)S(1)} %shard_map.289.refs_5_) | copy-start | bytes 3538948
  54.5 8.1 %collective-permute-start.13 = (bf16[16,48,768]{2,1,0:T(8,128)(2,1)S(1)}, bf16[16,48,768]{2,1,0:T(8,128)(2,1)S(1)}, u32[]{:S(2)}, u32[]{:S(2)}) collective-permute-start(bf16[16,48,768]{2,1,0:T(8,128)(2,1)S(1)} %shard_map.289.refs_5_), channel_id=1, source_target_pairs={{0,1},{1,0},{2,3},{3,2},{4,5},{5,4},{6,7},{7,6},{8,9},{9,8},{10,11... | collective-permute-start | bytes 3538952 | tf_op jit(solution)/shard_map/ppermute | solution.py:1060
  96.9 13.3 %collective-permute-start.15 = (bf16[16,48,768]{2,1,0:T(8,128)(2,1)}, bf16[16,48,768]{2,1,0:T(8,128)(2,1)S(1)}, u32[]{:S(2)}, u32[]{:S(2)}) collective-permute-start(bf16[16,48,768]{2,1,0:T(8,128)(2,1)} %bitcast.52), channel_id=1, source_target_pairs={{0,1},{1,0},{2,3},{3,2},{4,5},{5,4},{6,7},{7,6},{8,9},{9,8},{10,11... | collective-permute-start | bytes 3538952 | tf_op jit(solution)/shard_map/ppermute | solution.py:1060
  97.2 13.1 %copy-start.2 = (bf16[768,768]{1,0:T(8,128)(2,1)S(1)}, bf16[768,768]{1,0:T(8,128)(2,1)}, u32[]{:S(2)}) copy-start(bf16[768,768]{1,0:T(8,128)(2,1)} %get-tuple-element.98) | copy-start | bytes 3538948
  109.8 13.9 %collective-permute-start.16 = (bf16[16,48,768]{2,1,0:T(8,128)(2,1)S(1)}, bf16[16,48,768]{2,1,0:T(8,128)(2,1)S(1)}, u32[]{:S(2)}, u32[]{:S(2)}) collective-permute-start(bf16[16,48,768]{2,1,0:T(8,128)(2,1)S(1)} %bitcast.45), channel_id=1, source_target_pairs={{0,1},{1,0},{2,3},{3,2},{4,5},{5,4},{6,7},{7,6},{8,9},{9,8},{10,11... | collective-permute-start | bytes 3538952 | tf_op jit(solution)/shard_map/ppermute | solution.py:1060
  110.5 15.5 %collective-permute-start.17 = (bf16[8,48,768]{2,1,0:T(8,128)(2,1)S(1)}, bf16[8,48,768]{2,1,0:T(8,128)(2,1)S(1)}, u32[]{:S(2)}, u32[]{:S(2)}) collective-permute-start(bf16[8,48,768]{2,1,0:T(8,128)(2,1)S(1)} %get-tuple-element.101.rest_0_), channel_id=1, source_target_pairs={{0,4},{1,5},{2,6},{3,7},{4,0},{5,1},{6,2},{7,3},{8,12},{9,13},{10,... | collective-permute-start | bytes 1769480 | tf_op jit(solution)/shard_map/ppermute | solution.py:1060
  124.0 15.3 %collective-permute-start.18 = (bf16[8,48,768]{2,1,0:T(8,128)(2,1)S(1)}, bf16[8,48,768]{2,1,0:T(8,128)(2,1)S(1)}, u32[]{:S(2)}, u32[]{:S(2)}) collective-permute-start(bf16[8,48,768]{2,1,0:T(8,128)(2,1)S(1)} %get-tuple-element.109.rest_0_), channel_id=1, source_target_pairs={{0,2},{1,3},{2,0},{3,1},{4,6},{5,7},{6,4},{7,5},{8,10},{9,11},{10,... | collective-permute-start | bytes 1769480 | tf_op jit(solution)/shard_map/ppermute | solution.py:1060
  126.1 14.7 %collective-permute-start.19 = (bf16[4,48,768]{2,1,0:T(8,128)(2,1)S(1)}, bf16[4,48,768]{2,1,0:T(8,128)(2,1)S(1)}, u32[]{:S(2)}, u32[]{:S(2)}) collective-permute-start(bf16[4,48,768]{2,1,0:T(8,128)(2,1)S(1)} %get-tuple-element.111.rest_1_), channel_id=1, source_target_pairs={{0,8},{1,9},{2,10},{3,11},{4,12},{5,13},{6,14},{7,15},{8,0},{9,1},... | collective-permute-start | bytes 884744 | tf_op jit(solution)/shard_map/ppermute | solution.py:1060
  139.4 12.9 %collective-permute-start.20 = (bf16[4,48,768]{2,1,0:T(8,128)(2,1)S(1)}, bf16[4,48,768]{2,1,0:T(8,128)(2,1)S(1)}, u32[]{:S(2)}, u32[]{:S(2)}) collective-permute-start(bf16[4,48,768]{2,1,0:T(8,128)(2,1)S(1)} %get-tuple-element.116.rest_0_), channel_id=1, source_target_pairs={{0,4},{1,5},{2,6},{3,7},{4,0},{5,1},{6,2},{7,3},{8,12},{9,13},{10,... | collective-permute-start | bytes 884744 | tf_op jit(solution)/shard_map/ppermute | solution.py:1060
  140.9 22.7 %collective-permute-start.22 = (bf16[2,48,768]{2,1,0:T(8,128)(2,1)S(1)}, bf16[2,48,768]{2,1,0:T(8,128)(2,1)S(1)}, u32[]{:S(2)}, u32[]{:S(2)}) collective-permute-start(bf16[2,48,768]{2,1,0:T(8,128)(2,1)S(1)} %get-tuple-element.118.rest_1_), channel_id=1, source_target_pairs={{0,2},{1,3},{2,0},{3,1},{4,6},{5,7},{6,4},{7,5},{8,10},{9,11},{10,... | collective-permute-start | bytes 442376 | tf_op jit(solution)/shard_map/ppermute | solution.py:1060
  152.4 11.2 %collective-permute-start.21 = (bf16[2,48,768]{2,1,0:T(8,128)(2,1)S(1)}, bf16[2,48,768]{2,1,0:T(8,128)(2,1)S(1)}, u32[]{:S(2)}, u32[]{:S(2)}) collective-permute-start(bf16[2,48,768]{2,1,0:T(8,128)(2,1)S(1)} %get-tuple-element.122.rest_1_), channel_id=1, source_target_pairs={{0,8},{1,9},{2,10},{3,11},{4,12},{5,13},{6,14},{7,15},{8,0},{9,1},... | collective-permute-start | bytes 442376 | tf_op jit(solution)/shard_map/ppermute | solution.py:1060
  163.7 14.6 %copy-start.14 = (f32[4,16,384]{2,1,0:T(8,128)S(1)}, f32[4,16,384]{2,1,0:T(8,128)}, u32[]{:S(2)}) copy-start(f32[4,16,384]{2,1,0:T(8,128)} %get-tuple-element.128.sums2_ref) | copy-start | bytes 294916
  163.7 14.5 %copy-start.15 = (f32[16,768]{1,0:T(8,128)S(1)}, f32[16,768]{1,0:T(8,128)}, u32[]{:S(2)}) copy-start(f32[16,768]{1,0:T(8,128)} %get-tuple-element.129.db_ref) | copy-start | bytes 147460
  163.7 14.5 %collective-permute-start.23 = (bf16[2,48,768]{2,1,0:T(8,128)(2,1)S(1)}, bf16[2,48,768]{2,1,0:T(8,128)(2,1)S(1)}, u32[]{:S(2)}, u32[]{:S(2)}) collective-permute-start(bf16[2,48,768]{2,1,0:T(8,128)(2,1)S(1)} %get-tuple-element.127.rest_0_), channel_id=1, source_target_pairs={{0,16},{1,17},{2,18},{3,19},{4,20},{5,21},{6,22},{7,23},{8,24},{9,... | collective-permute-start | bytes 442376 | tf_op jit(solution)/shard_map/ppermute | solution.py:1060
  178.6 16.5 %copy-start.3 = (f32[48,768]{1,0:T(8,128)S(1)}, f32[48,768]{1,0:T(8,128)}, u32[]{:S(2)}) copy-start(f32[48,768]{1,0:T(8,128)} %refs_6_.1) | copy-start | bytes 442372
  178.6 16.5 %copy-start.4 = (f32[48,768]{1,0:T(8,128)S(1)}, f32[48,768]{1,0:T(8,128)}, u32[]{:S(2)}) copy-start(f32[48,768]{1,0:T(8,128)} %refs_7_.1) | copy-start | bytes 442372
  178.6 16.5 %copy-start.5 = (f32[48,768]{1,0:T(8,128)S(1)}, f32[48,768]{1,0:T(8,128)}, u32[]{:S(2)}) copy-start(f32[48,768]{1,0:T(8,128)} %refs_8_.1) | copy-start | bytes 442372
  178.7 16.5 %copy-start.6 = (f32[48,384]{1,0:T(8,128)S(1)}, f32[48,384]{1,0:T(8,128)}, u32[]{:S(2)}) copy-start(f32[48,384]{1,0:T(8,128)} %refs_0_.1) | copy-start | bytes 221188
  178.7 16.5 %copy-start.7 = (f32[48,384]{1,0:T(8,128)S(1)}, f32[48,384]{1,0:T(8,128)}, u32[]{:S(2)}) copy-start(f32[48,384]{1,0:T(8,128)} %refs_3_.3) | copy-start | bytes 221188
  178.7 16.5 %copy-start.8 = (f32[48,384]{1,0:T(8,128)S(1)}, f32[48,384]{1,0:T(8,128)}, u32[]{:S(2)}) copy-start(f32[48,384]{1,0:T(8,128)} %refs_1_.1) | copy-start | bytes 221188
  178.7 16.5 %copy-start.9 = (f32[48,384]{1,0:T(8,128)S(1)}, f32[48,384]{1,0:T(8,128)}, u32[]{:S(2)}) copy-start(f32[48,384]{1,0:T(8,128)} %refs_2_.3) | copy-start | bytes 221188
  178.7 16.5 %copy-start.10 = (f32[48,384]{1,0:T(8,128)S(1)}, f32[48,384]{1,0:T(8,128)}, u32[]{:S(2)}) copy-start(f32[48,384]{1,0:T(8,128)} %refs_4_.1) | copy-start | bytes 221188
  178.7 16.5 %copy-start.11 = (f32[48,384]{1,0:T(8,128)S(1)}, f32[48,384]{1,0:T(8,128)}, u32[]{:S(2)}) copy-start(f32[48,384]{1,0:T(8,128)} %refs_5_.1) | copy-start | bytes 221188
  178.7 4.2 %collective-permute-start.24 = (bf16[64,384]{1,0:T(8,128)(2,1)S(1)}, bf16[64,384]{1,0:T(8,128)(2,1)S(1)}, u32[]{:S(2)}, u32[]{:S(2)}) collective-permute-start(bf16[64,384]{1,0:T(8,128)(2,1)S(1)} %get-tuple-element.131.refs_0_), channel_id=1, source_target_pairs={{0,2},{1,3},{2,0},{3,1},{4,6},{5,7},{6,4},{7,5},{8,10},{9,11},{10,... | collective-permute-start | bytes 147464 | tf_op jit(solution)/shard_map/ppermute | solution.py:1060
  179.8 4.1 %collective-permute-start.25 = (bf16[64,384]{1,0:T(8,128)(2,1)S(1)}, bf16[64,384]{1,0:T(8,128)(2,1)S(1)}, u32[]{:S(2)}, u32[]{:S(2)}) collective-permute-start(bf16[64,384]{1,0:T(8,128)(2,1)S(1)} %get-tuple-element.131.refs_0_), channel_id=1, source_target_pairs={{0,4},{1,5},{2,6},{3,7},{4,0},{5,1},{6,2},{7,3},{8,12},{9,13},{10,... | collective-permute-start | bytes 147464 | tf_op jit(solution)/shard_map/ppermute | solution.py:1060
  180.5 5.0 %collective-permute-start.26 = (bf16[64,384]{1,0:T(8,128)(2,1)S(1)}, bf16[64,384]{1,0:T(8,128)(2,1)S(1)}, u32[]{:S(2)}, u32[]{:S(2)}) collective-permute-start(bf16[64,384]{1,0:T(8,128)(2,1)S(1)} %get-tuple-element.131.refs_0_), channel_id=1, source_target_pairs={{0,6},{1,7},{2,4},{3,5},{4,2},{5,3},{6,0},{7,1},{8,14},{9,15},{10,... | collective-permute-start | bytes 147464 | tf_op jit(solution)/shard_map/ppermute | solution.py:1060
  185.5 4.5 %collective-permute-start.27 = (bf16[64,384]{1,0:T(8,128)(2,1)S(1)}, bf16[64,384]{1,0:T(8,128)(2,1)S(1)}, u32[]{:S(2)}, u32[]{:S(2)}) collective-permute-start(bf16[64,384]{1,0:T(8,128)(2,1)S(1)} %shard_map.307.refs_0_), channel_id=1, source_target_pairs={{0,8},{1,9},{2,10},{3,11},{4,12},{5,13},{6,14},{7,15},{8,0},{9,1},... | collective-permute-start | bytes 147464 | tf_op jit(solution)/shard_map/ppermute | solution.py:1060
  186.8 5.5 %collective-permute-start.28 = (bf16[64,384]{1,0:T(8,128)(2,1)S(1)}, bf16[64,384]{1,0:T(8,128)(2,1)S(1)}, u32[]{:S(2)}, u32[]{:S(2)}) collective-permute-start(bf16[64,384]{1,0:T(8,128)(2,1)S(1)} %shard_map.307.refs_0_), channel_id=1, source_target_pairs={{0,16},{1,17},{2,18},{3,19},{4,20},{5,21},{6,22},{7,23},{8,24},{9,... | collective-permute-start | bytes 147464 | tf_op jit(solution)/shard_map/ppermute | solution.py:1060
  187.9 5.9 %collective-permute-start.29 = (bf16[64,384]{1,0:T(8,128)(2,1)S(1)}, bf16[64,384]{1,0:T(8,128)(2,1)S(1)}, u32[]{:S(2)}, u32[]{:S(2)}) collective-permute-start(bf16[64,384]{1,0:T(8,128)(2,1)S(1)} %shard_map.307.refs_0_), channel_id=1, source_target_pairs={{0,24},{1,25},{2,26},{3,27},{4,28},{5,29},{6,30},{7,31},{8,16},{9,... | collective-permute-start | bytes 147464 | tf_op jit(solution)/shard_map/ppermute | solution.py:1060
  193.8 1.3 collective-permute-start.30
  195.2 2.0 %copy-start.16 = (f32[744]{0:T(1024)S(1)}, f32[744]{0:T(1024)}, u32[]{:S(2)}) copy-start(f32[744]{0:T(1024)} %param.25) | copy-start | bytes 8932
  (4 other events, 6.5 us)
where the time goes:
time: 199 us; the launch traced here: 198 us
  Pallas kernels  134 us (67%)
  starting transfers between devices  35.5 us (18%)
  waiting for transfers between devices  22.1 us (11%)
  local copies, waits for them, and re-layouts  2.44 us (1%)
    pallas_call x30, Pallas kernels, kernel_call(): pl.pallas_call(body, out_shape=tuple(out), in_specs=specs, out_specs=tupl...  133 us
    ppermute x31, starting transfers between devices, swap(): return lax.ppermute(x, 'dp', [(i, i ^ bit) for i in range(n)])  35.5 us
    ppermute x31, waiting for transfers between devices, swap(): return lax.ppermute(x, 'dp', [(i, i ^ bit) for i in range(n)])  22.1 us
  transfers between devices with their start and end apart: 31, of which 16 were waited for; matrix products, arithmetic and copies ran while one was open for 1% of the time, Pallas kernels for 50%

commit v1 on v0

--- a/solution.py
+++ b/solution.py
@@ -98,9 +98,9 @@
     return pl.ds(pl.multiple_of(k % groups * 8, 8), 8), pl.ds(pl.multiple_of(k // groups * 128, 128), 128)
 
 
-def tiles(h, imgs, tile):
+def tiles(h, imgs, tile, loop):
     count = imgs // 8 * (D // 128)
-    if isinstance(h, int):
+    if loop and isinstance(h, int):
         return lax.fori_loop(0, count, tile, 0)
     for k in range(count):
         tile(k, 0)
@@ -244,7 +244,7 @@
                 conv_ref[r, w, at, lanes] = acc[w]
             return 0
 
-        return tiles(h, imgs, tile)
+        return tiles(h, imgs, tile, True)
 
     every_row(begin, end, side, conv)
     gain = small_ref[GAIN_ONE : GAIN_ONE + 1, :][None]
@@ -498,12 +498,8 @@
         start(give(k))
         sums_ref[3] += jnp.sum(bb.astype(F32), axis=0)
 
-    def half_of(a, _):
-        quarter(2 * a)
-        quarter(2 * a + 1)
-        return 0
-
-    lax.fori_loop(0, 2, half_of, 0)
+    for k in range(4):
+        quarter(k)
     out_ref[...] = acc[...].astype(BF16).reshape(out_ref.shape)
     deal(me, d_masks, False, 0, gnear_ref, lambda at, g: wide[g, at, :])
     deal(me, d_masks, False, HALF_PIECES, gfar_ref, lambda at, g: wide[g, at, :])
@@ -781,7 +777,7 @@
 
 
 def images_kernel(begin, end, conv_hbm, small_hbm, partner_ref, weight_ref, res_hbm, *rest):
-    g_hbm, token_ref, small_ref, raw_ref, conv_ref, taps, res_ref, out_ref, mix_ref, row_ref, sel_ref, rest_ref, sem, csem, pair_sums = rest[-15:]
+    g_hbm, token_ref, small_ref, raw_ref, conv_ref, taps, res_ref, out_ref, mix_ref, row_ref, sel_ref, rest_ref, sem, csem, pair_sums, rsem = rest[-16:]
     side, _, imgs, _ = conv_hbm.shape
     low = max(begin - 3, 0)
     high = min(end + 3, side)
@@ -798,7 +794,7 @@
         add_columns(conv_ref, pair_sums, h)
 
     def enter(h):
-        return dma(res_hbm.at[h], res_ref.at[h % 2], sem.at[0, h % 2])
+        return dma(res_hbm.at[h], res_ref.at[h - begin], rsem.at[h - begin])
 
     def leave(h):
         return dma(out_ref.at[h - begin], g_hbm.at[h], sem.at[1, 0])
@@ -806,7 +802,8 @@
     for h in range(low, high):
         bring(h).start()
         if h == min(begin + 3, high - 1):
-            enter(begin).start()
+            for r in range(begin, end):
+                enter(r).start()
     spread(weight_ref, mix_ref)
     for i in range(imgs):
         row_ref[pl.ds(lax.rem(partner_ref[i], imgs), 1), :] = jnp.full((1, row_ref.shape[1]), i, jnp.int32)
@@ -819,18 +816,13 @@
         widen(h)
 
     def row(h, kys):
-        s = h % 2
-
-        @pl.when(h + 1 < end)
-        def _():
-            enter(h + 1).start()
-
         @pl.when(h + 3 < high)
         def _():
             widen(h + 3)
 
         enter(h).wait()
-        rest_ref[...] = res_ref[s].astype(F32)
+        rest_ref[...] = res_ref[h - begin].astype(F32)
+
         def tile(k, _):
             at, lanes = tile_of(k, imgs)
             base = [rest_ref[w, at, lanes] for w in range(side)]
@@ -839,9 +831,10 @@
                 out_ref[h - begin, w, at, lanes] = acc[w]
             return 0
 
-        return tiles(h, imgs, tile)
+        return tiles(h, imgs, tile, False)
 
     every_row(begin, end, side, row)
+
     def unmix(r):
         v = out_ref[r]
         part = (others * v).reshape(side * imgs, D)
@@ -852,8 +845,12 @@
         out_ref[r] = mix * v + back.reshape(side, imgs, D)
         leave(begin + r).start()
 
-    for r in range(end - begin):
-        unmix(r)
+    def two(i, _):
+        unmix(2 * i)
+        unmix(2 * i + 1)
+        return 0
+
+    lax.fori_loop(0, (end - begin) // 2, two, 0)
     for h in range(begin, end):
         leave(h).wait()
 
@@ -869,7 +866,7 @@
             pltpu.VMEM(conv.shape, BF16),
             pltpu.VMEM(conv.shape, F32),
             pltpu.VMEM((77, 8, D), F32),
-            pltpu.VMEM((2, side, imgs, D), BF16),
+            pltpu.VMEM((end - begin, side, imgs, D), BF16),
             pltpu.VMEM((end - begin, side, imgs, D), F32),
             pltpu.VMEM((imgs, D), F32),
             pltpu.VMEM((imgs, side * imgs), jnp.int32),
@@ -878,6 +875,7 @@
             pltpu.SemaphoreType.DMA((2, 2)),
             pltpu.SemaphoreType.DMA((side + 1,)),
             pltpu.VMEM((side, side // 2, imgs, D), F32),
+            pltpu.SemaphoreType.DMA((end - begin,)),
         ],
         (conv, small, partner, weight, res) + tuple(so_far),
         after,
@@ -956,8 +954,33 @@
     )
 
 
-def small_kernel(hops, me_ref, gk_ref, sums1_ref, sums2_ref, near_ref, far_ref, db_ref, keep_ref, come_ref, sum_ref, send_ref, total):
-    grads = keep_ref[...] + come_ref[...].astype(F32)
+def part_kernel(*refs):
+    ins, outs = refs[:4], refs[-4:]
+    for i in range(2):
+        keep_ref, come_ref = ins[2 * i], ins[2 * i + 1]
+        for slot, out_ref in enumerate(outs):
+            out_ref[i] = (keep_ref[slot].astype(F32) + come_ref[slot].astype(F32)).astype(out_ref.dtype)
+
+
+def part(p_keep, p_come, d_keep, d_come, after=()):
+    shape = (2,) + p_keep.shape[1:]
+    return kernel_call(
+        part_kernel,
+        [near(shape, F32)] + [near(shape, BF16)] * 3,
+        [VMEM] * 4,
+        [],
+        (p_keep, p_come, d_keep, d_come),
+        after,
+        0.5,
+        12,
+    )
+
+
+def small_kernel(hops, me_ref, gk_ref, sums1_ref, sums2_ref, near_ref, far_ref, db_ref, keep_ref, *rest):
+    sum_ref, send_ref, total = rest[-3:]
+    grads = keep_ref[...]
+    for come_ref in rest[:-3]:
+        grads = grads + come_ref[...].astype(F32)
     sum_ref[...] = grads
     rows = lambda x: jnp.sum(x, axis=0, keepdims=True)
     for t in range(49):
@@ -992,13 +1015,13 @@
     send_ref[...] = total[...].astype(BF16)
 
 
-def small_total(hops, me, gk, sums1, sums2, near_hb, far_hb, db, keep, come):
+def small_total(hops, me, gk, sums1, sums2, near_hb, far_hb, db, keep, *come):
     return kernel_call(
         functools.partial(small_kernel, hops),
         [near(keep.shape, F32), near((SQUARES + 2, D), BF16)],
-        [SMEM] + [VMEM] * 8,
+        [SMEM] + [VMEM] * (7 + len(come)),
         [pltpu.VMEM((SQUARES + 2, D), F32)],
-        (me, gk, sums1, sums2, near_hb, far_hb, db, keep, come),
+        (me, gk, sums1, sums2, near_hb, far_hb, db, keep, *come),
         (),
         1,
         8,
@@ -1094,7 +1117,7 @@
     if by_hops:
         p_order = [16, 8, 4, 2, 1]
         w_order = [16, 8, 2, 4, 1]
-        d_order = [16, 2, 8, 4, 1]
+        d_order = p_order
         p_masks, w_masks, d_masks = p_order, w_order, d_order
 
     img = images.transpose(1, 2, 0, 3)
@@ -1115,11 +1138,11 @@
     if by_hops:
         down = join(down, swap(down, w_order[1], n))
     mixed, *made, token = conv_forward(small, (img, partner, mix_weight), cut[0], cut[1])
-    for part in (1, 2):
+    for piece in (1, 2):
         if by_hops:
-            pair = join(pair, swap(pair, p_order[part + 1], n), (token,))
-            down = join(down, swap(down, w_order[part + 1], n), (token,))
-        *made, token = conv_forward(small, (mixed,), cut[part], cut[part + 1], tuple(made), (pair, down))
+            pair = join(pair, swap(pair, p_order[piece + 1], n), (token,))
+            down = join(down, swap(down, w_order[piece + 1], n), (token,))
+        *made, token = conv_forward(small, (mixed,), cut[piece], cut[piece + 1], tuple(made), (pair, down))
     unit1, inv1, norm1 = made
     if by_hops:
         pair = (pair, swap(pair, p_order[4], n))
@@ -1158,15 +1181,10 @@
     if by_hops:
         p_keep, p_send = fold(p_keep, p_come, after=(sums1,))
         p_come = swap(p_send, p_order[2], n)
-        d_keep, d_send = fold(d_keep, d_come, after=(sums1,))
-        d_come = swap(d_send, d_order[1], n)
-        grad, token = back(0, half, (), (p_send, d_send))
-        p_keep, p_send = fold(p_keep, p_come, after=(token,))
-        p_come = swap(p_send, p_order[1], n)
-        grad, token = back(half, side, (grad,), (p_send,))
-        keep, send = fold(p_keep, p_come, d_keep, d_come, after=(token,))
-        come = swap(send, p_order[0], n)
-        gk = taps_grad(back_conv, mixed, (0, 1, 2), (send,))
+        grad, token = back(0, side, (), (p_send,))
+        keep, *send = part(p_keep, p_come, d_keep, d_come, after=(token,))
+        come = [swap(x, bits, n) for x, bits in zip(send, (16, 8, 24))]
+        gk = taps_grad(back_conv, mixed, (0, 1, 2), tuple(send))
     else:
         grad, _ = back(0, side)
         gk = taps_grad(back_conv, mixed, (0, 1, 2))
@@ -1176,9 +1194,9 @@
                 for x in ((p_near, p_far), (d_near, d_far))
             ]
         )
-        come = jnp.zeros(keep.shape, BF16)
-
-    grads, total = small_total(n if by_hops else 0, mine, gk, sums1, sums2, near_hb, far_hb, gdb, keep, come)
+        come = ()
+
+    grads, total = small_total(n if by_hops else 0, mine, gk, sums1, sums2, near_hb, far_hb, gdb, keep, *come)
     rounds = [bits[k : k + 2] for k in range(1, len(bits), 2)] + [bits[:1]]
     for step, pair_bits in enumerate(rounds):
         others = [pair_bits[0], pair_bits[-1], sum(pair_bits)] if len(pair_bits) == 2 else pair_bits

time: 199 us -> 195 us (0.980)
  Pallas kernels: 134 us -> 130 us
    pallas_call x30 -> x27, Pallas kernels: 133 us -> 129 us  [kernel_call(): pl.pallas_call(body, out_shape=tuple(out), in_specs=specs, out_specs=tupl...]
  transfers between devices with their start and end apart: 31 -> 31, of which waited for: 16 -> 16; matrix products, arithmetic and copies ran while one was open for 1% -> 1% of each run, Pallas kernels for 50% -> 49%
where the time goes in v1:
time: 195 us
  Pallas kernels  130 us (67%)
  starting transfers between devices  35.5 us (18%)
  waiting for transfers between devices  23.3 us (12%)
  local copies, waits for them, and re-layouts  2.45 us (1%)
  between operations  1.96 us (1%)
    pallas_call x27, Pallas kernels, kernel_call(): pl.pallas_call(body, out_shape=tuple(out), in_specs=specs, out_specs=tupl...  129 us
    ppermute x31, starting transfers between devices, swap(): return lax.ppermute(x, 'dp', [(i, i ^ bit) for i in range(n)])  35.5 us
    ppermute x31, waiting for transfers between devices, swap(): return lax.ppermute(x, 'dp', [(i, i ^ bit) for i in range(n)])  23.3 us
  transfers between devices with their start and end apart: 31, of which 16 were waited for; matrix products, arithmetic and copies ran while one was open for 1% of the time, Pallas kernels for 49%

profile of v1, /device:TPU:0, one launch (start us, length us, event | category | flops | bytes accessed | tf_op | source)
XLA Modules:
  0.0 194.6 jit_solution(7897319696553877670)
XLA Ops:
  1.3 1.0 shard_map.280
  2.4 3.0 %collective-permute-start = (bf16[744]{0:T(1024)(128)(2,1)S(1)}, bf16[744]{0:T(1024)(128)(2,1)S(1)}, u32[]{:S(2)}, u32[]{:S(2)}) collective-permute-start(bf16[744]{0:T(1024)(128)(2,1)S(1)} %convert_element_type.8), channel_id=1, source_target_pairs={{0,2},{1,3},{2,0},{3,1},{4,6},{5,7},{6,4},{7,5},{8,10},{9,11},{10,... | collective-permute-start | bytes 4472 | tf_op jit(solution)/shard_map/ppermute | solution.py:1083
  5.4 1.6 collective-permute-done
  7.0 2.1 %collective-permute-start.1 = (bf16[2,744]{1,0:T(2,128)(2,1)S(1)}, bf16[2,744]{1,0:T(2,128)(2,1)S(1)}, u32[]{:S(2)}, u32[]{:S(2)}) collective-permute-start(bf16[2,744]{1,0:T(2,128)(2,1)S(1)} %pad_maximum_fusion.3), channel_id=1, source_target_pairs={{0,4},{1,5},{2,6},{3,7},{4,0},{5,1},{6,2},{7,3},{8,12},{9,13},{10,... | collective-permute-start | bytes 8936 | tf_op jit(solution)/shard_map/ppermute | solution.py:1083
  9.1 2.6 %collective-permute-start.2 = (bf16[1,48,768]{2,1,0:T(8,128)(2,1)S(1)}, bf16[1,48,768]{2,1,0:T(8,128)(2,1)S(1)}, u32[]{:S(2)}, u32[]{:S(2)}) collective-permute-start(bf16[1,48,768]{2,1,0:T(8,128)(2,1)S(1)} %get-tuple-element.75.first_ref), channel_id=1, source_target_pairs={{0,16},{1,17},{2,18},{3,19},{4,20},{5,21},{6,22},{7,23},{8,24},{9,... | collective-permute-start | bytes 221192 | tf_op jit(solution)/shard_map/ppermute | solution.py:1083
  11.7 2.6 %collective-permute-done.2.second_ref = bf16[1,48,768]{2,1,0:T(8,128)(2,1)S(1)} collective-permute-done((bf16[1,48,768]{2,1,0:T(8,128)(2,1)S(1)}, bf16[1,48,768]{2,1,0:T(8,128)(2,1)S(1)}, u32[]{:S(2)}, u32[]{:S(2)}) %collective-permute-start.2) | collective-permute-done | bytes 73760 | tf_op jit(solution)/shard_map/ppermute | solution.py:1083
  14.4 1.6 collective-permute-start.3
  16.0 3.3 %collective-permute-start.8 = (bf16[1,48,768]{2,1,0:T(8,128)(2,1)S(1)}, bf16[1,48,768]{2,1,0:T(8,128)(2,1)S(1)}, u32[]{:S(2)}, u32[]{:S(2)}) collective-permute-start(bf16[1,48,768]{2,1,0:T(8,128)(2,1)S(1)} %get-tuple-element.84.first_ref), channel_id=1, source_target_pairs={{0,16},{1,17},{2,18},{3,19},{4,20},{5,21},{6,22},{7,23},{8,24},{9,... | collective-permute-start | bytes 221192 | tf_op jit(solution)/shard_map/ppermute | solution.py:1083
  19.4 1.6 collective-permute-start.4
  21.0 1.2 collective-permute-done.8.second_ref
  22.2 0.9 collective-permute-start.9
  23.1 1.1 collective-permute-done.4
  24.3 0.8 collective-permute-done.5.second_ref
  25.7 1.7 collective-permute-done.9.second_ref
  27.4 1.6 collective-permute-start.10
  29.2 0.8 reshape.99.refs_0_.small_hbm
  30.0 9.1 %shard_map.283 = (f32[14,14,16,384]{3,2,1,0:T(8,128)}, bf16[14,14,16,384]{3,2,1,0:T(8,128)(2,1)}, f32[14,14,16,1]{3,2,1,0:T(8,128)}, bf16[14,14,16,384]{3,2,1,0:T(8,128)(2,1)}, f32[8,128]{1,0:T(8,128)S(1)}) custom-call(f32[62,384]{1,0:T(8,128)} %reshape.99.refs_0_.small_hbm, bf16[14,14,16,384]{3,2,1,0:T(8,128)(2,1)} %bitcast.46, s32[16]{0:T(128)S(1)} %copy-done.12, ...), custom_call_target="tpu_custom_call" | custom-call | flops 7500000256 | tf_op jit(solution)/shard_map/pallas_call | solution.py:71
  40.4 10.9 %shard_map.288 = (bf16[14,14,16,384]{3,2,1,0:T(8,128)(2,1)}, f32[14,14,16,1]{3,2,1,0:T(8,128)}, bf16[14,14,16,384]{3,2,1,0:T(8,128)(2,1)}, f32[8,128]{1,0:T(8,128)S(1)}) custom-call(f32[62,384]{1,0:T(8,128)} %reshape.99.refs_0_.small_hbm, ...), custom_call_target="tpu_custom_call", output_to_operand_aliasing={{0}: (2, {}), {1}: (3, {}), {2}: (4, {})} | custom-call | flops 10499999744 | tf_op jit(solution)/shard_map/pallas_call | solution.py:71
  51.3 1.7 collective-permute-done.12.second_ref
  53.2 1.2 collective-permute-done.11.second_ref
  54.6 8.0 %shard_map.291 = (bf16[14,14,16,384]{3,2,1,0:T(8,128)(2,1)}, f32[14,14,16,1]{3,2,1,0:T(8,128)}, bf16[14,14,16,384]{3,2,1,0:T(8,128)(2,1)}, f32[8,128]{1,0:T(8,128)}) custom-call(f32[62,384]{1,0:T(8,128)} %reshape.99.refs_0_.small_hbm, ...), custom_call_target="tpu_custom_call", output_to_operand_aliasing={{0}: (2, {}), {1}: (3, {}), {2}: (4, {})} | custom-call | flops 6000000000 | tf_op jit(solution)/shard_map/pallas_call | solution.py:71
  62.6 1.1 copy-done.20
  64.0 32.2 %shard_map.292 = (bf16[3136,1536]{1,0:T(8,128)(2,1)}, bf16[3136,1536]{1,0:T(8,128)(2,1)}, bf16[768,768]{1,0:T(8,128)(2,1)}, bf16[768,768]{1,0:T(8,128)(2,1)}, f3...) custom-call(s32[1]{0:T(128)} %bitcast.me_ref, ...), custom_call_target="tpu_custom_call" | custom-call | flops 33999998976 | tf_op jit(solution)/shard_map/pallas_call | solution.py:71
  96.5 12.7 %shard_map.293 = (bf16[768,768]{1,0:T(8,128)(2,1)S(1)}, f32[16,768]{1,0:T(8,128)S(1)}, bf16[3136,768]{1,0:T(8,128)(2,1)}) custom-call(s32[1]{0:T(128)} %bitcast.me_ref, bf16[3136,384]{1,0:T(8,128)(2,1)} %bitcast.58, bf16[3136,1536]{1,0:T(8,128)(2,1)} %get-tuple-element.92.act_hbm, bf16[3136,1536]{1,0:T(8,128)(2,1)} %get-tuple-element.93.dg_hbm, ...), custom_call_target="tpu_custom_call" | custom-call | flops 12999999488 | tf_op jit(solution)/shard_map/pallas_call | solution.py:71
  109.8 1.1 collective-permute-start.17
  111.0 12.6 %shard_map.295 = (bf16[768,768]{1,0:T(8,128)(2,1)S(1)}, f32[16,768]{1,0:T(8,128)S(1)}, bf16[3136,768]{1,0:T(8,128)(2,1)}) custom-call(s32[1]{0:T(128)} %bitcast.me_ref, bf16[3136,384]{1,0:T(8,128)(2,1)} %bitcast.59, bf16[3136,1536]{1,0:T(8,128)(2,1)} %get-tuple-element.92.act_hbm, bf16[3136,1536]{1,0:T(8,128)(2,1)} %get-tuple-element.93.dg_hbm, ...), custom_call_target="tpu_custom_call" | custom-call | flops 12999999488 | tf_op jit(solution)/shard_map/pallas_call | solution.py:71
  123.8 1.0 collective-permute-start.18
  125.4 0.8 collective-permute-start.20
  126.2 11.0 %shard_map.298 = (bf16[3136,384]{1,0:T(8,128)(2,1)}, f32[3,16,384]{2,1,0:T(8,128)S(1)}) custom-call(s32[1]{0:T(128)} %bitcast.me_ref, bf16[3136,768]{1,0:T(8,128)(2,1)} %get-tuple-element.98.pnear_hbm, bf16[3136,768]{1,0:T(8,128)(2,1)} %get-tuple-element.99.pfar_hbm, bf16[3136,384]{1,0:T(8,128)(2,1)} %bitcast.60, f32[3136,1]{1,0:T(8,128)} %bitcast.64, ...), custom_call_target="tpu_custom_call" | custom-call | flops 11000000512 | tf_op jit(solution)/shard_map/pallas_call | solution.py:71
  137.2 1.8 collective-permute-done.18.refs_1_
  139.1 0.8 collective-permute-start.19
  139.8 16.4 %shard_map.300 = (f32[14,14,16,384]{3,2,1,0:T(8,128)}, f32[8,128]{1,0:T(8,128)S(1)}) custom-call(bf16[14,14,16,384]{3,2,1,0:T(8,128)(2,1)} %bitcast.56, f32[62,384]{1,0:T(8,128)} %reshape.99.refs_0_.small_hbm, s32[16]{0:T(128)S(1)} %copy-done.12, f32[16]{0:T(128)S(1)} %copy-done.13, bf16[14,14,16,384]{3,2,1,0:T(8,128)(2,1)} %bitcast.55, ...), custom_call_target="tpu_custom_call" | custom-call | flops 22000001024 | tf_op jit(solution)/shard_map/pallas_call | solution.py:71
  156.4 1.9 collective-permute-start.21
  158.3 0.7 collective-permute-start.22
  159.0 1.8 collective-permute-start.23
  160.8 13.0 %shard_map.302.gk_ref = f32[49,8,384]{2,1,0:T(8,128)S(1)} custom-call(bf16[14,14,16,384]{3,2,1,0:T(8,128)(2,1)} %bitcast.57, f32[14,14,16,384]{3,2,1,0:T(8,128)} %get-tuple-element.79.refs_1_.mixed_hbm, bf16[2,48,768]{2,1,0:T(8,128)(2,1)S(1)} %get-tuple-element.117.rest_0_, bf16[2,48,768]{2,1,0:T(8,128)(2,1)S(1)} %get-tuple-element.118.rest_1_, ...), custom_call_target="tpu_custom_call" | custom-call | flops 14099999744 | tf_op jit(solution)/shard_map/pallas_call | solution.py:71
  174.4 1.1 collective-permute-start.24
  175.5 1.3 collective-permute-start.25
  176.8 1.2 collective-permute-start.26
  178.5 1.0 collective-permute-done.25.refs_2_
  179.6 2.2 %collective-permute-done.26.refs_3_ = bf16[64,384]{1,0:T(8,128)(2,1)S(1)} collective-permute-done((bf16[64,384]{1,0:T(8,128)(2,1)S(1)}, bf16[64,384]{1,0:T(8,128)(2,1)S(1)}, u32[]{:S(2)}, u32[]{:S(2)}) %collective-permute-start.26) | collective-permute-done | bytes 49184 | tf_op jit(solution)/shard_map/ppermute | solution.py:1083
  182.1 2.4 %collective-permute-start.28 = (bf16[64,384]{1,0:T(8,128)(2,1)S(1)}, bf16[64,384]{1,0:T(8,128)(2,1)S(1)}, u32[]{:S(2)}, u32[]{:S(2)}) collective-permute-start(bf16[64,384]{1,0:T(8,128)(2,1)S(1)} %shard_map.304.refs_0_), channel_id=1, source_target_pairs={{0,16},{1,17},{2,18},{3,19},{4,20},{5,21},{6,22},{7,23},{8,24},{9,... | collective-permute-start | bytes 147464 | tf_op jit(solution)/shard_map/ppermute | solution.py:1083
  184.5 1.7 collective-permute-start.29
  186.3 0.8 collective-permute-done.28.refs_2_
  187.1 3.3 %collective-permute-done.29.refs_3_ = bf16[64,384]{1,0:T(8,128)(2,1)S(1)} collective-permute-done((bf16[64,384]{1,0:T(8,128)(2,1)S(1)}, bf16[64,384]{1,0:T(8,128)(2,1)S(1)}, u32[]{:S(2)}, u32[]{:S(2)}) %collective-permute-start.29) | collective-permute-done | bytes 49184 | tf_op jit(solution)/shard_map/ppermute | solution.py:1083
  190.5 1.2 collective-permute-done.30.refs_1_
  191.9 1.3 shard_map.307
  193.9 0.7 multiply_subtract_fusion
  (101 shorter events, 7.2 us)
Async XLA Ops:
  2.4 4.6 %collective-permute-start = (bf16[744]{0:T(1024)(128)(2,1)S(1)}, bf16[744]{0:T(1024)(128)(2,1)S(1)}, u32[]{:S(2)}, u32[]{:S(2)}) collective-permute-start(bf16[744]{0:T(1024)(128)(2,1)S(1)} %convert_element_type.8), channel_id=1, source_target_pairs={{0,2},{1,3},{2,0},{3,1},{4,6},{5,7},{6,4},{7,5},{8,10},{9,11},{10,... | collective-permute-start | bytes 4472 | tf_op jit(solution)/shard_map/ppermute | solution.py:1083
  7.0 4.7 %collective-permute-start.1 = (bf16[2,744]{1,0:T(2,128)(2,1)S(1)}, bf16[2,744]{1,0:T(2,128)(2,1)S(1)}, u32[]{:S(2)}, u32[]{:S(2)}) collective-permute-start(bf16[2,744]{1,0:T(2,128)(2,1)S(1)} %pad_maximum_fusion.3), channel_id=1, source_target_pairs={{0,4},{1,5},{2,6},{3,7},{4,0},{5,1},{6,2},{7,3},{8,12},{9,13},{10,... | collective-permute-start | bytes 8936 | tf_op jit(solution)/shard_map/ppermute | solution.py:1083
  9.1 5.3 %collective-permute-start.2 = (bf16[1,48,768]{2,1,0:T(8,128)(2,1)S(1)}, bf16[1,48,768]{2,1,0:T(8,128)(2,1)S(1)}, u32[]{:S(2)}, u32[]{:S(2)}) collective-permute-start(bf16[1,48,768]{2,1,0:T(8,128)(2,1)S(1)} %get-tuple-element.75.first_ref), channel_id=1, source_target_pairs={{0,16},{1,17},{2,18},{3,19},{4,20},{5,21},{6,22},{7,23},{8,24},{9,... | collective-permute-start | bytes 221192 | tf_op jit(solution)/shard_map/ppermute | solution.py:1083
  14.4 5.0 %collective-permute-start.3 = (bf16[2,2,744]{2,1,0:T(2,128)(2,1)S(1)}, bf16[2,2,744]{2,1,0:T(2,128)(2,1)S(1)}, u32[]{:S(2)}, u32[]{:S(2)}) collective-permute-start(bf16[2,2,744]{2,1,0:T(2,128)(2,1)S(1)} %pad_maximum_fusion.2), channel_id=1, source_target_pairs={{0,8},{1,9},{2,10},{3,11},{4,12},{5,13},{6,14},{7,15},{8,0},{9,1},... | collective-permute-start | bytes 17864 | tf_op jit(solution)/shard_map/ppermute | solution.py:1083
  16.0 6.2 %collective-permute-start.8 = (bf16[1,48,768]{2,1,0:T(8,128)(2,1)S(1)}, bf16[1,48,768]{2,1,0:T(8,128)(2,1)S(1)}, u32[]{:S(2)}, u32[]{:S(2)}) collective-permute-start(bf16[1,48,768]{2,1,0:T(8,128)(2,1)S(1)} %get-tuple-element.84.first_ref), channel_id=1, source_target_pairs={{0,16},{1,17},{2,18},{3,19},{4,20},{5,21},{6,22},{7,23},{8,24},{9,... | collective-permute-start | bytes 221192 | tf_op jit(solution)/shard_map/ppermute | solution.py:1083
  19.3 5.8 %collective-permute-start.5 = (bf16[2,48,768]{2,1,0:T(8,128)(2,1)S(1)}, bf16[2,48,768]{2,1,0:T(8,128)(2,1)S(1)}, u32[]{:S(2)}, u32[]{:S(2)}) collective-permute-start(bf16[2,48,768]{2,1,0:T(8,128)(2,1)S(1)} %shard_map.281.first_ref), channel_id=1, source_target_pairs={{0,8},{1,9},{2,10},{3,11},{4,12},{5,13},{6,14},{7,15},{8,0},{9,1},... | collective-permute-start | bytes 442376 | tf_op jit(solution)/shard_map/ppermute | solution.py:1083
  19.4 4.8 %collective-permute-start.4 = (bf16[2,2,2,744]{3,2,1,0:T(2,128)(2,1)S(1)}, bf16[2,2,2,744]{3,2,1,0:T(2,128)(2,1)S(1)}, u32[]{:S(2)}, u32[]{:S(2)}) collective-permute-start(bf16[2,2,2,744]{3,2,1,0:T(2,128)(2,1)S(1)} %pad_maximum_fusion.1), channel_id=1, source_target_pairs={{0,16},{1,17},{2,18},{3,19},{4,20},{5,21},{6,22},{7,23},{8,24},{9,... | collective-permute-start | bytes 35720 | tf_op jit(solution)/shard_map/ppermute | solution.py:1083
  22.2 5.2 %collective-permute-start.9 = (bf16[2,48,768]{2,1,0:T(8,128)(2,1)S(1)}, bf16[2,48,768]{2,1,0:T(8,128)(2,1)S(1)}, u32[]{:S(2)}, u32[]{:S(2)}) collective-permute-start(bf16[2,48,768]{2,1,0:T(8,128)(2,1)S(1)} %shard_map.285.first_ref), channel_id=1, source_target_pairs={{0,8},{1,9},{2,10},{3,11},{4,12},{5,13},{6,14},{7,15},{8,0},{9,1},... | collective-permute-start | bytes 442376 | tf_op jit(solution)/shard_map/ppermute | solution.py:1083
  25.1 4.9 %copy-start.12 = (s32[16]{0:T(128)S(1)}, s32[16]{0:T(128)}, u32[]{:S(2)}) copy-start(s32[16]{0:T(128)} %partner_ref.1) | copy-start | bytes 196
  25.1 4.9 %copy-start.13 = (f32[16]{0:T(128)S(1)}, f32[16]{0:T(128)}, u32[]{:S(2)}) copy-start(f32[16]{0:T(128)} %weight_ref.1) | copy-start | bytes 196
  25.1 14.6 %collective-permute-start.7 = (bf16[4,48,768]{2,1,0:T(8,128)(2,1)S(1)}, bf16[4,48,768]{2,1,0:T(8,128)(2,1)S(1)}, u32[]{:S(2)}, u32[]{:S(2)}) collective-permute-start(bf16[4,48,768]{2,1,0:T(8,128)(2,1)S(1)} %shard_map.282.first_ref), channel_id=1, source_target_pairs={{0,4},{1,5},{2,6},{3,7},{4,0},{5,1},{6,2},{7,3},{8,12},{9,13},{10,... | collective-permute-start | bytes 884744 | tf_op jit(solution)/shard_map/ppermute | solution.py:1083
  25.7 3.3 %collective-permute-start.6 = (bf16[2,2,2,2,744]{4,3,2,1,0:T(2,128)(2,1)S(1)}, bf16[2,2,2,2,744]{4,3,2,1,0:T(2,128)(2,1)S(1)}, u32[]{:S(2)}, u32[]{:S(2)}) collective-permute-start(bf16[2,2,2,2,744]{4,3,2,1,0:T(2,128)(2,1)S(1)} %pad_maximum_fusion), channel_id=1, source_target_pairs={{0,1},{1,0},{2,3},{3,2},{4,5},{5,4},{6,7},{7,6},{8,9},{9,8},{10,11... | collective-permute-start | bytes 71432 | tf_op jit(solution)/shard_map/ppermute | solution.py:1083
  27.4 11.7 %collective-permute-start.10 = (bf16[4,48,768]{2,1,0:T(8,128)(2,1)S(1)}, bf16[4,48,768]{2,1,0:T(8,128)(2,1)S(1)}, u32[]{:S(2)}, u32[]{:S(2)}) collective-permute-start(bf16[4,48,768]{2,1,0:T(8,128)(2,1)S(1)} %shard_map.286.first_ref), channel_id=1, source_target_pairs={{0,2},{1,3},{2,0},{3,1},{4,6},{5,7},{6,4},{7,5},{8,10},{9,11},{10,... | collective-permute-start | bytes 884744 | tf_op jit(solution)/shard_map/ppermute | solution.py:1083
  39.2 13.8 %collective-permute-start.12 = (bf16[8,48,768]{2,1,0:T(8,128)(2,1)S(1)}, bf16[8,48,768]{2,1,0:T(8,128)(2,1)S(1)}, u32[]{:S(2)}, u32[]{:S(2)}) collective-permute-start(bf16[8,48,768]{2,1,0:T(8,128)(2,1)S(1)} %shard_map.287.refs_6_.first_ref), channel_id=1, source_target_pairs={{0,4},{1,5},{2,6},{3,7},{4,0},{5,1},{6,2},{7,3},{8,12},{9,13},{10,... | collective-permute-start | bytes 1769480 | tf_op jit(solution)/shard_map/ppermute | solution.py:1083
  39.8 14.6 %collective-permute-start.11 = (bf16[8,48,768]{2,1,0:T(8,128)(2,1)S(1)}, bf16[8,48,768]{2,1,0:T(8,128)(2,1)S(1)}, u32[]{:S(2)}, u32[]{:S(2)}) collective-permute-start(bf16[8,48,768]{2,1,0:T(8,128)(2,1)S(1)} %shard_map.284.refs_5_.first_ref), channel_id=1, source_target_pairs={{0,2},{1,3},{2,0},{3,1},{4,6},{5,7},{6,4},{7,5},{8,10},{9,11},{10,... | collective-permute-start | bytes 1769480 | tf_op jit(solution)/shard_map/ppermute | solution.py:1083
  53.1 9.4 %copy-start.1 = (bf16[16,48,768]{2,1,0:T(8,128)(2,1)}, bf16[16,48,768]{2,1,0:T(8,128)(2,1)S(1)}, u32[]{:S(2)}) copy-start(bf16[16,48,768]{2,1,0:T(8,128)(2,1)S(1)} %shard_map.290.refs_6_) | copy-start | bytes 3538948
  53.1 9.4 %collective-permute-start.14 = (bf16[16,48,768]{2,1,0:T(8,128)(2,1)S(1)}, bf16[16,48,768]{2,1,0:T(8,128)(2,1)S(1)}, u32[]{:S(2)}, u32[]{:S(2)}) collective-permute-start(bf16[16,48,768]{2,1,0:T(8,128)(2,1)S(1)} %shard_map.290.refs_6_), channel_id=1, source_target_pairs={{0,1},{1,0},{2,3},{3,2},{4,5},{5,4},{6,7},{7,6},{8,9},{9,8},{10,11... | collective-permute-start | bytes 3538952 | tf_op jit(solution)/shard_map/ppermute | solution.py:1083
  54.5 8.1 %copy-start = (bf16[16,48,768]{2,1,0:T(8,128)(2,1)}, bf16[16,48,768]{2,1,0:T(8,128)(2,1)S(1)}, u32[]{:S(2)}) copy-start(bf16[16,48,768]{2,1,0:T(8,128)(2,1)S(1)} %shard_map.289.refs_5_) | copy-start | bytes 3538948
  54.5 8.1 %collective-permute-start.13 = (bf16[16,48,768]{2,1,0:T(8,128)(2,1)S(1)}, bf16[16,48,768]{2,1,0:T(8,128)(2,1)S(1)}, u32[]{:S(2)}, u32[]{:S(2)}) collective-permute-start(bf16[16,48,768]{2,1,0:T(8,128)(2,1)S(1)} %shard_map.289.refs_5_), channel_id=1, source_target_pairs={{0,1},{1,0},{2,3},{3,2},{4,5},{5,4},{6,7},{7,6},{8,9},{9,8},{10,11... | collective-permute-start | bytes 3538952 | tf_op jit(solution)/shard_map/ppermute | solution.py:1083
  96.3 13.3 %collective-permute-start.15 = (bf16[16,48,768]{2,1,0:T(8,128)(2,1)}, bf16[16,48,768]{2,1,0:T(8,128)(2,1)S(1)}, u32[]{:S(2)}, u32[]{:S(2)}) collective-permute-start(bf16[16,48,768]{2,1,0:T(8,128)(2,1)} %bitcast.52), channel_id=1, source_target_pairs={{0,1},{1,0},{2,3},{3,2},{4,5},{5,4},{6,7},{7,6},{8,9},{9,8},{10,11... | collective-permute-start | bytes 3538952 | tf_op jit(solution)/shard_map/ppermute | solution.py:1083
  96.4 13.1 %copy-start.2 = (bf16[768,768]{1,0:T(8,128)(2,1)S(1)}, bf16[768,768]{1,0:T(8,128)(2,1)}, u32[]{:S(2)}) copy-start(bf16[768,768]{1,0:T(8,128)(2,1)} %get-tuple-element.94) | copy-start | bytes 3538948
  109.1 14.4 %collective-permute-start.16 = (bf16[16,48,768]{2,1,0:T(8,128)(2,1)S(1)}, bf16[16,48,768]{2,1,0:T(8,128)(2,1)S(1)}, u32[]{:S(2)}, u32[]{:S(2)}) collective-permute-start(bf16[16,48,768]{2,1,0:T(8,128)(2,1)S(1)} %bitcast.45), channel_id=1, source_target_pairs={{0,1},{1,0},{2,3},{3,2},{4,5},{5,4},{6,7},{7,6},{8,9},{9,8},{10,11... | collective-permute-start | bytes 3538952 | tf_op jit(solution)/shard_map/ppermute | solution.py:1083
  109.8 15.4 %collective-permute-start.17 = (bf16[8,48,768]{2,1,0:T(8,128)(2,1)S(1)}, bf16[8,48,768]{2,1,0:T(8,128)(2,1)S(1)}, u32[]{:S(2)}, u32[]{:S(2)}) collective-permute-start(bf16[8,48,768]{2,1,0:T(8,128)(2,1)S(1)} %get-tuple-element.97.rest_0_), channel_id=1, source_target_pairs={{0,2},{1,3},{2,0},{3,1},{4,6},{5,7},{6,4},{7,5},{8,10},{9,11},{10,... | collective-permute-start | bytes 1769480 | tf_op jit(solution)/shard_map/ppermute | solution.py:1083
  123.8 15.1 %collective-permute-start.18 = (bf16[8,48,768]{2,1,0:T(8,128)(2,1)S(1)}, bf16[8,48,768]{2,1,0:T(8,128)(2,1)S(1)}, u32[]{:S(2)}, u32[]{:S(2)}) collective-permute-start(bf16[8,48,768]{2,1,0:T(8,128)(2,1)S(1)} %get-tuple-element.105.rest_0_), channel_id=1, source_target_pairs={{0,2},{1,3},{2,0},{3,1},{4,6},{5,7},{6,4},{7,5},{8,10},{9,11},{10,... | collective-permute-start | bytes 1769480 | tf_op jit(solution)/shard_map/ppermute | solution.py:1083
  125.4 30.8 %collective-permute-start.20 = (bf16[4,48,768]{2,1,0:T(8,128)(2,1)S(1)}, bf16[4,48,768]{2,1,0:T(8,128)(2,1)S(1)}, u32[]{:S(2)}, u32[]{:S(2)}) collective-permute-start(bf16[4,48,768]{2,1,0:T(8,128)(2,1)S(1)} %get-tuple-element.107.rest_1_), channel_id=1, source_target_pairs={{0,4},{1,5},{2,6},{3,7},{4,0},{5,1},{6,2},{7,3},{8,12},{9,13},{10,... | collective-permute-start | bytes 884744 | tf_op jit(solution)/shard_map/ppermute | solution.py:1083
  139.1 17.2 %collective-permute-start.19 = (bf16[4,48,768]{2,1,0:T(8,128)(2,1)S(1)}, bf16[4,48,768]{2,1,0:T(8,128)(2,1)S(1)}, u32[]{:S(2)}, u32[]{:S(2)}) collective-permute-start(bf16[4,48,768]{2,1,0:T(8,128)(2,1)S(1)} %get-tuple-element.112.rest_0_), channel_id=1, source_target_pairs={{0,4},{1,5},{2,6},{3,7},{4,0},{5,1},{6,2},{7,3},{8,12},{9,13},{10,... | collective-permute-start | bytes 884744 | tf_op jit(solution)/shard_map/ppermute | solution.py:1083
  156.4 17.4 %collective-permute-start.21 = (bf16[2,48,768]{2,1,0:T(8,128)(2,1)S(1)}, bf16[2,48,768]{2,1,0:T(8,128)(2,1)S(1)}, u32[]{:S(2)}, u32[]{:S(2)}) collective-permute-start(bf16[2,48,768]{2,1,0:T(8,128)(2,1)S(1)} %get-tuple-element.117.rest_0_), channel_id=1, source_target_pairs={{0,16},{1,17},{2,18},{3,19},{4,20},{5,21},{6,22},{7,23},{8,24},{9,... | collective-permute-start | bytes 442376 | tf_op jit(solution)/shard_map/ppermute | solution.py:1083
  158.3 15.5 %collective-permute-start.22 = (bf16[2,48,768]{2,1,0:T(8,128)(2,1)S(1)}, bf16[2,48,768]{2,1,0:T(8,128)(2,1)S(1)}, u32[]{:S(2)}, u32[]{:S(2)}) collective-permute-start(bf16[2,48,768]{2,1,0:T(8,128)(2,1)S(1)} %get-tuple-element.118.rest_1_), channel_id=1, source_target_pairs={{0,8},{1,9},{2,10},{3,11},{4,12},{5,13},{6,14},{7,15},{8,0},{9,1},... | collective-permute-start | bytes 442376 | tf_op jit(solution)/shard_map/ppermute | solution.py:1083
  159.0 14.8 %copy-start.14 = (f32[4,16,384]{2,1,0:T(8,128)S(1)}, f32[4,16,384]{2,1,0:T(8,128)}, u32[]{:S(2)}) copy-start(f32[4,16,384]{2,1,0:T(8,128)} %get-tuple-element.120.sums2_ref) | copy-start | bytes 294916
  159.0 14.8 %copy-start.15 = (f32[16,768]{1,0:T(8,128)S(1)}, f32[16,768]{1,0:T(8,128)}, u32[]{:S(2)}) copy-start(f32[16,768]{1,0:T(8,128)} %get-tuple-element.121.db_ref) | copy-start | bytes 147460
  159.0 14.8 %collective-permute-start.23 = (bf16[2,48,768]{2,1,0:T(8,128)(2,1)S(1)}, bf16[2,48,768]{2,1,0:T(8,128)(2,1)S(1)}, u32[]{:S(2)}, u32[]{:S(2)}) collective-permute-start(bf16[2,48,768]{2,1,0:T(8,128)(2,1)S(1)} %get-tuple-element.119.rest_2_), channel_id=1, source_target_pairs={{0,24},{1,25},{2,26},{3,27},{4,28},{5,29},{6,30},{7,31},{8,16},{9,... | collective-permute-start | bytes 442376 | tf_op jit(solution)/shard_map/ppermute | solution.py:1083
  174.3 17.5 %copy-start.3 = (f32[48,768]{1,0:T(8,128)S(1)}, f32[48,768]{1,0:T(8,128)}, u32[]{:S(2)}) copy-start(f32[48,768]{1,0:T(8,128)} %refs_6_.1) | copy-start | bytes 442372
  174.3 17.5 %copy-start.4 = (f32[48,768]{1,0:T(8,128)S(1)}, f32[48,768]{1,0:T(8,128)}, u32[]{:S(2)}) copy-start(f32[48,768]{1,0:T(8,128)} %refs_7_.1) | copy-start | bytes 442372
  174.3 17.5 %copy-start.5 = (f32[48,768]{1,0:T(8,128)S(1)}, f32[48,768]{1,0:T(8,128)}, u32[]{:S(2)}) copy-start(f32[48,768]{1,0:T(8,128)} %refs_8_.1) | copy-start | bytes 442372
  174.3 17.5 %copy-start.6 = (f32[48,384]{1,0:T(8,128)S(1)}, f32[48,384]{1,0:T(8,128)}, u32[]{:S(2)}) copy-start(f32[48,384]{1,0:T(8,128)} %refs_0_.1) | copy-start | bytes 221188
  174.3 17.5 %copy-start.7 = (f32[48,384]{1,0:T(8,128)S(1)}, f32[48,384]{1,0:T(8,128)}, u32[]{:S(2)}) copy-start(f32[48,384]{1,0:T(8,128)} %refs_3_.3) | copy-start | bytes 221188
  174.3 17.5 %copy-start.8 = (f32[48,384]{1,0:T(8,128)S(1)}, f32[48,384]{1,0:T(8,128)}, u32[]{:S(2)}) copy-start(f32[48,384]{1,0:T(8,128)} %refs_1_.1) | copy-start | bytes 221188
  174.3 17.5 %copy-start.9 = (f32[48,384]{1,0:T(8,128)S(1)}, f32[48,384]{1,0:T(8,128)}, u32[]{:S(2)}) copy-start(f32[48,384]{1,0:T(8,128)} %refs_2_.3) | copy-start | bytes 221188
  174.4 17.5 %copy-start.10 = (f32[48,384]{1,0:T(8,128)S(1)}, f32[48,384]{1,0:T(8,128)}, u32[]{:S(2)}) copy-start(f32[48,384]{1,0:T(8,128)} %refs_4_.1) | copy-start | bytes 221188
  174.4 17.5 %copy-start.11 = (f32[48,384]{1,0:T(8,128)S(1)}, f32[48,384]{1,0:T(8,128)}, u32[]{:S(2)}) copy-start(f32[48,384]{1,0:T(8,128)} %refs_5_.1) | copy-start | bytes 221188
  174.4 4.2 %collective-permute-start.24 = (bf16[64,384]{1,0:T(8,128)(2,1)S(1)}, bf16[64,384]{1,0:T(8,128)(2,1)S(1)}, u32[]{:S(2)}, u32[]{:S(2)}) collective-permute-start(bf16[64,384]{1,0:T(8,128)(2,1)S(1)} %get-tuple-element.123.refs_0_), channel_id=1, source_target_pairs={{0,2},{1,3},{2,0},{3,1},{4,6},{5,7},{6,4},{7,5},{8,10},{9,11},{10,... | collective-permute-start | bytes 147464 | tf_op jit(solution)/shard_map/ppermute | solution.py:1083
  175.5 4.1 %collective-permute-start.25 = (bf16[64,384]{1,0:T(8,128)(2,1)S(1)}, bf16[64,384]{1,0:T(8,128)(2,1)S(1)}, u32[]{:S(2)}, u32[]{:S(2)}) collective-permute-start(bf16[64,384]{1,0:T(8,128)(2,1)S(1)} %get-tuple-element.123.refs_0_), channel_id=1, source_target_pairs={{0,4},{1,5},{2,6},{3,7},{4,0},{5,1},{6,2},{7,3},{8,12},{9,13},{10,... | collective-permute-start | bytes 147464 | tf_op jit(solution)/shard_map/ppermute | solution.py:1083
  176.8 5.0 %collective-permute-start.26 = (bf16[64,384]{1,0:T(8,128)(2,1)S(1)}, bf16[64,384]{1,0:T(8,128)(2,1)S(1)}, u32[]{:S(2)}, u32[]{:S(2)}) collective-permute-start(bf16[64,384]{1,0:T(8,128)(2,1)S(1)} %get-tuple-element.123.refs_0_), channel_id=1, source_target_pairs={{0,6},{1,7},{2,4},{3,5},{4,2},{5,3},{6,0},{7,1},{8,14},{9,15},{10,... | collective-permute-start | bytes 147464 | tf_op jit(solution)/shard_map/ppermute | solution.py:1083
  181.8 4.5 %collective-permute-start.27 = (bf16[64,384]{1,0:T(8,128)(2,1)S(1)}, bf16[64,384]{1,0:T(8,128)(2,1)S(1)}, u32[]{:S(2)}, u32[]{:S(2)}) collective-permute-start(bf16[64,384]{1,0:T(8,128)(2,1)S(1)} %shard_map.304.refs_0_), channel_id=1, source_target_pairs={{0,8},{1,9},{2,10},{3,11},{4,12},{5,13},{6,14},{7,15},{8,0},{9,1},... | collective-permute-start | bytes 147464 | tf_op jit(solution)/shard_map/ppermute | solution.py:1083
  182.1 5.0 %collective-permute-start.28 = (bf16[64,384]{1,0:T(8,128)(2,1)S(1)}, bf16[64,384]{1,0:T(8,128)(2,1)S(1)}, u32[]{:S(2)}, u32[]{:S(2)}) collective-permute-start(bf16[64,384]{1,0:T(8,128)(2,1)S(1)} %shard_map.304.refs_0_), channel_id=1, source_target_pairs={{0,16},{1,17},{2,18},{3,19},{4,20},{5,21},{6,22},{7,23},{8,24},{9,... | collective-permute-start | bytes 147464 | tf_op jit(solution)/shard_map/ppermute | solution.py:1083
  184.5 5.9 %collective-permute-start.29 = (bf16[64,384]{1,0:T(8,128)(2,1)S(1)}, bf16[64,384]{1,0:T(8,128)(2,1)S(1)}, u32[]{:S(2)}, u32[]{:S(2)}) collective-permute-start(bf16[64,384]{1,0:T(8,128)(2,1)S(1)} %shard_map.304.refs_0_), channel_id=1, source_target_pairs={{0,24},{1,25},{2,26},{3,27},{4,28},{5,29},{6,30},{7,31},{8,16},{9,... | collective-permute-start | bytes 147464 | tf_op jit(solution)/shard_map/ppermute | solution.py:1083
  190.4 1.3 collective-permute-start.30
  191.8 2.0 %copy-start.16 = (f32[744]{0:T(1024)S(1)}, f32[744]{0:T(1024)}, u32[]{:S(2)}) copy-start(f32[744]{0:T(1024)} %param.25) | copy-start | bytes 8932
  (4 other events, 6.5 us)

commit v2 on v1

--- a/solution.py
+++ b/solution.py
@@ -466,7 +466,7 @@
     for g in range(6):
         wide[g] = wd_ref[:, pl.ds(g * 128, 128)].astype(F32)
         for k in range(4):
-            wk[k, :, pl.ds(g * 128, 128)] = wide[g, pl.ds(k, D, stride=4), :].astype(BF16)
+            wk[k // 2, pl.ds(k % 2 * D, D), pl.ds(g * 128, 128)] = wide[g, pl.ds(k, D, stride=4), :].astype(BF16)
     sums_ref[...] = jnp.zeros(sums_ref.shape, F32)
     rows = half * half * imgs
     shape = (half * half, imgs, D)
@@ -479,27 +479,28 @@
         pairs = ((bb_ref, bb_hbm), (res_ref, res_hbm))
         return [dma(a.at[k], b.at[:, k // 2, :, k % 2], rsem.at[j, k]) for j, (a, b) in enumerate(pairs)]
 
-    def quarter(k):
+    for a in range(2):
         dy = dy_ref[...].reshape(rows, 2 * D)
-        x = out2_ref[:, k // 2, :, k % 2].reshape(rows, D)
-        back = lax.dot_general(dy, wk[k], COLS, preferred_element_type=F32).reshape(shape)
-        acc[...] += jnp.dot(x, wk[k], preferred_element_type=F32)
+        x = jnp.concatenate([out2_ref[:, a, :, b].reshape(rows, D) for b in range(2)], axis=1)
+        both = lax.dot_general(dy, wk[a], COLS, preferred_element_type=F32)
+        acc[...] += jnp.dot(x, wk[a], preferred_element_type=F32)
         gd = lax.dot_general(x, dy, ROWS, preferred_element_type=F32)
-        for g in range(6):
-            wide[g, pl.ds(k, D, stride=4), :] = gd[:, g * 128 : (g + 1) * 128]
-        unit = unit_ref[:, k // 2, :, k % 2].reshape(shape).astype(F32)
-        sums_ref[0] += jnp.sum(back * unit, axis=0)
-        sums_ref[1] += jnp.sum(back, axis=0)
-        res = norm_back(back, unit, inv_ref[:, k // 2, :, k % 2].reshape(half * half, imgs, 1), gain)
-        res_ref[k] = res.astype(BF16).reshape(half, half, imgs, D)
-        sums_ref[2] += jnp.sum(res * keep * branch_ref[:, k // 2, :, k % 2].reshape(shape).astype(F32), axis=0)
-        bb = (res * scale).astype(BF16)
-        bb_ref[k] = bb.reshape(half, half, imgs, D)
-        start(give(k))
-        sums_ref[3] += jnp.sum(bb.astype(F32), axis=0)
-
-    for k in range(4):
-        quarter(k)
+        for b in range(2):
+            k = 2 * a + b
+            for g in range(6):
+                wide[g, pl.ds(k, D, stride=4), :] = gd[b * D : (b + 1) * D, g * 128 : (g + 1) * 128]
+            back = both[:, b * D : (b + 1) * D].reshape(shape)
+            unit = unit_ref[:, a, :, b].reshape(shape).astype(F32)
+            sums_ref[0] += jnp.sum(back * unit, axis=0)
+            sums_ref[1] += jnp.sum(back, axis=0)
+            res = norm_back(back, unit, inv_ref[:, a, :, b].reshape(half * half, imgs, 1), gain)
+            res_ref[k] = res.astype(BF16).reshape(half, half, imgs, D)
+            sums_ref[2] += jnp.sum(res * keep * branch_ref[:, a, :, b].reshape(shape).astype(F32), axis=0)
+            bb = (res * scale).astype(BF16)
+            bb_ref[k] = bb.reshape(half, half, imgs, D)
+            start(give(k))
+            sums_ref[3] += jnp.sum(bb.astype(F32), axis=0)
+
     out_ref[...] = acc[...].astype(BF16).reshape(out_ref.shape)
     deal(me, d_masks, False, 0, gnear_ref, lambda at, g: wide[g, at, :])
     deal(me, d_masks, False, HALF_PIECES, gfar_ref, lambda at, g: wide[g, at, :])
@@ -528,7 +529,7 @@
         + [two(D, BF16), two(D, F32), two(FF, BF16), two(FF, BF16)]
         + [whole(D, BF16), whole(D, BF16), whole(1, F32), whole(D, BF16)]
         + [pltpu.VMEM((4 * D, 2 * D), BF16), pltpu.VMEM(dy.shape, BF16), part, part]
-        + [pltpu.VMEM((area, 2 * D), F32), pltpu.VMEM((6, 4 * D, 128), F32), pltpu.VMEM((4, D, 2 * D), BF16)]
+        + [pltpu.VMEM((area, 2 * D), F32), pltpu.VMEM((6, 4 * D, 128), F32), pltpu.VMEM((2, 2 * D, 2 * D), BF16)]
         + [pltpu.SemaphoreType.DMA((2, 2)), pltpu.SemaphoreType.DMA((2, 2)), pltpu.SemaphoreType.DMA((4,))]
         + [pltpu.SemaphoreType.DMA((1,)), pltpu.SemaphoreType.DMA((2, 4))],
         (me, norm, mixed, *pair, *down, dy, small, mask),
@@ -539,7 +540,7 @@
 
 
 def pair_grad_kernel(block, first, masks, me_ref, bb_hbm, act_hbm, dg_hbm, norm_hbm, pair_hbm, *rest):
-    g_ref, hb_ref, p_hbm, pair_ref, acc, bb_ref, act_ref, dg_ref, norm_ref, p_ref, sem, osem, wsem = rest[-13:]
+    g_ref, hb_ref, p_hbm, pair_ref, acc, turned, bb_ref, act_ref, dg_ref, norm_ref, p_ref, sem, osem, wsem = rest[-14:]
     rows = bb_hbm.shape[0]
     imgs = hb_ref.shape[0]
     steps = rows // block
@@ -584,21 +585,22 @@
         wait(enter(i))
         b = bb_ref[s]
         back = lax.dot_general(b, pair_ref[:, D:], COLS, preferred_element_type=F32)
-        acc[:, D:] += lax.dot_general(act_ref[s], b, ROWS, preferred_element_type=F32)
+        acc[D:, :] += lax.dot_general(b, act_ref[s], ROWS, preferred_element_type=F32)
         p = (back * dg_ref[s].astype(F32)).astype(BF16)
         p_ref[s] = p
         hb_ref[...] += jnp.sum(p.astype(F32).reshape(block // imgs, imgs, wide), axis=0)
-        acc[:, :D] += lax.dot_general(p, norm_ref[s], ROWS, preferred_element_type=F32)
+        acc[:D, :] += lax.dot_general(norm_ref[s], p, ROWS, preferred_element_type=F32)
         leave(i).start()
         return 0
 
     lax.fori_loop(0, steps, body, 0)
-    deal(me, masks, True, first, g_ref, lambda at, g: acc[at, pl.ds(g * 128, 128)])
+    turned[...] = acc[...].T
+    deal(me, masks, True, first, g_ref, lambda at, g: turned[at, pl.ds(g * 128, 128)])
     for i in range(max(steps - 2, 0), steps):
         leave(i).wait()
 
 
-def pair_grad(first, masks, me, bb, act, dg, norm, pair, imgs, after=(), block=448):
+def pair_grad(first, masks, me, bb, act, dg, norm, pair, imgs, after=(), block=784):
     rows = bb.shape[0]
     wide = FF // 2
     two = lambda width: pltpu.VMEM((2, block, width), BF16)
@@ -606,13 +608,13 @@
         functools.partial(pair_grad_kernel, block, first, masks),
         [near((wide, 2 * D), BF16), near((imgs, wide), F32), far((rows, wide), BF16)],
         [SMEM] + [HBM] * 5,
-        [pltpu.VMEM((wide, 2 * D), BF16), pltpu.VMEM((wide, 2 * D), F32)]
+        [pltpu.VMEM((wide, 2 * D), BF16), pltpu.VMEM((2 * D, wide), F32), pltpu.VMEM((wide, 2 * D), F32)]
         + [two(D), two(wide), two(wide), two(D), two(wide)]
         + [pltpu.SemaphoreType.DMA((4, 2)), pltpu.SemaphoreType.DMA((2,)), pltpu.SemaphoreType.DMA((1,))],
         (me, bb, act, dg, norm, pair),
         after,
         13,
-        28,
+        44,
     )
 
 
@@ -1128,9 +1130,9 @@
     cut = [0, 3, 10, side]
     gates = None
     if by_hops:
-        gates = {0: pair}
+        gates = {1: pair}
         pair = join(pair, swap(pair, p_order[0], n))
-        gates[2] = pair
+        gates[3] = pair
         down = join(down, swap(down, w_order[0], n))
         pair = join(pair, swap(pair, p_order[1], n))
         gates[4] = pair

time: 195 us -> 193 us (0.990)
  waiting for transfers between devices: 23.3 us -> 20.2 us
  Pallas kernels: 130 us -> 127 us
  starting transfers between devices: 35.5 us -> 38.5 us
    ppermute x31, waiting for transfers between devices: 23.3 us -> 20.2 us  [swap(): return lax.ppermute(x, 'dp', [(i, i ^ bit) for i in range(n)])]
    ppermute x31, starting transfers between devices: 35.5 us -> 38.5 us  [swap(): return lax.ppermute(x, 'dp', [(i, i ^ bit) for i in range(n)])]
    pallas_call x27, Pallas kernels: 129 us -> 126 us  [kernel_call(): pl.pallas_call(body, out_shape=tuple(out), in_specs=specs, out_specs=tupl...]
  transfers between devices with their start and end apart: 31 -> 31, of which waited for: 16 -> 17; matrix products, arithmetic and copies ran while one was open for 1% -> 1% of each run, Pallas kernels for 49% -> 49%
where the time goes in v2:
time: 193 us; the launch traced here: 192 us
  Pallas kernels  127 us (66%)
  starting transfers between devices  38.5 us (20%)
  waiting for transfers between devices  20.2 us (10%)
  local copies, waits for them, and re-layouts  2.44 us (1%)
  between operations  1.96 us (1%)
    pallas_call x27, Pallas kernels, kernel_call(): pl.pallas_call(body, out_shape=tuple(out), in_specs=specs, out_specs=tupl...  126 us
    ppermute x31, starting transfers between devices, swap(): return lax.ppermute(x, 'dp', [(i, i ^ bit) for i in range(n)])  38.5 us
    ppermute x31, waiting for transfers between devices, swap(): return lax.ppermute(x, 'dp', [(i, i ^ bit) for i in range(n)])  20.2 us
  transfers between devices with their start and end apart: 31, of which 17 were waited for; matrix products, arithmetic and copies ran while one was open for 1% of the time, Pallas kernels for 49%

profile of v2, /device:TPU:0, one launch (start us, length us, event | category | flops | bytes accessed | tf_op | source)
XLA Modules:
  0.0 192.3 jit_solution(2001207267899516076)
XLA Ops:
  0.7 0.8 convert_element_type.8
  1.4 2.9 %collective-permute-start = (bf16[744]{0:T(1024)(128)(2,1)S(1)}, bf16[744]{0:T(1024)(128)(2,1)S(1)}, u32[]{:S(2)}, u32[]{:S(2)}) collective-permute-start(bf16[744]{0:T(1024)(128)(2,1)S(1)} %convert_element_type.8), channel_id=1, source_target_pairs={{0,2},{1,3},{2,0},{3,1},{4,6},{5,7},{6,4},{7,5},{8,10},{9,11},{10,... | collective-permute-start | bytes 4472 | tf_op jit(solution)/shard_map/ppermute | solution.py:1085
  4.3 1.0 shard_map.280
  6.0 2.1 %collective-permute-start.1 = (bf16[2,744]{1,0:T(2,128)(2,1)S(1)}, bf16[2,744]{1,0:T(2,128)(2,1)S(1)}, u32[]{:S(2)}, u32[]{:S(2)}) collective-permute-start(bf16[2,744]{1,0:T(2,128)(2,1)S(1)} %pad_maximum_fusion.3), channel_id=1, source_target_pairs={{0,4},{1,5},{2,6},{3,7},{4,0},{5,1},{6,2},{7,3},{8,12},{9,13},{10,... | collective-permute-start | bytes 8936 | tf_op jit(solution)/shard_map/ppermute | solution.py:1085
  8.1 1.6 collective-permute-done.1
  9.7 2.1 %collective-permute-start.2 = (bf16[2,2,744]{2,1,0:T(2,128)(2,1)S(1)}, bf16[2,2,744]{2,1,0:T(2,128)(2,1)S(1)}, u32[]{:S(2)}, u32[]{:S(2)}) collective-permute-start(bf16[2,2,744]{2,1,0:T(2,128)(2,1)S(1)} %pad_maximum_fusion.2), channel_id=1, source_target_pairs={{0,8},{1,9},{2,10},{3,11},{4,12},{5,13},{6,14},{7,15},{8,0},{9,1},... | collective-permute-start | bytes 17864 | tf_op jit(solution)/shard_map/ppermute | solution.py:1085
  11.8 2.6 %collective-permute-start.3 = (bf16[1,48,768]{2,1,0:T(8,128)(2,1)S(1)}, bf16[1,48,768]{2,1,0:T(8,128)(2,1)S(1)}, u32[]{:S(2)}, u32[]{:S(2)}) collective-permute-start(bf16[1,48,768]{2,1,0:T(8,128)(2,1)S(1)} %get-tuple-element.75.first_ref), channel_id=1, source_target_pairs={{0,16},{1,17},{2,18},{3,19},{4,20},{5,21},{6,22},{7,23},{8,24},{9,... | collective-permute-start | bytes 221192 | tf_op jit(solution)/shard_map/ppermute | solution.py:1085
  14.8 3.4 %collective-permute-done.3.second_ref = bf16[1,48,768]{2,1,0:T(8,128)(2,1)S(1)} collective-permute-done((bf16[1,48,768]{2,1,0:T(8,128)(2,1)S(1)}, bf16[1,48,768]{2,1,0:T(8,128)(2,1)S(1)}, u32[]{:S(2)}, u32[]{:S(2)}) %collective-permute-start.3) | collective-permute-done | bytes 73760 | tf_op jit(solution)/shard_map/ppermute | solution.py:1085
  18.3 2.3 %collective-permute-start.4 = (bf16[2,2,2,744]{3,2,1,0:T(2,128)(2,1)S(1)}, bf16[2,2,2,744]{3,2,1,0:T(2,128)(2,1)S(1)}, u32[]{:S(2)}, u32[]{:S(2)}) collective-permute-start(bf16[2,2,2,744]{3,2,1,0:T(2,128)(2,1)S(1)} %pad_maximum_fusion.1), channel_id=1, source_target_pairs={{0,16},{1,17},{2,18},{3,19},{4,20},{5,21},{6,22},{7,23},{8,24},{9,... | collective-permute-start | bytes 35720 | tf_op jit(solution)/shard_map/ppermute | solution.py:1085
  20.6 2.0 %collective-permute-start.9 = (bf16[2,48,768]{2,1,0:T(8,128)(2,1)S(1)}, bf16[2,48,768]{2,1,0:T(8,128)(2,1)S(1)}, u32[]{:S(2)}, u32[]{:S(2)}) collective-permute-start(bf16[2,48,768]{2,1,0:T(8,128)(2,1)S(1)} %shard_map.285.first_ref), channel_id=1, source_target_pairs={{0,8},{1,9},{2,10},{3,11},{4,12},{5,13},{6,14},{7,15},{8,0},{9,1},... | collective-permute-start | bytes 442376 | tf_op jit(solution)/shard_map/ppermute | solution.py:1085
  23.7 1.4 collective-permute-start.7
  25.2 0.6 collective-permute-done.9.second_ref
  25.8 1.5 collective-permute-start.10
  27.5 0.8 reshape.99.refs_0_.small_hbm
  28.4 9.1 %shard_map.283 = (f32[14,14,16,384]{3,2,1,0:T(8,128)}, bf16[14,14,16,384]{3,2,1,0:T(8,128)(2,1)}, f32[14,14,16,1]{3,2,1,0:T(8,128)}, bf16[14,14,16,384]{3,2,1,0:T(8,128)(2,1)}, f32[8,128]{1,0:T(8,128)S(1)}) custom-call(f32[62,384]{1,0:T(8,128)} %reshape.99.refs_0_.small_hbm, bf16[14,14,16,384]{3,2,1,0:T(8,128)(2,1)} %bitcast.46, s32[16]{0:T(128)S(1)} %copy-done.12, ...), custom_call_target="tpu_custom_call" | custom-call | flops 7500000256 | tf_op jit(solution)/shard_map/pallas_call | solution.py:71
  37.6 1.6 collective-permute-start.12
  39.8 10.9 %shard_map.288 = (bf16[14,14,16,384]{3,2,1,0:T(8,128)(2,1)}, f32[14,14,16,1]{3,2,1,0:T(8,128)}, bf16[14,14,16,384]{3,2,1,0:T(8,128)(2,1)}, f32[8,128]{1,0:T(8,128)S(1)}) custom-call(f32[62,384]{1,0:T(8,128)} %reshape.99.refs_0_.small_hbm, ...), custom_call_target="tpu_custom_call", output_to_operand_aliasing={{0}: (2, {}), {1}: (3, {}), {2}: (4, {})} | custom-call | flops 10499999744 | tf_op jit(solution)/shard_map/pallas_call | solution.py:71
  50.7 1.8 collective-permute-done.12.second_ref
  53.3 7.7 %shard_map.291 = (bf16[14,14,16,384]{3,2,1,0:T(8,128)(2,1)}, f32[14,14,16,1]{3,2,1,0:T(8,128)}, bf16[14,14,16,384]{3,2,1,0:T(8,128)(2,1)}, f32[8,128]{1,0:T(8,128)}) custom-call(f32[62,384]{1,0:T(8,128)} %reshape.99.refs_0_.small_hbm, ...), custom_call_target="tpu_custom_call", output_to_operand_aliasing={{0}: (2, {}), {1}: (3, {}), {2}: (4, {})} | custom-call | flops 6000000000 | tf_op jit(solution)/shard_map/pallas_call | solution.py:71
  61.1 1.1 copy-done.20
  62.5 31.5 %shard_map.292 = (bf16[3136,1536]{1,0:T(8,128)(2,1)}, bf16[3136,1536]{1,0:T(8,128)(2,1)}, bf16[768,768]{1,0:T(8,128)(2,1)}, bf16[768,768]{1,0:T(8,128)(2,1)}, f3...) custom-call(s32[1]{0:T(128)} %bitcast.me_ref, ...), custom_call_target="tpu_custom_call" | custom-call | flops 33999998976 | tf_op jit(solution)/shard_map/pallas_call | solution.py:71
  94.4 12.1 %shard_map.293 = (bf16[768,768]{1,0:T(8,128)(2,1)S(1)}, f32[16,768]{1,0:T(8,128)S(1)}, bf16[3136,768]{1,0:T(8,128)(2,1)}) custom-call(s32[1]{0:T(128)} %bitcast.me_ref, bf16[3136,384]{1,0:T(8,128)(2,1)} %bitcast.58, bf16[3136,1536]{1,0:T(8,128)(2,1)} %get-tuple-element.92.act_hbm, bf16[3136,1536]{1,0:T(8,128)(2,1)} %get-tuple-element.93.dg_hbm, ...), custom_call_target="tpu_custom_call" | custom-call | flops 12999999488 | tf_op jit(solution)/shard_map/pallas_call | solution.py:71
  107.1 1.1 collective-permute-start.17
  108.2 11.8 %shard_map.295 = (bf16[768,768]{1,0:T(8,128)(2,1)S(1)}, f32[16,768]{1,0:T(8,128)S(1)}, bf16[3136,768]{1,0:T(8,128)(2,1)}) custom-call(s32[1]{0:T(128)} %bitcast.me_ref, bf16[3136,384]{1,0:T(8,128)(2,1)} %bitcast.59, bf16[3136,1536]{1,0:T(8,128)(2,1)} %get-tuple-element.92.act_hbm, bf16[3136,1536]{1,0:T(8,128)(2,1)} %get-tuple-element.93.dg_hbm, ...), custom_call_target="tpu_custom_call" | custom-call | flops 12999999488 | tf_op jit(solution)/shard_map/pallas_call | solution.py:71
  120.3 1.0 collective-permute-start.18
  121.4 1.3 collective-permute-done.17.refs_1_
  122.8 1.4 collective-permute-start.20
  124.2 11.0 %shard_map.298 = (bf16[3136,384]{1,0:T(8,128)(2,1)}, f32[3,16,384]{2,1,0:T(8,128)S(1)}) custom-call(s32[1]{0:T(128)} %bitcast.me_ref, bf16[3136,768]{1,0:T(8,128)(2,1)} %get-tuple-element.98.pnear_hbm, bf16[3136,768]{1,0:T(8,128)(2,1)} %get-tuple-element.99.pfar_hbm, bf16[3136,384]{1,0:T(8,128)(2,1)} %bitcast.60, f32[3136,1]{1,0:T(8,128)} %bitcast.64, ...), custom_call_target="tpu_custom_call" | custom-call | flops 11000000512 | tf_op jit(solution)/shard_map/pallas_call | solution.py:71
  135.7 1.4 collective-permute-start.19
  137.1 16.4 %shard_map.300 = (f32[14,14,16,384]{3,2,1,0:T(8,128)}, f32[8,128]{1,0:T(8,128)S(1)}) custom-call(bf16[14,14,16,384]{3,2,1,0:T(8,128)(2,1)} %bitcast.56, f32[62,384]{1,0:T(8,128)} %reshape.99.refs_0_.small_hbm, s32[16]{0:T(128)S(1)} %copy-done.12, f32[16]{0:T(128)S(1)} %copy-done.13, bf16[14,14,16,384]{3,2,1,0:T(8,128)(2,1)} %bitcast.55, ...), custom_call_target="tpu_custom_call" | custom-call | flops 22000001024 | tf_op jit(solution)/shard_map/pallas_call | solution.py:71
  153.7 2.1 %collective-permute-start.21 = (bf16[2,48,768]{2,1,0:T(8,128)(2,1)S(1)}, bf16[2,48,768]{2,1,0:T(8,128)(2,1)S(1)}, u32[]{:S(2)}, u32[]{:S(2)}) collective-permute-start(bf16[2,48,768]{2,1,0:T(8,128)(2,1)S(1)} %get-tuple-element.117.rest_0_), channel_id=1, source_target_pairs={{0,16},{1,17},{2,18},{3,19},{4,20},{5,21},{6,22},{7,23},{8,24},{9,... | collective-permute-start | bytes 442376 | tf_op jit(solution)/shard_map/ppermute | solution.py:1085
  155.8 1.7 collective-permute-start.22
  157.5 0.9 collective-permute-start.23
  158.4 13.0 %shard_map.302.gk_ref = f32[49,8,384]{2,1,0:T(8,128)S(1)} custom-call(bf16[14,14,16,384]{3,2,1,0:T(8,128)(2,1)} %bitcast.57, f32[14,14,16,384]{3,2,1,0:T(8,128)} %get-tuple-element.79.refs_1_.mixed_hbm, bf16[2,48,768]{2,1,0:T(8,128)(2,1)S(1)} %get-tuple-element.117.rest_0_, bf16[2,48,768]{2,1,0:T(8,128)(2,1)S(1)} %get-tuple-element.118.rest_1_, ...), custom_call_target="tpu_custom_call" | custom-call | flops 14099999744 | tf_op jit(solution)/shard_map/pallas_call | solution.py:71
  171.9 1.0 collective-permute-start.24
  173.0 0.7 collective-permute-start.25
  173.6 1.8 collective-permute-start.26
  175.5 0.6 collective-permute-done.24.refs_1_
  176.1 1.0 collective-permute-done.25.refs_2_
  177.1 1.6 collective-permute-done.26.refs_3_
  178.7 1.2 collective-permute-start.27
  179.9 2.4 %collective-permute-start.28 = (bf16[64,384]{1,0:T(8,128)(2,1)S(1)}, bf16[64,384]{1,0:T(8,128)(2,1)S(1)}, u32[]{:S(2)}, u32[]{:S(2)}) collective-permute-start(bf16[64,384]{1,0:T(8,128)(2,1)S(1)} %shard_map.304.refs_0_), channel_id=1, source_target_pairs={{0,16},{1,17},{2,18},{3,19},{4,20},{5,21},{6,22},{7,23},{8,24},{9,... | collective-permute-start | bytes 147464 | tf_op jit(solution)/shard_map/ppermute | solution.py:1085
  182.2 0.9 collective-permute-start.29
  183.3 2.0 %collective-permute-done.28.refs_2_ = bf16[64,384]{1,0:T(8,128)(2,1)S(1)} collective-permute-done((bf16[64,384]{1,0:T(8,128)(2,1)S(1)}, bf16[64,384]{1,0:T(8,128)(2,1)S(1)}, u32[]{:S(2)}, u32[]{:S(2)}) %collective-permute-start.28) | collective-permute-done | bytes 49184 | tf_op jit(solution)/shard_map/ppermute | solution.py:1085
  185.4 2.7 %collective-permute-done.29.refs_3_ = bf16[64,384]{1,0:T(8,128)(2,1)S(1)} collective-permute-done((bf16[64,384]{1,0:T(8,128)(2,1)S(1)}, bf16[64,384]{1,0:T(8,128)(2,1)S(1)}, u32[]{:S(2)}, u32[]{:S(2)}) %collective-permute-start.29) | collective-permute-done | bytes 49184 | tf_op jit(solution)/shard_map/ppermute | solution.py:1085
  188.2 1.2 collective-permute-done.30.refs_1_
  189.6 1.3 shard_map.307
  191.6 0.7 multiply_subtract_fusion
  (101 shorter events, 7.0 us)
Async XLA Ops:
  0.6 5.3 %copy-start.16 = (f32[744]{0:T(1024)S(1)}, f32[744]{0:T(1024)}, u32[]{:S(2)}) copy-start(f32[744]{0:T(1024)} %param.25) | copy-start | bytes 8932
  1.4 4.5 %collective-permute-start = (bf16[744]{0:T(1024)(128)(2,1)S(1)}, bf16[744]{0:T(1024)(128)(2,1)S(1)}, u32[]{:S(2)}, u32[]{:S(2)}) collective-permute-start(bf16[744]{0:T(1024)(128)(2,1)S(1)} %convert_element_type.8), channel_id=1, source_target_pairs={{0,2},{1,3},{2,0},{3,1},{4,6},{5,7},{6,4},{7,5},{8,10},{9,11},{10,... | collective-permute-start | bytes 4472 | tf_op jit(solution)/shard_map/ppermute | solution.py:1085
  6.0 3.7 %collective-permute-start.1 = (bf16[2,744]{1,0:T(2,128)(2,1)S(1)}, bf16[2,744]{1,0:T(2,128)(2,1)S(1)}, u32[]{:S(2)}, u32[]{:S(2)}) collective-permute-start(bf16[2,744]{1,0:T(2,128)(2,1)S(1)} %pad_maximum_fusion.3), channel_id=1, source_target_pairs={{0,4},{1,5},{2,6},{3,7},{4,0},{5,1},{6,2},{7,3},{8,12},{9,13},{10,... | collective-permute-start | bytes 8936 | tf_op jit(solution)/shard_map/ppermute | solution.py:1085
  9.7 5.1 %collective-permute-start.2 = (bf16[2,2,744]{2,1,0:T(2,128)(2,1)S(1)}, bf16[2,2,744]{2,1,0:T(2,128)(2,1)S(1)}, u32[]{:S(2)}, u32[]{:S(2)}) collective-permute-start(bf16[2,2,744]{2,1,0:T(2,128)(2,1)S(1)} %pad_maximum_fusion.2), channel_id=1, source_target_pairs={{0,8},{1,9},{2,10},{3,11},{4,12},{5,13},{6,14},{7,15},{8,0},{9,1},... | collective-permute-start | bytes 17864 | tf_op jit(solution)/shard_map/ppermute | solution.py:1085
  11.8 6.3 %collective-permute-start.3 = (bf16[1,48,768]{2,1,0:T(8,128)(2,1)S(1)}, bf16[1,48,768]{2,1,0:T(8,128)(2,1)S(1)}, u32[]{:S(2)}, u32[]{:S(2)}) collective-permute-start(bf16[1,48,768]{2,1,0:T(8,128)(2,1)S(1)} %get-tuple-element.75.first_ref), channel_id=1, source_target_pairs={{0,16},{1,17},{2,18},{3,19},{4,20},{5,21},{6,22},{7,23},{8,24},{9,... | collective-permute-start | bytes 221192 | tf_op jit(solution)/shard_map/ppermute | solution.py:1085
  14.4 6.1 %collective-permute-start.8 = (bf16[1,48,768]{2,1,0:T(8,128)(2,1)S(1)}, bf16[1,48,768]{2,1,0:T(8,128)(2,1)S(1)}, u32[]{:S(2)}, u32[]{:S(2)}) collective-permute-start(bf16[1,48,768]{2,1,0:T(8,128)(2,1)S(1)} %get-tuple-element.84.first_ref), channel_id=1, source_target_pairs={{0,16},{1,17},{2,18},{3,19},{4,20},{5,21},{6,22},{7,23},{8,24},{9,... | collective-permute-start | bytes 221192 | tf_op jit(solution)/shard_map/ppermute | solution.py:1085
  18.2 5.5 %collective-permute-start.5 = (bf16[2,48,768]{2,1,0:T(8,128)(2,1)S(1)}, bf16[2,48,768]{2,1,0:T(8,128)(2,1)S(1)}, u32[]{:S(2)}, u32[]{:S(2)}) collective-permute-start(bf16[2,48,768]{2,1,0:T(8,128)(2,1)S(1)} %shard_map.281.first_ref), channel_id=1, source_target_pairs={{0,8},{1,9},{2,10},{3,11},{4,12},{5,13},{6,14},{7,15},{8,0},{9,1},... | collective-permute-start | bytes 442376 | tf_op jit(solution)/shard_map/ppermute | solution.py:1085
  18.3 4.8 %collective-permute-start.4 = (bf16[2,2,2,744]{3,2,1,0:T(2,128)(2,1)S(1)}, bf16[2,2,2,744]{3,2,1,0:T(2,128)(2,1)S(1)}, u32[]{:S(2)}, u32[]{:S(2)}) collective-permute-start(bf16[2,2,2,744]{3,2,1,0:T(2,128)(2,1)S(1)} %pad_maximum_fusion.1), channel_id=1, source_target_pairs={{0,16},{1,17},{2,18},{3,19},{4,20},{5,21},{6,22},{7,23},{8,24},{9,... | collective-permute-start | bytes 35720 | tf_op jit(solution)/shard_map/ppermute | solution.py:1085
  20.6 5.2 %collective-permute-start.9 = (bf16[2,48,768]{2,1,0:T(8,128)(2,1)S(1)}, bf16[2,48,768]{2,1,0:T(8,128)(2,1)S(1)}, u32[]{:S(2)}, u32[]{:S(2)}) collective-permute-start(bf16[2,48,768]{2,1,0:T(8,128)(2,1)S(1)} %shard_map.285.first_ref), channel_id=1, source_target_pairs={{0,8},{1,9},{2,10},{3,11},{4,12},{5,13},{6,14},{7,15},{8,0},{9,1},... | collective-permute-start | bytes 442376 | tf_op jit(solution)/shard_map/ppermute | solution.py:1085
  23.7 4.6 %copy-start.12 = (s32[16]{0:T(128)S(1)}, s32[16]{0:T(128)}, u32[]{:S(2)}) copy-start(s32[16]{0:T(128)} %partner_ref.1) | copy-start | bytes 196
  23.7 4.6 %copy-start.13 = (f32[16]{0:T(128)S(1)}, f32[16]{0:T(128)}, u32[]{:S(2)}) copy-start(f32[16]{0:T(128)} %weight_ref.1) | copy-start | bytes 196
  23.7 15.4 %collective-permute-start.7 = (bf16[4,48,768]{2,1,0:T(8,128)(2,1)S(1)}, bf16[4,48,768]{2,1,0:T(8,128)(2,1)S(1)}, u32[]{:S(2)}, u32[]{:S(2)}) collective-permute-start(bf16[4,48,768]{2,1,0:T(8,128)(2,1)S(1)} %shard_map.282.first_ref), channel_id=1, source_target_pairs={{0,4},{1,5},{2,6},{3,7},{4,0},{5,1},{6,2},{7,3},{8,12},{9,13},{10,... | collective-permute-start | bytes 884744 | tf_op jit(solution)/shard_map/ppermute | solution.py:1085
  25.2 2.2 %collective-permute-start.6 = (bf16[2,2,2,2,744]{4,3,2,1,0:T(2,128)(2,1)S(1)}, bf16[2,2,2,2,744]{4,3,2,1,0:T(2,128)(2,1)S(1)}, u32[]{:S(2)}, u32[]{:S(2)}) collective-permute-start(bf16[2,2,2,2,744]{4,3,2,1,0:T(2,128)(2,1)S(1)} %pad_maximum_fusion), channel_id=1, source_target_pairs={{0,1},{1,0},{2,3},{3,2},{4,5},{5,4},{6,7},{7,6},{8,9},{9,8},{10,11... | collective-permute-start | bytes 71432 | tf_op jit(solution)/shard_map/ppermute | solution.py:1085
  25.8 11.7 %collective-permute-start.10 = (bf16[4,48,768]{2,1,0:T(8,128)(2,1)S(1)}, bf16[4,48,768]{2,1,0:T(8,128)(2,1)S(1)}, u32[]{:S(2)}, u32[]{:S(2)}) collective-permute-start(bf16[4,48,768]{2,1,0:T(8,128)(2,1)S(1)} %shard_map.286.first_ref), channel_id=1, source_target_pairs={{0,2},{1,3},{2,0},{3,1},{4,6},{5,7},{6,4},{7,5},{8,10},{9,11},{10,... | collective-permute-start | bytes 884744 | tf_op jit(solution)/shard_map/ppermute | solution.py:1085
  37.6 14.9 %collective-permute-start.12 = (bf16[8,48,768]{2,1,0:T(8,128)(2,1)S(1)}, bf16[8,48,768]{2,1,0:T(8,128)(2,1)S(1)}, u32[]{:S(2)}, u32[]{:S(2)}) collective-permute-start(bf16[8,48,768]{2,1,0:T(8,128)(2,1)S(1)} %shard_map.287.refs_6_.first_ref), channel_id=1, source_target_pairs={{0,4},{1,5},{2,6},{3,7},{4,0},{5,1},{6,2},{7,3},{8,12},{9,13},{10,... | collective-permute-start | bytes 1769480 | tf_op jit(solution)/shard_map/ppermute | solution.py:1085
  39.2 13.7 %collective-permute-start.11 = (bf16[8,48,768]{2,1,0:T(8,128)(2,1)S(1)}, bf16[8,48,768]{2,1,0:T(8,128)(2,1)S(1)}, u32[]{:S(2)}, u32[]{:S(2)}) collective-permute-start(bf16[8,48,768]{2,1,0:T(8,128)(2,1)S(1)} %shard_map.284.refs_5_.first_ref), channel_id=1, source_target_pairs={{0,2},{1,3},{2,0},{3,1},{4,6},{5,7},{6,4},{7,5},{8,10},{9,11},{10,... | collective-permute-start | bytes 1769480 | tf_op jit(solution)/shard_map/ppermute | solution.py:1085
  52.6 8.4 %copy-start.1 = (bf16[16,48,768]{2,1,0:T(8,128)(2,1)}, bf16[16,48,768]{2,1,0:T(8,128)(2,1)S(1)}, u32[]{:S(2)}) copy-start(bf16[16,48,768]{2,1,0:T(8,128)(2,1)S(1)} %shard_map.290.refs_6_) | copy-start | bytes 3538948
  52.6 8.4 %collective-permute-start.14 = (bf16[16,48,768]{2,1,0:T(8,128)(2,1)S(1)}, bf16[16,48,768]{2,1,0:T(8,128)(2,1)S(1)}, u32[]{:S(2)}, u32[]{:S(2)}) collective-permute-start(bf16[16,48,768]{2,1,0:T(8,128)(2,1)S(1)} %shard_map.290.refs_6_), channel_id=1, source_target_pairs={{0,1},{1,0},{2,3},{3,2},{4,5},{5,4},{6,7},{7,6},{8,9},{9,8},{10,11... | collective-permute-start | bytes 3538952 | tf_op jit(solution)/shard_map/ppermute | solution.py:1085
  52.9 8.1 %copy-start = (bf16[16,48,768]{2,1,0:T(8,128)(2,1)}, bf16[16,48,768]{2,1,0:T(8,128)(2,1)S(1)}, u32[]{:S(2)}) copy-start(bf16[16,48,768]{2,1,0:T(8,128)(2,1)S(1)} %shard_map.289.refs_5_) | copy-start | bytes 3538948
  52.9 8.1 %collective-permute-start.13 = (bf16[16,48,768]{2,1,0:T(8,128)(2,1)S(1)}, bf16[16,48,768]{2,1,0:T(8,128)(2,1)S(1)}, u32[]{:S(2)}, u32[]{:S(2)}) collective-permute-start(bf16[16,48,768]{2,1,0:T(8,128)(2,1)S(1)} %shard_map.289.refs_5_), channel_id=1, source_target_pairs={{0,1},{1,0},{2,3},{3,2},{4,5},{5,4},{6,7},{7,6},{8,9},{9,8},{10,11... | collective-permute-start | bytes 3538952 | tf_op jit(solution)/shard_map/ppermute | solution.py:1085
  94.0 12.8 %collective-permute-start.15 = (bf16[16,48,768]{2,1,0:T(8,128)(2,1)}, bf16[16,48,768]{2,1,0:T(8,128)(2,1)S(1)}, u32[]{:S(2)}, u32[]{:S(2)}) collective-permute-start(bf16[16,48,768]{2,1,0:T(8,128)(2,1)} %bitcast.52), channel_id=1, source_target_pairs={{0,1},{1,0},{2,3},{3,2},{4,5},{5,4},{6,7},{7,6},{8,9},{9,8},{10,11... | collective-permute-start | bytes 3538952 | tf_op jit(solution)/shard_map/ppermute | solution.py:1085
  94.4 12.5 %copy-start.2 = (bf16[768,768]{1,0:T(8,128)(2,1)S(1)}, bf16[768,768]{1,0:T(8,128)(2,1)}, u32[]{:S(2)}) copy-start(bf16[768,768]{1,0:T(8,128)(2,1)} %get-tuple-element.94) | copy-start | bytes 3538948
  106.5 13.5 %collective-permute-start.16 = (bf16[16,48,768]{2,1,0:T(8,128)(2,1)S(1)}, bf16[16,48,768]{2,1,0:T(8,128)(2,1)S(1)}, u32[]{:S(2)}, u32[]{:S(2)}) collective-permute-start(bf16[16,48,768]{2,1,0:T(8,128)(2,1)S(1)} %bitcast.45), channel_id=1, source_target_pairs={{0,1},{1,0},{2,3},{3,2},{4,5},{5,4},{6,7},{7,6},{8,9},{9,8},{10,11... | collective-permute-start | bytes 3538952 | tf_op jit(solution)/shard_map/ppermute | solution.py:1085
  107.1 15.6 %collective-permute-start.17 = (bf16[8,48,768]{2,1,0:T(8,128)(2,1)S(1)}, bf16[8,48,768]{2,1,0:T(8,128)(2,1)S(1)}, u32[]{:S(2)}, u32[]{:S(2)}) collective-permute-start(bf16[8,48,768]{2,1,0:T(8,128)(2,1)S(1)} %get-tuple-element.97.rest_0_), channel_id=1, source_target_pairs={{0,2},{1,3},{2,0},{3,1},{4,6},{5,7},{6,4},{7,5},{8,10},{9,11},{10,... | collective-permute-start | bytes 1769480 | tf_op jit(solution)/shard_map/ppermute | solution.py:1085
  120.3 15.3 %collective-permute-start.18 = (bf16[8,48,768]{2,1,0:T(8,128)(2,1)S(1)}, bf16[8,48,768]{2,1,0:T(8,128)(2,1)S(1)}, u32[]{:S(2)}, u32[]{:S(2)}) collective-permute-start(bf16[8,48,768]{2,1,0:T(8,128)(2,1)S(1)} %get-tuple-element.105.rest_0_), channel_id=1, source_target_pairs={{0,2},{1,3},{2,0},{3,1},{4,6},{5,7},{6,4},{7,5},{8,10},{9,11},{10,... | collective-permute-start | bytes 1769480 | tf_op jit(solution)/shard_map/ppermute | solution.py:1085
  122.8 30.8 %collective-permute-start.20 = (bf16[4,48,768]{2,1,0:T(8,128)(2,1)S(1)}, bf16[4,48,768]{2,1,0:T(8,128)(2,1)S(1)}, u32[]{:S(2)}, u32[]{:S(2)}) collective-permute-start(bf16[4,48,768]{2,1,0:T(8,128)(2,1)S(1)} %get-tuple-element.107.rest_1_), channel_id=1, source_target_pairs={{0,4},{1,5},{2,6},{3,7},{4,0},{5,1},{6,2},{7,3},{8,12},{9,13},{10,... | collective-permute-start | bytes 884744 | tf_op jit(solution)/shard_map/ppermute | solution.py:1085
  135.7 17.8 %collective-permute-start.19 = (bf16[4,48,768]{2,1,0:T(8,128)(2,1)S(1)}, bf16[4,48,768]{2,1,0:T(8,128)(2,1)S(1)}, u32[]{:S(2)}, u32[]{:S(2)}) collective-permute-start(bf16[4,48,768]{2,1,0:T(8,128)(2,1)S(1)} %get-tuple-element.112.rest_0_), channel_id=1, source_target_pairs={{0,4},{1,5},{2,6},{3,7},{4,0},{5,1},{6,2},{7,3},{8,12},{9,13},{10,... | collective-permute-start | bytes 884744 | tf_op jit(solution)/shard_map/ppermute | solution.py:1085
  153.7 17.7 %collective-permute-start.21 = (bf16[2,48,768]{2,1,0:T(8,128)(2,1)S(1)}, bf16[2,48,768]{2,1,0:T(8,128)(2,1)S(1)}, u32[]{:S(2)}, u32[]{:S(2)}) collective-permute-start(bf16[2,48,768]{2,1,0:T(8,128)(2,1)S(1)} %get-tuple-element.117.rest_0_), channel_id=1, source_target_pairs={{0,16},{1,17},{2,18},{3,19},{4,20},{5,21},{6,22},{7,23},{8,24},{9,... | collective-permute-start | bytes 442376 | tf_op jit(solution)/shard_map/ppermute | solution.py:1085
  155.8 15.6 %collective-permute-start.22 = (bf16[2,48,768]{2,1,0:T(8,128)(2,1)S(1)}, bf16[2,48,768]{2,1,0:T(8,128)(2,1)S(1)}, u32[]{:S(2)}, u32[]{:S(2)}) collective-permute-start(bf16[2,48,768]{2,1,0:T(8,128)(2,1)S(1)} %get-tuple-element.118.rest_1_), channel_id=1, source_target_pairs={{0,8},{1,9},{2,10},{3,11},{4,12},{5,13},{6,14},{7,15},{8,0},{9,1},... | collective-permute-start | bytes 442376 | tf_op jit(solution)/shard_map/ppermute | solution.py:1085
  157.5 13.9 %copy-start.14 = (f32[4,16,384]{2,1,0:T(8,128)S(1)}, f32[4,16,384]{2,1,0:T(8,128)}, u32[]{:S(2)}) copy-start(f32[4,16,384]{2,1,0:T(8,128)} %get-tuple-element.120.sums2_ref) | copy-start | bytes 294916
  157.5 13.9 %copy-start.15 = (f32[16,768]{1,0:T(8,128)S(1)}, f32[16,768]{1,0:T(8,128)}, u32[]{:S(2)}) copy-start(f32[16,768]{1,0:T(8,128)} %get-tuple-element.121.db_ref) | copy-start | bytes 147460
  157.5 13.9 %collective-permute-start.23 = (bf16[2,48,768]{2,1,0:T(8,128)(2,1)S(1)}, bf16[2,48,768]{2,1,0:T(8,128)(2,1)S(1)}, u32[]{:S(2)}, u32[]{:S(2)}) collective-permute-start(bf16[2,48,768]{2,1,0:T(8,128)(2,1)S(1)} %get-tuple-element.119.rest_2_), channel_id=1, source_target_pairs={{0,24},{1,25},{2,26},{3,27},{4,28},{5,29},{6,30},{7,31},{8,16},{9,... | collective-permute-start | bytes 442376 | tf_op jit(solution)/shard_map/ppermute | solution.py:1085
  171.8 17.6 %copy-start.3 = (f32[48,768]{1,0:T(8,128)S(1)}, f32[48,768]{1,0:T(8,128)}, u32[]{:S(2)}) copy-start(f32[48,768]{1,0:T(8,128)} %refs_6_.1) | copy-start | bytes 442372
  171.8 17.7 %copy-start.4 = (f32[48,768]{1,0:T(8,128)S(1)}, f32[48,768]{1,0:T(8,128)}, u32[]{:S(2)}) copy-start(f32[48,768]{1,0:T(8,128)} %refs_7_.1) | copy-start | bytes 442372
  171.8 17.6 %copy-start.5 = (f32[48,768]{1,0:T(8,128)S(1)}, f32[48,768]{1,0:T(8,128)}, u32[]{:S(2)}) copy-start(f32[48,768]{1,0:T(8,128)} %refs_8_.1) | copy-start | bytes 442372
  171.8 17.6 %copy-start.6 = (f32[48,384]{1,0:T(8,128)S(1)}, f32[48,384]{1,0:T(8,128)}, u32[]{:S(2)}) copy-start(f32[48,384]{1,0:T(8,128)} %refs_0_.1) | copy-start | bytes 221188
  171.9 17.6 %copy-start.7 = (f32[48,384]{1,0:T(8,128)S(1)}, f32[48,384]{1,0:T(8,128)}, u32[]{:S(2)}) copy-start(f32[48,384]{1,0:T(8,128)} %refs_3_.3) | copy-start | bytes 221188
  171.9 17.6 %copy-start.8 = (f32[48,384]{1,0:T(8,128)S(1)}, f32[48,384]{1,0:T(8,128)}, u32[]{:S(2)}) copy-start(f32[48,384]{1,0:T(8,128)} %refs_1_.1) | copy-start | bytes 221188
  171.9 17.6 %copy-start.9 = (f32[48,384]{1,0:T(8,128)S(1)}, f32[48,384]{1,0:T(8,128)}, u32[]{:S(2)}) copy-start(f32[48,384]{1,0:T(8,128)} %refs_2_.3) | copy-start | bytes 221188
  171.9 17.6 %copy-start.10 = (f32[48,384]{1,0:T(8,128)S(1)}, f32[48,384]{1,0:T(8,128)}, u32[]{:S(2)}) copy-start(f32[48,384]{1,0:T(8,128)} %refs_4_.1) | copy-start | bytes 221188
  171.9 17.6 %copy-start.11 = (f32[48,384]{1,0:T(8,128)S(1)}, f32[48,384]{1,0:T(8,128)}, u32[]{:S(2)}) copy-start(f32[48,384]{1,0:T(8,128)} %refs_5_.1) | copy-start | bytes 221188
  171.9 4.2 %collective-permute-start.24 = (bf16[64,384]{1,0:T(8,128)(2,1)S(1)}, bf16[64,384]{1,0:T(8,128)(2,1)S(1)}, u32[]{:S(2)}, u32[]{:S(2)}) collective-permute-start(bf16[64,384]{1,0:T(8,128)(2,1)S(1)} %get-tuple-element.123.refs_0_), channel_id=1, source_target_pairs={{0,2},{1,3},{2,0},{3,1},{4,6},{5,7},{6,4},{7,5},{8,10},{9,11},{10,... | collective-permute-start | bytes 147464 | tf_op jit(solution)/shard_map/ppermute | solution.py:1085
  173.0 4.1 %collective-permute-start.25 = (bf16[64,384]{1,0:T(8,128)(2,1)S(1)}, bf16[64,384]{1,0:T(8,128)(2,1)S(1)}, u32[]{:S(2)}, u32[]{:S(2)}) collective-permute-start(bf16[64,384]{1,0:T(8,128)(2,1)S(1)} %get-tuple-element.123.refs_0_), channel_id=1, source_target_pairs={{0,4},{1,5},{2,6},{3,7},{4,0},{5,1},{6,2},{7,3},{8,12},{9,13},{10,... | collective-permute-start | bytes 147464 | tf_op jit(solution)/shard_map/ppermute | solution.py:1085
  173.6 5.0 %collective-permute-start.26 = (bf16[64,384]{1,0:T(8,128)(2,1)S(1)}, bf16[64,384]{1,0:T(8,128)(2,1)S(1)}, u32[]{:S(2)}, u32[]{:S(2)}) collective-permute-start(bf16[64,384]{1,0:T(8,128)(2,1)S(1)} %get-tuple-element.123.refs_0_), channel_id=1, source_target_pairs={{0,6},{1,7},{2,4},{3,5},{4,2},{5,3},{6,0},{7,1},{8,14},{9,15},{10,... | collective-permute-start | bytes 147464 | tf_op jit(solution)/shard_map/ppermute | solution.py:1085
  178.7 4.7 %collective-permute-start.27 = (bf16[64,384]{1,0:T(8,128)(2,1)S(1)}, bf16[64,384]{1,0:T(8,128)(2,1)S(1)}, u32[]{:S(2)}, u32[]{:S(2)}) collective-permute-start(bf16[64,384]{1,0:T(8,128)(2,1)S(1)} %shard_map.304.refs_0_), channel_id=1, source_target_pairs={{0,8},{1,9},{2,10},{3,11},{4,12},{5,13},{6,14},{7,15},{8,0},{9,1},... | collective-permute-start | bytes 147464 | tf_op jit(solution)/shard_map/ppermute | solution.py:1085
  179.9 5.5 %collective-permute-start.28 = (bf16[64,384]{1,0:T(8,128)(2,1)S(1)}, bf16[64,384]{1,0:T(8,128)(2,1)S(1)}, u32[]{:S(2)}, u32[]{:S(2)}) collective-permute-start(bf16[64,384]{1,0:T(8,128)(2,1)S(1)} %shard_map.304.refs_0_), channel_id=1, source_target_pairs={{0,16},{1,17},{2,18},{3,19},{4,20},{5,21},{6,22},{7,23},{8,24},{9,... | collective-permute-start | bytes 147464 | tf_op jit(solution)/shard_map/ppermute | solution.py:1085
  182.2 5.9 %collective-permute-start.29 = (bf16[64,384]{1,0:T(8,128)(2,1)S(1)}, bf16[64,384]{1,0:T(8,128)(2,1)S(1)}, u32[]{:S(2)}, u32[]{:S(2)}) collective-permute-start(bf16[64,384]{1,0:T(8,128)(2,1)S(1)} %shard_map.304.refs_0_), channel_id=1, source_target_pairs={{0,24},{1,25},{2,26},{3,27},{4,28},{5,29},{6,30},{7,31},{8,16},{9,... | collective-permute-start | bytes 147464 | tf_op jit(solution)/shard_map/ppermute | solution.py:1085
  188.1 1.3 collective-permute-start.30
  (4 other events, 6.5 us)

commit v3 on v2

--- a/solution.py
+++ b/solution.py
@@ -1127,7 +1127,7 @@
     flat = lambda a: a.reshape(pixels, a.shape[-1])
     square = lambda a: a.reshape(side, side, imgs, a.shape[-1])
 
-    cut = [0, 3, 10, side]
+    cut = [0, 3, 12, side]
     gates = None
     if by_hops:
         gates = {1: pair}

time: 193 us -> 190 us (0.984)
  transfers between devices with their start and end apart: 31 -> 31, of which waited for: 17 -> 14; matrix products, arithmetic and copies ran while one was open for 1% -> 1% of each run, Pallas kernels for 49% -> 49%
where the time goes in v3:
time: 190 us
  Pallas kernels  127 us (67%)
  starting transfers between devices  37.5 us (20%)
  waiting for transfers between devices  19 us (10%)
  local copies, waits for them, and re-layouts  2.44 us (1%)
  between operations  1.98 us (1%)
    pallas_call x27, Pallas kernels, kernel_call(): pl.pallas_call(body, out_shape=tuple(out), in_specs=specs, out_specs=tupl...  126 us
    ppermute x31, starting transfers between devices, swap(): return lax.ppermute(x, 'dp', [(i, i ^ bit) for i in range(n)])  37.5 us
    ppermute x31, waiting for transfers between devices, swap(): return lax.ppermute(x, 'dp', [(i, i ^ bit) for i in range(n)])  19 us
  transfers between devices with their start and end apart: 31, of which 14 were waited for; matrix products, arithmetic and copies ran while one was open for 1% of the time, Pallas kernels for 49%

profile of v3, /device:TPU:0, one launch (start us, length us, event | category | flops | bytes accessed | tf_op | source)
XLA Modules:
  0.0 190.0 jit_solution(17773204674680924102)
XLA Ops:
  0.7 0.8 convert_element_type.8
  1.4 2.9 %collective-permute-start = (bf16[744]{0:T(1024)(128)(2,1)S(1)}, bf16[744]{0:T(1024)(128)(2,1)S(1)}, u32[]{:S(2)}, u32[]{:S(2)}) collective-permute-start(bf16[744]{0:T(1024)(128)(2,1)S(1)} %convert_element_type.8), channel_id=1, source_target_pairs={{0,2},{1,3},{2,0},{3,1},{4,6},{5,7},{6,4},{7,5},{8,10},{9,11},{10,... | collective-permute-start | bytes 4472 | tf_op jit(solution)/shard_map/ppermute | solution.py:1085
  4.3 1.0 shard_map.280
  6.0 2.1 %collective-permute-start.1 = (bf16[2,744]{1,0:T(2,128)(2,1)S(1)}, bf16[2,744]{1,0:T(2,128)(2,1)S(1)}, u32[]{:S(2)}, u32[]{:S(2)}) collective-permute-start(bf16[2,744]{1,0:T(2,128)(2,1)S(1)} %pad_maximum_fusion.3), channel_id=1, source_target_pairs={{0,4},{1,5},{2,6},{3,7},{4,0},{5,1},{6,2},{7,3},{8,12},{9,13},{10,... | collective-permute-start | bytes 8936 | tf_op jit(solution)/shard_map/ppermute | solution.py:1085
  8.1 1.6 collective-permute-done.1
  9.7 2.1 %collective-permute-start.2 = (bf16[2,2,744]{2,1,0:T(2,128)(2,1)S(1)}, bf16[2,2,744]{2,1,0:T(2,128)(2,1)S(1)}, u32[]{:S(2)}, u32[]{:S(2)}) collective-permute-start(bf16[2,2,744]{2,1,0:T(2,128)(2,1)S(1)} %pad_maximum_fusion.2), channel_id=1, source_target_pairs={{0,8},{1,9},{2,10},{3,11},{4,12},{5,13},{6,14},{7,15},{8,0},{9,1},... | collective-permute-start | bytes 17864 | tf_op jit(solution)/shard_map/ppermute | solution.py:1085
  11.8 2.6 %collective-permute-start.3 = (bf16[1,48,768]{2,1,0:T(8,128)(2,1)S(1)}, bf16[1,48,768]{2,1,0:T(8,128)(2,1)S(1)}, u32[]{:S(2)}, u32[]{:S(2)}) collective-permute-start(bf16[1,48,768]{2,1,0:T(8,128)(2,1)S(1)} %get-tuple-element.75.first_ref), channel_id=1, source_target_pairs={{0,16},{1,17},{2,18},{3,19},{4,20},{5,21},{6,22},{7,23},{8,24},{9,... | collective-permute-start | bytes 221192 | tf_op jit(solution)/shard_map/ppermute | solution.py:1085
  14.8 3.4 %collective-permute-done.3.second_ref = bf16[1,48,768]{2,1,0:T(8,128)(2,1)S(1)} collective-permute-done((bf16[1,48,768]{2,1,0:T(8,128)(2,1)S(1)}, bf16[1,48,768]{2,1,0:T(8,128)(2,1)S(1)}, u32[]{:S(2)}, u32[]{:S(2)}) %collective-permute-start.3) | collective-permute-done | bytes 73760 | tf_op jit(solution)/shard_map/ppermute | solution.py:1085
  18.3 2.3 %collective-permute-start.4 = (bf16[2,2,2,744]{3,2,1,0:T(2,128)(2,1)S(1)}, bf16[2,2,2,744]{3,2,1,0:T(2,128)(2,1)S(1)}, u32[]{:S(2)}, u32[]{:S(2)}) collective-permute-start(bf16[2,2,2,744]{3,2,1,0:T(2,128)(2,1)S(1)} %pad_maximum_fusion.1), channel_id=1, source_target_pairs={{0,16},{1,17},{2,18},{3,19},{4,20},{5,21},{6,22},{7,23},{8,24},{9,... | collective-permute-start | bytes 35720 | tf_op jit(solution)/shard_map/ppermute | solution.py:1085
  20.6 2.0 %collective-permute-start.9 = (bf16[2,48,768]{2,1,0:T(8,128)(2,1)S(1)}, bf16[2,48,768]{2,1,0:T(8,128)(2,1)S(1)}, u32[]{:S(2)}, u32[]{:S(2)}) collective-permute-start(bf16[2,48,768]{2,1,0:T(8,128)(2,1)S(1)} %shard_map.285.first_ref), channel_id=1, source_target_pairs={{0,8},{1,9},{2,10},{3,11},{4,12},{5,13},{6,14},{7,15},{8,0},{9,1},... | collective-permute-start | bytes 442376 | tf_op jit(solution)/shard_map/ppermute | solution.py:1085
  23.7 1.4 collective-permute-start.7
  25.2 0.6 collective-permute-done.9.second_ref
  25.8 1.5 collective-permute-start.10
  27.5 0.8 reshape.99.refs_0_.small_hbm
  28.4 9.1 %shard_map.283 = (f32[14,14,16,384]{3,2,1,0:T(8,128)}, bf16[14,14,16,384]{3,2,1,0:T(8,128)(2,1)}, f32[14,14,16,1]{3,2,1,0:T(8,128)}, bf16[14,14,16,384]{3,2,1,0:T(8,128)(2,1)}, f32[8,128]{1,0:T(8,128)S(1)}) custom-call(f32[62,384]{1,0:T(8,128)} %reshape.99.refs_0_.small_hbm, bf16[14,14,16,384]{3,2,1,0:T(8,128)(2,1)} %bitcast.52, s32[16]{0:T(128)S(1)} %copy-done.12, ...), custom_call_target="tpu_custom_call" | custom-call | flops 7500000256 | tf_op jit(solution)/shard_map/pallas_call | solution.py:71
  37.6 1.6 collective-permute-start.12
  39.2 0.6 collective-permute-start.11
  39.8 13.0 %shard_map.288 = (bf16[14,14,16,384]{3,2,1,0:T(8,128)(2,1)}, f32[14,14,16,1]{3,2,1,0:T(8,128)}, bf16[14,14,16,384]{3,2,1,0:T(8,128)(2,1)}, f32[8,128]{1,0:T(8,128)S(1)}) custom-call(f32[62,384]{1,0:T(8,128)} %reshape.99.refs_0_.small_hbm, ...), custom_call_target="tpu_custom_call", output_to_operand_aliasing={{0}: (2, {}), {1}: (3, {}), {2}: (4, {})} | custom-call | flops 13500000256 | tf_op jit(solution)/shard_map/pallas_call | solution.py:71
  53.7 5.5 %shard_map.291 = (bf16[14,14,16,384]{3,2,1,0:T(8,128)(2,1)}, f32[14,14,16,1]{3,2,1,0:T(8,128)}, bf16[14,14,16,384]{3,2,1,0:T(8,128)(2,1)}, f32[8,128]{1,0:T(8,128)}) custom-call(f32[62,384]{1,0:T(8,128)} %reshape.99.refs_0_.small_hbm, ...), custom_call_target="tpu_custom_call", output_to_operand_aliasing={{0}: (2, {}), {1}: (3, {}), {2}: (4, {})} | custom-call | flops 3000000000 | tf_op jit(solution)/shard_map/pallas_call | solution.py:71
  59.2 1.1 copy-done.20
  60.6 31.5 %shard_map.292 = (bf16[3136,1536]{1,0:T(8,128)(2,1)}, bf16[3136,1536]{1,0:T(8,128)(2,1)}, bf16[768,768]{1,0:T(8,128)(2,1)}, bf16[768,768]{1,0:T(8,128)(2,1)}, f3...) custom-call(s32[1]{0:T(128)} %bitcast.me_ref, ...), custom_call_target="tpu_custom_call" | custom-call | flops 33999998976 | tf_op jit(solution)/shard_map/pallas_call | solution.py:71
  92.6 12.1 %shard_map.293 = (bf16[768,768]{1,0:T(8,128)(2,1)S(1)}, f32[16,768]{1,0:T(8,128)S(1)}, bf16[3136,768]{1,0:T(8,128)(2,1)}) custom-call(s32[1]{0:T(128)} %bitcast.me_ref, bf16[3136,384]{1,0:T(8,128)(2,1)} %bitcast.63, bf16[3136,1536]{1,0:T(8,128)(2,1)} %get-tuple-element.92.act_hbm, bf16[3136,1536]{1,0:T(8,128)(2,1)} %get-tuple-element.93.dg_hbm, ...), custom_call_target="tpu_custom_call" | custom-call | flops 12999999488 | tf_op jit(solution)/shard_map/pallas_call | solution.py:71
  105.2 1.6 collective-permute-start.17
  106.8 11.8 %shard_map.295 = (bf16[768,768]{1,0:T(8,128)(2,1)S(1)}, f32[16,768]{1,0:T(8,128)S(1)}, bf16[3136,768]{1,0:T(8,128)(2,1)}) custom-call(s32[1]{0:T(128)} %bitcast.me_ref, bf16[3136,384]{1,0:T(8,128)(2,1)} %bitcast.64, bf16[3136,1536]{1,0:T(8,128)(2,1)} %get-tuple-element.92.act_hbm, bf16[3136,1536]{1,0:T(8,128)(2,1)} %get-tuple-element.93.dg_hbm, ...), custom_call_target="tpu_custom_call" | custom-call | flops 12999999488 | tf_op jit(solution)/shard_map/pallas_call | solution.py:71
  119.5 1.3 collective-permute-done.17.refs_1_
  120.9 1.1 collective-permute-start.20
  122.0 11.0 %shard_map.298 = (bf16[3136,384]{1,0:T(8,128)(2,1)}, f32[3,16,384]{2,1,0:T(8,128)S(1)}) custom-call(s32[1]{0:T(128)} %bitcast.me_ref, bf16[3136,768]{1,0:T(8,128)(2,1)} %get-tuple-element.98.pnear_hbm, bf16[3136,768]{1,0:T(8,128)(2,1)} %get-tuple-element.99.pfar_hbm, bf16[3136,384]{1,0:T(8,128)(2,1)} %bitcast.47, f32[3136,1]{1,0:T(8,128)} %bitcast.51, ...), custom_call_target="tpu_custom_call" | custom-call | flops 11000000512 | tf_op jit(solution)/shard_map/pallas_call | solution.py:71
  133.0 1.2 collective-permute-done.18.refs_1_
  134.3 0.6 collective-permute-start.19
  134.9 16.4 %shard_map.300 = (f32[14,14,16,384]{3,2,1,0:T(8,128)}, f32[8,128]{1,0:T(8,128)S(1)}) custom-call(bf16[14,14,16,384]{3,2,1,0:T(8,128)(2,1)} %bitcast.61, f32[62,384]{1,0:T(8,128)} %reshape.99.refs_0_.small_hbm, s32[16]{0:T(128)S(1)} %copy-done.12, f32[16]{0:T(128)S(1)} %copy-done.13, bf16[14,14,16,384]{3,2,1,0:T(8,128)(2,1)} %bitcast.60, ...), custom_call_target="tpu_custom_call" | custom-call | flops 22000001024 | tf_op jit(solution)/shard_map/pallas_call | solution.py:71
  151.4 2.1 %collective-permute-start.21 = (bf16[2,48,768]{2,1,0:T(8,128)(2,1)S(1)}, bf16[2,48,768]{2,1,0:T(8,128)(2,1)S(1)}, u32[]{:S(2)}, u32[]{:S(2)}) collective-permute-start(bf16[2,48,768]{2,1,0:T(8,128)(2,1)S(1)} %get-tuple-element.117.rest_0_), channel_id=1, source_target_pairs={{0,16},{1,17},{2,18},{3,19},{4,20},{5,21},{6,22},{7,23},{8,24},{9,... | collective-permute-start | bytes 442376 | tf_op jit(solution)/shard_map/ppermute | solution.py:1085
  153.6 1.7 collective-permute-start.22
  155.2 0.9 collective-permute-start.23
  156.2 13.0 %shard_map.302.gk_ref = f32[49,8,384]{2,1,0:T(8,128)S(1)} custom-call(bf16[14,14,16,384]{3,2,1,0:T(8,128)(2,1)} %bitcast.62, f32[14,14,16,384]{3,2,1,0:T(8,128)} %get-tuple-element.79.refs_1_.mixed_hbm, bf16[2,48,768]{2,1,0:T(8,128)(2,1)S(1)} %get-tuple-element.117.rest_0_, bf16[2,48,768]{2,1,0:T(8,128)(2,1)S(1)} %get-tuple-element.118.rest_1_, ...), custom_call_target="tpu_custom_call" | custom-call | flops 14099999744 | tf_op jit(solution)/shard_map/pallas_call | solution.py:71
  169.7 1.0 collective-permute-start.24
  170.7 1.0 collective-permute-start.25
  171.8 1.5 collective-permute-start.26
  173.3 0.6 collective-permute-done.24.refs_1_
  173.9 1.0 collective-permute-done.25.refs_2_
  174.8 1.9 %collective-permute-done.26.refs_3_ = bf16[64,384]{1,0:T(8,128)(2,1)S(1)} collective-permute-done((bf16[64,384]{1,0:T(8,128)(2,1)S(1)}, bf16[64,384]{1,0:T(8,128)(2,1)S(1)}, u32[]{:S(2)}, u32[]{:S(2)}) %collective-permute-start.26) | collective-permute-done | bytes 49184 | tf_op jit(solution)/shard_map/ppermute | solution.py:1085
  176.8 1.1 collective-permute-start.27
  177.9 2.1 %collective-permute-start.28 = (bf16[64,384]{1,0:T(8,128)(2,1)S(1)}, bf16[64,384]{1,0:T(8,128)(2,1)S(1)}, u32[]{:S(2)}, u32[]{:S(2)}) collective-permute-start(bf16[64,384]{1,0:T(8,128)(2,1)S(1)} %shard_map.304.refs_0_), channel_id=1, source_target_pairs={{0,16},{1,17},{2,18},{3,19},{4,20},{5,21},{6,22},{7,23},{8,24},{9,... | collective-permute-start | bytes 147464 | tf_op jit(solution)/shard_map/ppermute | solution.py:1085
  180.0 1.3 collective-permute-start.29
  181.2 2.2 %collective-permute-done.28.refs_2_ = bf16[64,384]{1,0:T(8,128)(2,1)S(1)} collective-permute-done((bf16[64,384]{1,0:T(8,128)(2,1)S(1)}, bf16[64,384]{1,0:T(8,128)(2,1)S(1)}, u32[]{:S(2)}, u32[]{:S(2)}) %collective-permute-start.28) | collective-permute-done | bytes 49184 | tf_op jit(solution)/shard_map/ppermute | solution.py:1085
  183.4 2.5 %collective-permute-done.29.refs_3_ = bf16[64,384]{1,0:T(8,128)(2,1)S(1)} collective-permute-done((bf16[64,384]{1,0:T(8,128)(2,1)S(1)}, bf16[64,384]{1,0:T(8,128)(2,1)S(1)}, u32[]{:S(2)}, u32[]{:S(2)}) %collective-permute-start.29) | collective-permute-done | bytes 49184 | tf_op jit(solution)/shard_map/ppermute | solution.py:1085
  186.0 1.2 collective-permute-done.30.refs_1_
  187.4 1.3 shard_map.307
  189.3 0.7 multiply_subtract_fusion
  (101 shorter events, 6.4 us)
Async XLA Ops:
  0.6 5.3 %copy-start.16 = (f32[744]{0:T(1024)S(1)}, f32[744]{0:T(1024)}, u32[]{:S(2)}) copy-start(f32[744]{0:T(1024)} %param.25) | copy-start | bytes 8932
  1.4 4.5 %collective-permute-start = (bf16[744]{0:T(1024)(128)(2,1)S(1)}, bf16[744]{0:T(1024)(128)(2,1)S(1)}, u32[]{:S(2)}, u32[]{:S(2)}) collective-permute-start(bf16[744]{0:T(1024)(128)(2,1)S(1)} %convert_element_type.8), channel_id=1, source_target_pairs={{0,2},{1,3},{2,0},{3,1},{4,6},{5,7},{6,4},{7,5},{8,10},{9,11},{10,... | collective-permute-start | bytes 4472 | tf_op jit(solution)/shard_map/ppermute | solution.py:1085
  6.0 3.7 %collective-permute-start.1 = (bf16[2,744]{1,0:T(2,128)(2,1)S(1)}, bf16[2,744]{1,0:T(2,128)(2,1)S(1)}, u32[]{:S(2)}, u32[]{:S(2)}) collective-permute-start(bf16[2,744]{1,0:T(2,128)(2,1)S(1)} %pad_maximum_fusion.3), channel_id=1, source_target_pairs={{0,4},{1,5},{2,6},{3,7},{4,0},{5,1},{6,2},{7,3},{8,12},{9,13},{10,... | collective-permute-start | bytes 8936 | tf_op jit(solution)/shard_map/ppermute | solution.py:1085
  9.7 5.1 %collective-permute-start.2 = (bf16[2,2,744]{2,1,0:T(2,128)(2,1)S(1)}, bf16[2,2,744]{2,1,0:T(2,128)(2,1)S(1)}, u32[]{:S(2)}, u32[]{:S(2)}) collective-permute-start(bf16[2,2,744]{2,1,0:T(2,128)(2,1)S(1)} %pad_maximum_fusion.2), channel_id=1, source_target_pairs={{0,8},{1,9},{2,10},{3,11},{4,12},{5,13},{6,14},{7,15},{8,0},{9,1},... | collective-permute-start | bytes 17864 | tf_op jit(solution)/shard_map/ppermute | solution.py:1085
  11.8 6.3 %collective-permute-start.3 = (bf16[1,48,768]{2,1,0:T(8,128)(2,1)S(1)}, bf16[1,48,768]{2,1,0:T(8,128)(2,1)S(1)}, u32[]{:S(2)}, u32[]{:S(2)}) collective-permute-start(bf16[1,48,768]{2,1,0:T(8,128)(2,1)S(1)} %get-tuple-element.75.first_ref), channel_id=1, source_target_pairs={{0,16},{1,17},{2,18},{3,19},{4,20},{5,21},{6,22},{7,23},{8,24},{9,... | collective-permute-start | bytes 221192 | tf_op jit(solution)/shard_map/ppermute | solution.py:1085
  14.4 6.1 %collective-permute-start.8 = (bf16[1,48,768]{2,1,0:T(8,128)(2,1)S(1)}, bf16[1,48,768]{2,1,0:T(8,128)(2,1)S(1)}, u32[]{:S(2)}, u32[]{:S(2)}) collective-permute-start(bf16[1,48,768]{2,1,0:T(8,128)(2,1)S(1)} %get-tuple-element.84.first_ref), channel_id=1, source_target_pairs={{0,16},{1,17},{2,18},{3,19},{4,20},{5,21},{6,22},{7,23},{8,24},{9,... | collective-permute-start | bytes 221192 | tf_op jit(solution)/shard_map/ppermute | solution.py:1085
  18.2 5.5 %collective-permute-start.5 = (bf16[2,48,768]{2,1,0:T(8,128)(2,1)S(1)}, bf16[2,48,768]{2,1,0:T(8,128)(2,1)S(1)}, u32[]{:S(2)}, u32[]{:S(2)}) collective-permute-start(bf16[2,48,768]{2,1,0:T(8,128)(2,1)S(1)} %shard_map.281.first_ref), channel_id=1, source_target_pairs={{0,8},{1,9},{2,10},{3,11},{4,12},{5,13},{6,14},{7,15},{8,0},{9,1},... | collective-permute-start | bytes 442376 | tf_op jit(solution)/shard_map/ppermute | solution.py:1085
  18.3 4.8 %collective-permute-start.4 = (bf16[2,2,2,744]{3,2,1,0:T(2,128)(2,1)S(1)}, bf16[2,2,2,744]{3,2,1,0:T(2,128)(2,1)S(1)}, u32[]{:S(2)}, u32[]{:S(2)}) collective-permute-start(bf16[2,2,2,744]{3,2,1,0:T(2,128)(2,1)S(1)} %pad_maximum_fusion.1), channel_id=1, source_target_pairs={{0,16},{1,17},{2,18},{3,19},{4,20},{5,21},{6,22},{7,23},{8,24},{9,... | collective-permute-start | bytes 35720 | tf_op jit(solution)/shard_map/ppermute | solution.py:1085
  20.6 5.2 %collective-permute-start.9 = (bf16[2,48,768]{2,1,0:T(8,128)(2,1)S(1)}, bf16[2,48,768]{2,1,0:T(8,128)(2,1)S(1)}, u32[]{:S(2)}, u32[]{:S(2)}) collective-permute-start(bf16[2,48,768]{2,1,0:T(8,128)(2,1)S(1)} %shard_map.285.first_ref), channel_id=1, source_target_pairs={{0,8},{1,9},{2,10},{3,11},{4,12},{5,13},{6,14},{7,15},{8,0},{9,1},... | collective-permute-start | bytes 442376 | tf_op jit(solution)/shard_map/ppermute | solution.py:1085
  23.7 4.6 %copy-start.12 = (s32[16]{0:T(128)S(1)}, s32[16]{0:T(128)}, u32[]{:S(2)}) copy-start(s32[16]{0:T(128)} %partner_ref.1) | copy-start | bytes 196
  23.7 4.6 %copy-start.13 = (f32[16]{0:T(128)S(1)}, f32[16]{0:T(128)}, u32[]{:S(2)}) copy-start(f32[16]{0:T(128)} %weight_ref.1) | copy-start | bytes 196
  23.7 15.4 %collective-permute-start.7 = (bf16[4,48,768]{2,1,0:T(8,128)(2,1)S(1)}, bf16[4,48,768]{2,1,0:T(8,128)(2,1)S(1)}, u32[]{:S(2)}, u32[]{:S(2)}) collective-permute-start(bf16[4,48,768]{2,1,0:T(8,128)(2,1)S(1)} %shard_map.282.first_ref), channel_id=1, source_target_pairs={{0,4},{1,5},{2,6},{3,7},{4,0},{5,1},{6,2},{7,3},{8,12},{9,13},{10,... | collective-permute-start | bytes 884744 | tf_op jit(solution)/shard_map/ppermute | solution.py:1085
  25.2 2.2 %collective-permute-start.6 = (bf16[2,2,2,2,744]{4,3,2,1,0:T(2,128)(2,1)S(1)}, bf16[2,2,2,2,744]{4,3,2,1,0:T(2,128)(2,1)S(1)}, u32[]{:S(2)}, u32[]{:S(2)}) collective-permute-start(bf16[2,2,2,2,744]{4,3,2,1,0:T(2,128)(2,1)S(1)} %pad_maximum_fusion), channel_id=1, source_target_pairs={{0,1},{1,0},{2,3},{3,2},{4,5},{5,4},{6,7},{7,6},{8,9},{9,8},{10,11... | collective-permute-start | bytes 71432 | tf_op jit(solution)/shard_map/ppermute | solution.py:1085
  25.8 11.7 %collective-permute-start.10 = (bf16[4,48,768]{2,1,0:T(8,128)(2,1)S(1)}, bf16[4,48,768]{2,1,0:T(8,128)(2,1)S(1)}, u32[]{:S(2)}, u32[]{:S(2)}) collective-permute-start(bf16[4,48,768]{2,1,0:T(8,128)(2,1)S(1)} %shard_map.286.first_ref), channel_id=1, source_target_pairs={{0,2},{1,3},{2,0},{3,1},{4,6},{5,7},{6,4},{7,5},{8,10},{9,11},{10,... | collective-permute-start | bytes 884744 | tf_op jit(solution)/shard_map/ppermute | solution.py:1085
  37.6 15.3 %collective-permute-start.12 = (bf16[8,48,768]{2,1,0:T(8,128)(2,1)S(1)}, bf16[8,48,768]{2,1,0:T(8,128)(2,1)S(1)}, u32[]{:S(2)}, u32[]{:S(2)}) collective-permute-start(bf16[8,48,768]{2,1,0:T(8,128)(2,1)S(1)} %shard_map.287.refs_6_.first_ref), channel_id=1, source_target_pairs={{0,4},{1,5},{2,6},{3,7},{4,0},{5,1},{6,2},{7,3},{8,12},{9,13},{10,... | collective-permute-start | bytes 1769480 | tf_op jit(solution)/shard_map/ppermute | solution.py:1085
  39.2 13.8 %collective-permute-start.11 = (bf16[8,48,768]{2,1,0:T(8,128)(2,1)S(1)}, bf16[8,48,768]{2,1,0:T(8,128)(2,1)S(1)}, u32[]{:S(2)}, u32[]{:S(2)}) collective-permute-start(bf16[8,48,768]{2,1,0:T(8,128)(2,1)S(1)} %shard_map.284.refs_5_.first_ref), channel_id=1, source_target_pairs={{0,2},{1,3},{2,0},{3,1},{4,6},{5,7},{6,4},{7,5},{8,10},{9,11},{10,... | collective-permute-start | bytes 1769480 | tf_op jit(solution)/shard_map/ppermute | solution.py:1085
  52.9 6.2 %copy-start.1 = (bf16[16,48,768]{2,1,0:T(8,128)(2,1)}, bf16[16,48,768]{2,1,0:T(8,128)(2,1)S(1)}, u32[]{:S(2)}) copy-start(bf16[16,48,768]{2,1,0:T(8,128)(2,1)S(1)} %shard_map.290.refs_6_) | copy-start | bytes 3538948
  53.0 6.2 %collective-permute-start.14 = (bf16[16,48,768]{2,1,0:T(8,128)(2,1)S(1)}, bf16[16,48,768]{2,1,0:T(8,128)(2,1)S(1)}, u32[]{:S(2)}, u32[]{:S(2)}) collective-permute-start(bf16[16,48,768]{2,1,0:T(8,128)(2,1)S(1)} %shard_map.290.refs_6_), channel_id=1, source_target_pairs={{0,1},{1,0},{2,3},{3,2},{4,5},{5,4},{6,7},{7,6},{8,9},{9,8},{10,11... | collective-permute-start | bytes 3538952 | tf_op jit(solution)/shard_map/ppermute | solution.py:1085
  53.1 6.0 %copy-start = (bf16[16,48,768]{2,1,0:T(8,128)(2,1)}, bf16[16,48,768]{2,1,0:T(8,128)(2,1)S(1)}, u32[]{:S(2)}) copy-start(bf16[16,48,768]{2,1,0:T(8,128)(2,1)S(1)} %shard_map.289.refs_5_) | copy-start | bytes 3538948
  53.1 6.1 %collective-permute-start.13 = (bf16[16,48,768]{2,1,0:T(8,128)(2,1)S(1)}, bf16[16,48,768]{2,1,0:T(8,128)(2,1)S(1)}, u32[]{:S(2)}, u32[]{:S(2)}) collective-permute-start(bf16[16,48,768]{2,1,0:T(8,128)(2,1)S(1)} %shard_map.289.refs_5_), channel_id=1, source_target_pairs={{0,1},{1,0},{2,3},{3,2},{4,5},{5,4},{6,7},{7,6},{8,9},{9,8},{10,11... | collective-permute-start | bytes 3538952 | tf_op jit(solution)/shard_map/ppermute | solution.py:1085
  92.2 12.8 %collective-permute-start.15 = (bf16[16,48,768]{2,1,0:T(8,128)(2,1)}, bf16[16,48,768]{2,1,0:T(8,128)(2,1)S(1)}, u32[]{:S(2)}, u32[]{:S(2)}) collective-permute-start(bf16[16,48,768]{2,1,0:T(8,128)(2,1)} %bitcast.58), channel_id=1, source_target_pairs={{0,1},{1,0},{2,3},{3,2},{4,5},{5,4},{6,7},{7,6},{8,9},{9,8},{10,11... | collective-permute-start | bytes 3538952 | tf_op jit(solution)/shard_map/ppermute | solution.py:1085
  92.6 12.4 %copy-start.2 = (bf16[768,768]{1,0:T(8,128)(2,1)S(1)}, bf16[768,768]{1,0:T(8,128)(2,1)}, u32[]{:S(2)}) copy-start(bf16[768,768]{1,0:T(8,128)(2,1)} %get-tuple-element.94) | copy-start | bytes 3538948
  104.7 14.0 %collective-permute-start.16 = (bf16[16,48,768]{2,1,0:T(8,128)(2,1)S(1)}, bf16[16,48,768]{2,1,0:T(8,128)(2,1)S(1)}, u32[]{:S(2)}, u32[]{:S(2)}) collective-permute-start(bf16[16,48,768]{2,1,0:T(8,128)(2,1)S(1)} %bitcast.45), channel_id=1, source_target_pairs={{0,1},{1,0},{2,3},{3,2},{4,5},{5,4},{6,7},{7,6},{8,9},{9,8},{10,11... | collective-permute-start | bytes 3538952 | tf_op jit(solution)/shard_map/ppermute | solution.py:1085
  105.2 15.6 %collective-permute-start.17 = (bf16[8,48,768]{2,1,0:T(8,128)(2,1)S(1)}, bf16[8,48,768]{2,1,0:T(8,128)(2,1)S(1)}, u32[]{:S(2)}, u32[]{:S(2)}) collective-permute-start(bf16[8,48,768]{2,1,0:T(8,128)(2,1)S(1)} %get-tuple-element.97.rest_0_), channel_id=1, source_target_pairs={{0,2},{1,3},{2,0},{3,1},{4,6},{5,7},{6,4},{7,5},{8,10},{9,11},{10,... | collective-permute-start | bytes 1769480 | tf_op jit(solution)/shard_map/ppermute | solution.py:1085
  118.9 15.3 %collective-permute-start.18 = (bf16[8,48,768]{2,1,0:T(8,128)(2,1)S(1)}, bf16[8,48,768]{2,1,0:T(8,128)(2,1)S(1)}, u32[]{:S(2)}, u32[]{:S(2)}) collective-permute-start(bf16[8,48,768]{2,1,0:T(8,128)(2,1)S(1)} %get-tuple-element.105.rest_0_), channel_id=1, source_target_pairs={{0,2},{1,3},{2,0},{3,1},{4,6},{5,7},{6,4},{7,5},{8,10},{9,11},{10,... | collective-permute-start | bytes 1769480 | tf_op jit(solution)/shard_map/ppermute | solution.py:1085
  120.9 30.4 %collective-permute-start.20 = (bf16[4,48,768]{2,1,0:T(8,128)(2,1)S(1)}, bf16[4,48,768]{2,1,0:T(8,128)(2,1)S(1)}, u32[]{:S(2)}, u32[]{:S(2)}) collective-permute-start(bf16[4,48,768]{2,1,0:T(8,128)(2,1)S(1)} %get-tuple-element.107.rest_1_), channel_id=1, source_target_pairs={{0,4},{1,5},{2,6},{3,7},{4,0},{5,1},{6,2},{7,3},{8,12},{9,13},{10,... | collective-permute-start | bytes 884744 | tf_op jit(solution)/shard_map/ppermute | solution.py:1085
  134.3 17.0 %collective-permute-start.19 = (bf16[4,48,768]{2,1,0:T(8,128)(2,1)S(1)}, bf16[4,48,768]{2,1,0:T(8,128)(2,1)S(1)}, u32[]{:S(2)}, u32[]{:S(2)}) collective-permute-start(bf16[4,48,768]{2,1,0:T(8,128)(2,1)S(1)} %get-tuple-element.112.rest_0_), channel_id=1, source_target_pairs={{0,4},{1,5},{2,6},{3,7},{4,0},{5,1},{6,2},{7,3},{8,12},{9,13},{10,... | collective-permute-start | bytes 884744 | tf_op jit(solution)/shard_map/ppermute | solution.py:1085
  151.4 17.7 %collective-permute-start.21 = (bf16[2,48,768]{2,1,0:T(8,128)(2,1)S(1)}, bf16[2,48,768]{2,1,0:T(8,128)(2,1)S(1)}, u32[]{:S(2)}, u32[]{:S(2)}) collective-permute-start(bf16[2,48,768]{2,1,0:T(8,128)(2,1)S(1)} %get-tuple-element.117.rest_0_), channel_id=1, source_target_pairs={{0,16},{1,17},{2,18},{3,19},{4,20},{5,21},{6,22},{7,23},{8,24},{9,... | collective-permute-start | bytes 442376 | tf_op jit(solution)/shard_map/ppermute | solution.py:1085
  153.6 15.6 %collective-permute-start.22 = (bf16[2,48,768]{2,1,0:T(8,128)(2,1)S(1)}, bf16[2,48,768]{2,1,0:T(8,128)(2,1)S(1)}, u32[]{:S(2)}, u32[]{:S(2)}) collective-permute-start(bf16[2,48,768]{2,1,0:T(8,128)(2,1)S(1)} %get-tuple-element.118.rest_1_), channel_id=1, source_target_pairs={{0,8},{1,9},{2,10},{3,11},{4,12},{5,13},{6,14},{7,15},{8,0},{9,1},... | collective-permute-start | bytes 442376 | tf_op jit(solution)/shard_map/ppermute | solution.py:1085
  155.2 13.9 %copy-start.14 = (f32[4,16,384]{2,1,0:T(8,128)S(1)}, f32[4,16,384]{2,1,0:T(8,128)}, u32[]{:S(2)}) copy-start(f32[4,16,384]{2,1,0:T(8,128)} %get-tuple-element.120.sums2_ref) | copy-start | bytes 294916
  155.2 13.9 %copy-start.15 = (f32[16,768]{1,0:T(8,128)S(1)}, f32[16,768]{1,0:T(8,128)}, u32[]{:S(2)}) copy-start(f32[16,768]{1,0:T(8,128)} %get-tuple-element.121.db_ref) | copy-start | bytes 147460
  155.2 13.9 %collective-permute-start.23 = (bf16[2,48,768]{2,1,0:T(8,128)(2,1)S(1)}, bf16[2,48,768]{2,1,0:T(8,128)(2,1)S(1)}, u32[]{:S(2)}, u32[]{:S(2)}) collective-permute-start(bf16[2,48,768]{2,1,0:T(8,128)(2,1)S(1)} %get-tuple-element.119.rest_2_), channel_id=1, source_target_pairs={{0,24},{1,25},{2,26},{3,27},{4,28},{5,29},{6,30},{7,31},{8,16},{9,... | collective-permute-start | bytes 442376 | tf_op jit(solution)/shard_map/ppermute | solution.py:1085
  169.6 17.6 %copy-start.3 = (f32[48,768]{1,0:T(8,128)S(1)}, f32[48,768]{1,0:T(8,128)}, u32[]{:S(2)}) copy-start(f32[48,768]{1,0:T(8,128)} %refs_6_.1) | copy-start | bytes 442372
  169.6 17.7 %copy-start.4 = (f32[48,768]{1,0:T(8,128)S(1)}, f32[48,768]{1,0:T(8,128)}, u32[]{:S(2)}) copy-start(f32[48,768]{1,0:T(8,128)} %refs_7_.1) | copy-start | bytes 442372
  169.6 17.6 %copy-start.5 = (f32[48,768]{1,0:T(8,128)S(1)}, f32[48,768]{1,0:T(8,128)}, u32[]{:S(2)}) copy-start(f32[48,768]{1,0:T(8,128)} %refs_8_.1) | copy-start | bytes 442372
  169.6 17.6 %copy-start.6 = (f32[48,384]{1,0:T(8,128)S(1)}, f32[48,384]{1,0:T(8,128)}, u32[]{:S(2)}) copy-start(f32[48,384]{1,0:T(8,128)} %refs_0_.1) | copy-start | bytes 221188
  169.6 17.6 %copy-start.7 = (f32[48,384]{1,0:T(8,128)S(1)}, f32[48,384]{1,0:T(8,128)}, u32[]{:S(2)}) copy-start(f32[48,384]{1,0:T(8,128)} %refs_3_.3) | copy-start | bytes 221188
  169.6 17.6 %copy-start.8 = (f32[48,384]{1,0:T(8,128)S(1)}, f32[48,384]{1,0:T(8,128)}, u32[]{:S(2)}) copy-start(f32[48,384]{1,0:T(8,128)} %refs_1_.1) | copy-start | bytes 221188
  169.7 17.6 %copy-start.9 = (f32[48,384]{1,0:T(8,128)S(1)}, f32[48,384]{1,0:T(8,128)}, u32[]{:S(2)}) copy-start(f32[48,384]{1,0:T(8,128)} %refs_2_.3) | copy-start | bytes 221188
  169.7 17.6 %copy-start.10 = (f32[48,384]{1,0:T(8,128)S(1)}, f32[48,384]{1,0:T(8,128)}, u32[]{:S(2)}) copy-start(f32[48,384]{1,0:T(8,128)} %refs_4_.1) | copy-start | bytes 221188
  169.7 17.6 %copy-start.11 = (f32[48,384]{1,0:T(8,128)S(1)}, f32[48,384]{1,0:T(8,128)}, u32[]{:S(2)}) copy-start(f32[48,384]{1,0:T(8,128)} %refs_5_.1) | copy-start | bytes 221188
  169.7 4.2 %collective-permute-start.24 = (bf16[64,384]{1,0:T(8,128)(2,1)S(1)}, bf16[64,384]{1,0:T(8,128)(2,1)S(1)}, u32[]{:S(2)}, u32[]{:S(2)}) collective-permute-start(bf16[64,384]{1,0:T(8,128)(2,1)S(1)} %get-tuple-element.123.refs_0_), channel_id=1, source_target_pairs={{0,2},{1,3},{2,0},{3,1},{4,6},{5,7},{6,4},{7,5},{8,10},{9,11},{10,... | collective-permute-start | bytes 147464 | tf_op jit(solution)/shard_map/ppermute | solution.py:1085
  170.7 4.1 %collective-permute-start.25 = (bf16[64,384]{1,0:T(8,128)(2,1)S(1)}, bf16[64,384]{1,0:T(8,128)(2,1)S(1)}, u32[]{:S(2)}, u32[]{:S(2)}) collective-permute-start(bf16[64,384]{1,0:T(8,128)(2,1)S(1)} %get-tuple-element.123.refs_0_), channel_id=1, source_target_pairs={{0,4},{1,5},{2,6},{3,7},{4,0},{5,1},{6,2},{7,3},{8,12},{9,13},{10,... | collective-permute-start | bytes 147464 | tf_op jit(solution)/shard_map/ppermute | solution.py:1085
  171.8 5.0 %collective-permute-start.26 = (bf16[64,384]{1,0:T(8,128)(2,1)S(1)}, bf16[64,384]{1,0:T(8,128)(2,1)S(1)}, u32[]{:S(2)}, u32[]{:S(2)}) collective-permute-start(bf16[64,384]{1,0:T(8,128)(2,1)S(1)} %get-tuple-element.123.refs_0_), channel_id=1, source_target_pairs={{0,6},{1,7},{2,4},{3,5},{4,2},{5,3},{6,0},{7,1},{8,14},{9,15},{10,... | collective-permute-start | bytes 147464 | tf_op jit(solution)/shard_map/ppermute | solution.py:1085
  176.8 4.5 %collective-permute-start.27 = (bf16[64,384]{1,0:T(8,128)(2,1)S(1)}, bf16[64,384]{1,0:T(8,128)(2,1)S(1)}, u32[]{:S(2)}, u32[]{:S(2)}) collective-permute-start(bf16[64,384]{1,0:T(8,128)(2,1)S(1)} %shard_map.304.refs_0_), channel_id=1, source_target_pairs={{0,8},{1,9},{2,10},{3,11},{4,12},{5,13},{6,14},{7,15},{8,0},{9,1},... | collective-permute-start | bytes 147464 | tf_op jit(solution)/shard_map/ppermute | solution.py:1085
  177.9 5.5 %collective-permute-start.28 = (bf16[64,384]{1,0:T(8,128)(2,1)S(1)}, bf16[64,384]{1,0:T(8,128)(2,1)S(1)}, u32[]{:S(2)}, u32[]{:S(2)}) collective-permute-start(bf16[64,384]{1,0:T(8,128)(2,1)S(1)} %shard_map.304.refs_0_), channel_id=1, source_target_pairs={{0,16},{1,17},{2,18},{3,19},{4,20},{5,21},{6,22},{7,23},{8,24},{9,... | collective-permute-start | bytes 147464 | tf_op jit(solution)/shard_map/ppermute | solution.py:1085
  180.0 5.9 %collective-permute-start.29 = (bf16[64,384]{1,0:T(8,128)(2,1)S(1)}, bf16[64,384]{1,0:T(8,128)(2,1)S(1)}, u32[]{:S(2)}, u32[]{:S(2)}) collective-permute-start(bf16[64,384]{1,0:T(8,128)(2,1)S(1)} %shard_map.304.refs_0_), channel_id=1, source_target_pairs={{0,24},{1,25},{2,26},{3,27},{4,28},{5,29},{6,30},{7,31},{8,16},{9,... | collective-permute-start | bytes 147464 | tf_op jit(solution)/shard_map/ppermute | solution.py:1085
  185.9 1.3 collective-permute-start.30
  (4 other events, 6.5 us)

commit v4 on v3

--- a/solution.py
+++ b/solution.py
@@ -244,7 +244,7 @@
                 conv_ref[r, w, at, lanes] = acc[w]
             return 0
 
-        return tiles(h, imgs, tile, True)
+        return tiles(h, imgs, tile, begin == 0)
 
     every_row(begin, end, side, conv)
     gain = small_ref[GAIN_ONE : GAIN_ONE + 1, :][None]

time: 190 us -> 190 us (level)
  transfers between devices with their start and end apart: 31 -> 31, of which waited for: 14 -> 15; matrix products, arithmetic and copies ran while one was open for 1% -> 1% of each run, Pallas kernels for 49% -> 49%
where the time goes in v4:
time: 190 us
  Pallas kernels  127 us (67%)
  starting transfers between devices  37.9 us (20%)
  waiting for transfers between devices  18.9 us (10%)
  local copies, waits for them, and re-layouts  2.44 us (1%)
  between operations  1.97 us (1%)
    pallas_call x27, Pallas kernels, kernel_call(): pl.pallas_call(body, out_shape=tuple(out), in_specs=specs, out_specs=tupl...  126 us
    ppermute x31, starting transfers between devices, swap(): return lax.ppermute(x, 'dp', [(i, i ^ bit) for i in range(n)])  37.9 us
    ppermute x31, waiting for transfers between devices, swap(): return lax.ppermute(x, 'dp', [(i, i ^ bit) for i in range(n)])  18.9 us
  transfers between devices with their start and end apart: 31, of which 15 were waited for; matrix products, arithmetic and copies ran while one was open for 1% of the time, Pallas kernels for 49%

profile of v4, /device:TPU:0, one launch (start us, length us, event | category | flops | bytes accessed | tf_op | source)
XLA Modules:
  0.0 189.8 jit_solution(128810987958633245)
XLA Ops:
  0.7 0.8 convert_element_type.8
  1.4 2.9 %collective-permute-start = (bf16[744]{0:T(1024)(128)(2,1)S(1)}, bf16[744]{0:T(1024)(128)(2,1)S(1)}, u32[]{:S(2)}, u32[]{:S(2)}) collective-permute-start(bf16[744]{0:T(1024)(128)(2,1)S(1)} %convert_element_type.8), channel_id=1, source_target_pairs={{0,2},{1,3},{2,0},{3,1},{4,6},{5,7},{6,4},{7,5},{8,10},{9,11},{10,... | collective-permute-start | bytes 4472 | tf_op jit(solution)/shard_map/ppermute | solution.py:1085
  4.3 1.0 shard_map.280
  6.0 2.1 %collective-permute-start.1 = (bf16[2,744]{1,0:T(2,128)(2,1)S(1)}, bf16[2,744]{1,0:T(2,128)(2,1)S(1)}, u32[]{:S(2)}, u32[]{:S(2)}) collective-permute-start(bf16[2,744]{1,0:T(2,128)(2,1)S(1)} %pad_maximum_fusion.3), channel_id=1, source_target_pairs={{0,4},{1,5},{2,6},{3,7},{4,0},{5,1},{6,2},{7,3},{8,12},{9,13},{10,... | collective-permute-start | bytes 8936 | tf_op jit(solution)/shard_map/ppermute | solution.py:1085
  8.1 1.6 collective-permute-done.1
  9.7 2.1 %collective-permute-start.2 = (bf16[2,2,744]{2,1,0:T(2,128)(2,1)S(1)}, bf16[2,2,744]{2,1,0:T(2,128)(2,1)S(1)}, u32[]{:S(2)}, u32[]{:S(2)}) collective-permute-start(bf16[2,2,744]{2,1,0:T(2,128)(2,1)S(1)} %pad_maximum_fusion.2), channel_id=1, source_target_pairs={{0,8},{1,9},{2,10},{3,11},{4,12},{5,13},{6,14},{7,15},{8,0},{9,1},... | collective-permute-start | bytes 17864 | tf_op jit(solution)/shard_map/ppermute | solution.py:1085
  11.8 2.6 %collective-permute-start.3 = (bf16[1,48,768]{2,1,0:T(8,128)(2,1)S(1)}, bf16[1,48,768]{2,1,0:T(8,128)(2,1)S(1)}, u32[]{:S(2)}, u32[]{:S(2)}) collective-permute-start(bf16[1,48,768]{2,1,0:T(8,128)(2,1)S(1)} %get-tuple-element.75.first_ref), channel_id=1, source_target_pairs={{0,16},{1,17},{2,18},{3,19},{4,20},{5,21},{6,22},{7,23},{8,24},{9,... | collective-permute-start | bytes 221192 | tf_op jit(solution)/shard_map/ppermute | solution.py:1085
  14.8 3.4 %collective-permute-done.3.second_ref = bf16[1,48,768]{2,1,0:T(8,128)(2,1)S(1)} collective-permute-done((bf16[1,48,768]{2,1,0:T(8,128)(2,1)S(1)}, bf16[1,48,768]{2,1,0:T(8,128)(2,1)S(1)}, u32[]{:S(2)}, u32[]{:S(2)}) %collective-permute-start.3) | collective-permute-done | bytes 73760 | tf_op jit(solution)/shard_map/ppermute | solution.py:1085
  18.3 2.3 %collective-permute-start.4 = (bf16[2,2,2,744]{3,2,1,0:T(2,128)(2,1)S(1)}, bf16[2,2,2,744]{3,2,1,0:T(2,128)(2,1)S(1)}, u32[]{:S(2)}, u32[]{:S(2)}) collective-permute-start(bf16[2,2,2,744]{3,2,1,0:T(2,128)(2,1)S(1)} %pad_maximum_fusion.1), channel_id=1, source_target_pairs={{0,16},{1,17},{2,18},{3,19},{4,20},{5,21},{6,22},{7,23},{8,24},{9,... | collective-permute-start | bytes 35720 | tf_op jit(solution)/shard_map/ppermute | solution.py:1085
  20.6 2.0 %collective-permute-start.9 = (bf16[2,48,768]{2,1,0:T(8,128)(2,1)S(1)}, bf16[2,48,768]{2,1,0:T(8,128)(2,1)S(1)}, u32[]{:S(2)}, u32[]{:S(2)}) collective-permute-start(bf16[2,48,768]{2,1,0:T(8,128)(2,1)S(1)} %shard_map.285.first_ref), channel_id=1, source_target_pairs={{0,8},{1,9},{2,10},{3,11},{4,12},{5,13},{6,14},{7,15},{8,0},{9,1},... | collective-permute-start | bytes 442376 | tf_op jit(solution)/shard_map/ppermute | solution.py:1085
  23.7 1.4 collective-permute-start.7
  25.2 0.6 collective-permute-done.9.second_ref
  25.8 1.5 collective-permute-start.10
  27.5 0.8 reshape.99.refs_0_.small_hbm
  28.4 9.1 %shard_map.283 = (f32[14,14,16,384]{3,2,1,0:T(8,128)}, bf16[14,14,16,384]{3,2,1,0:T(8,128)(2,1)}, f32[14,14,16,1]{3,2,1,0:T(8,128)}, bf16[14,14,16,384]{3,2,1,0:T(8,128)(2,1)}, f32[8,128]{1,0:T(8,128)S(1)}) custom-call(f32[62,384]{1,0:T(8,128)} %reshape.99.refs_0_.small_hbm, bf16[14,14,16,384]{3,2,1,0:T(8,128)(2,1)} %bitcast.52, s32[16]{0:T(128)S(1)} %copy-done.12, ...), custom_call_target="tpu_custom_call" | custom-call | flops 7500000256 | tf_op jit(solution)/shard_map/pallas_call | solution.py:71
  37.6 1.6 collective-permute-start.12
  39.2 0.6 collective-permute-start.11
  39.8 12.8 %shard_map.288 = (bf16[14,14,16,384]{3,2,1,0:T(8,128)(2,1)}, f32[14,14,16,1]{3,2,1,0:T(8,128)}, bf16[14,14,16,384]{3,2,1,0:T(8,128)(2,1)}, f32[8,128]{1,0:T(8,128)S(1)}) custom-call(f32[62,384]{1,0:T(8,128)} %reshape.99.refs_0_.small_hbm, ...), custom_call_target="tpu_custom_call", output_to_operand_aliasing={{0}: (2, {}), {1}: (3, {}), {2}: (4, {})} | custom-call | flops 13500000256 | tf_op jit(solution)/shard_map/pallas_call | solution.py:71
  53.5 5.2 %shard_map.291 = (bf16[14,14,16,384]{3,2,1,0:T(8,128)(2,1)}, f32[14,14,16,1]{3,2,1,0:T(8,128)}, bf16[14,14,16,384]{3,2,1,0:T(8,128)(2,1)}, f32[8,128]{1,0:T(8,128)}) custom-call(f32[62,384]{1,0:T(8,128)} %reshape.99.refs_0_.small_hbm, ...), custom_call_target="tpu_custom_call", output_to_operand_aliasing={{0}: (2, {}), {1}: (3, {}), {2}: (4, {})} | custom-call | flops 3000000000 | tf_op jit(solution)/shard_map/pallas_call | solution.py:71
  58.7 1.1 copy-done.20
  60.1 31.5 %shard_map.292 = (bf16[3136,1536]{1,0:T(8,128)(2,1)}, bf16[3136,1536]{1,0:T(8,128)(2,1)}, bf16[768,768]{1,0:T(8,128)(2,1)}, bf16[768,768]{1,0:T(8,128)(2,1)}, f3...) custom-call(s32[1]{0:T(128)} %bitcast.me_ref, ...), custom_call_target="tpu_custom_call" | custom-call | flops 33999998976 | tf_op jit(solution)/shard_map/pallas_call | solution.py:71
  92.1 12.1 %shard_map.293 = (bf16[768,768]{1,0:T(8,128)(2,1)S(1)}, f32[16,768]{1,0:T(8,128)S(1)}, bf16[3136,768]{1,0:T(8,128)(2,1)}) custom-call(s32[1]{0:T(128)} %bitcast.me_ref, bf16[3136,384]{1,0:T(8,128)(2,1)} %bitcast.63, bf16[3136,1536]{1,0:T(8,128)(2,1)} %get-tuple-element.92.act_hbm, bf16[3136,1536]{1,0:T(8,128)(2,1)} %get-tuple-element.93.dg_hbm, ...), custom_call_target="tpu_custom_call" | custom-call | flops 12999999488 | tf_op jit(solution)/shard_map/pallas_call | solution.py:71
  104.8 1.6 collective-permute-start.17
  106.3 11.8 %shard_map.295 = (bf16[768,768]{1,0:T(8,128)(2,1)S(1)}, f32[16,768]{1,0:T(8,128)S(1)}, bf16[3136,768]{1,0:T(8,128)(2,1)}) custom-call(s32[1]{0:T(128)} %bitcast.me_ref, bf16[3136,384]{1,0:T(8,128)(2,1)} %bitcast.64, bf16[3136,1536]{1,0:T(8,128)(2,1)} %get-tuple-element.92.act_hbm, bf16[3136,1536]{1,0:T(8,128)(2,1)} %get-tuple-element.93.dg_hbm, ...), custom_call_target="tpu_custom_call" | custom-call | flops 12999999488 | tf_op jit(solution)/shard_map/pallas_call | solution.py:71
  119.0 1.3 collective-permute-done.17.refs_1_
  120.4 1.3 collective-permute-start.20
  121.7 11.0 %shard_map.298 = (bf16[3136,384]{1,0:T(8,128)(2,1)}, f32[3,16,384]{2,1,0:T(8,128)S(1)}) custom-call(s32[1]{0:T(128)} %bitcast.me_ref, bf16[3136,768]{1,0:T(8,128)(2,1)} %get-tuple-element.98.pnear_hbm, bf16[3136,768]{1,0:T(8,128)(2,1)} %get-tuple-element.99.pfar_hbm, bf16[3136,384]{1,0:T(8,128)(2,1)} %bitcast.47, f32[3136,1]{1,0:T(8,128)} %bitcast.51, ...), custom_call_target="tpu_custom_call" | custom-call | flops 11000000512 | tf_op jit(solution)/shard_map/pallas_call | solution.py:71
  132.7 1.0 collective-permute-done.18.refs_1_
  133.8 0.8 collective-permute-start.19
  134.6 16.4 %shard_map.300 = (f32[14,14,16,384]{3,2,1,0:T(8,128)}, f32[8,128]{1,0:T(8,128)S(1)}) custom-call(bf16[14,14,16,384]{3,2,1,0:T(8,128)(2,1)} %bitcast.61, f32[62,384]{1,0:T(8,128)} %reshape.99.refs_0_.small_hbm, s32[16]{0:T(128)S(1)} %copy-done.12, f32[16]{0:T(128)S(1)} %copy-done.13, bf16[14,14,16,384]{3,2,1,0:T(8,128)(2,1)} %bitcast.60, ...), custom_call_target="tpu_custom_call" | custom-call | flops 22000001024 | tf_op jit(solution)/shard_map/pallas_call | solution.py:71
  151.2 2.1 %collective-permute-start.21 = (bf16[2,48,768]{2,1,0:T(8,128)(2,1)S(1)}, bf16[2,48,768]{2,1,0:T(8,128)(2,1)S(1)}, u32[]{:S(2)}, u32[]{:S(2)}) collective-permute-start(bf16[2,48,768]{2,1,0:T(8,128)(2,1)S(1)} %get-tuple-element.117.rest_0_), channel_id=1, source_target_pairs={{0,16},{1,17},{2,18},{3,19},{4,20},{5,21},{6,22},{7,23},{8,24},{9,... | collective-permute-start | bytes 442376 | tf_op jit(solution)/shard_map/ppermute | solution.py:1085
  153.3 1.7 collective-permute-start.22
  155.0 0.9 collective-permute-start.23
  155.9 13.0 %shard_map.302.gk_ref = f32[49,8,384]{2,1,0:T(8,128)S(1)} custom-call(bf16[14,14,16,384]{3,2,1,0:T(8,128)(2,1)} %bitcast.62, f32[14,14,16,384]{3,2,1,0:T(8,128)} %get-tuple-element.79.refs_1_.mixed_hbm, bf16[2,48,768]{2,1,0:T(8,128)(2,1)S(1)} %get-tuple-element.117.rest_0_, bf16[2,48,768]{2,1,0:T(8,128)(2,1)S(1)} %get-tuple-element.118.rest_1_, ...), custom_call_target="tpu_custom_call" | custom-call | flops 14099999744 | tf_op jit(solution)/shard_map/pallas_call | solution.py:71
  169.4 1.0 collective-permute-start.24
  170.5 0.8 collective-permute-start.25
  171.3 1.7 collective-permute-start.26
  173.0 0.6 collective-permute-done.24.refs_1_
  173.6 1.0 collective-permute-done.25.refs_2_
  174.6 1.7 collective-permute-done.26.refs_3_
  176.3 1.1 collective-permute-start.27
  177.4 2.3 %collective-permute-start.28 = (bf16[64,384]{1,0:T(8,128)(2,1)S(1)}, bf16[64,384]{1,0:T(8,128)(2,1)S(1)}, u32[]{:S(2)}, u32[]{:S(2)}) collective-permute-start(bf16[64,384]{1,0:T(8,128)(2,1)S(1)} %shard_map.304.refs_0_), channel_id=1, source_target_pairs={{0,16},{1,17},{2,18},{3,19},{4,20},{5,21},{6,22},{7,23},{8,24},{9,... | collective-permute-start | bytes 147464 | tf_op jit(solution)/shard_map/ppermute | solution.py:1085
  179.7 1.0 collective-permute-start.29
  180.9 2.0 %collective-permute-done.28.refs_2_ = bf16[64,384]{1,0:T(8,128)(2,1)S(1)} collective-permute-done((bf16[64,384]{1,0:T(8,128)(2,1)S(1)}, bf16[64,384]{1,0:T(8,128)(2,1)S(1)}, u32[]{:S(2)}, u32[]{:S(2)}) %collective-permute-start.28) | collective-permute-done | bytes 49184 | tf_op jit(solution)/shard_map/ppermute | solution.py:1085
  182.9 2.7 %collective-permute-done.29.refs_3_ = bf16[64,384]{1,0:T(8,128)(2,1)S(1)} collective-permute-done((bf16[64,384]{1,0:T(8,128)(2,1)S(1)}, bf16[64,384]{1,0:T(8,128)(2,1)S(1)}, u32[]{:S(2)}, u32[]{:S(2)}) %collective-permute-start.29) | collective-permute-done | bytes 49184 | tf_op jit(solution)/shard_map/ppermute | solution.py:1085
  185.7 1.2 collective-permute-done.30.refs_1_
  187.1 1.3 shard_map.307
  189.1 0.7 multiply_subtract_fusion
  (101 shorter events, 6.5 us)
Async XLA Ops:
  0.6 5.3 %copy-start.16 = (f32[744]{0:T(1024)S(1)}, f32[744]{0:T(1024)}, u32[]{:S(2)}) copy-start(f32[744]{0:T(1024)} %param.25) | copy-start | bytes 8932
  1.4 4.5 %collective-permute-start = (bf16[744]{0:T(1024)(128)(2,1)S(1)}, bf16[744]{0:T(1024)(128)(2,1)S(1)}, u32[]{:S(2)}, u32[]{:S(2)}) collective-permute-start(bf16[744]{0:T(1024)(128)(2,1)S(1)} %convert_element_type.8), channel_id=1, source_target_pairs={{0,2},{1,3},{2,0},{3,1},{4,6},{5,7},{6,4},{7,5},{8,10},{9,11},{10,... | collective-permute-start | bytes 4472 | tf_op jit(solution)/shard_map/ppermute | solution.py:1085
  6.0 3.7 %collective-permute-start.1 = (bf16[2,744]{1,0:T(2,128)(2,1)S(1)}, bf16[2,744]{1,0:T(2,128)(2,1)S(1)}, u32[]{:S(2)}, u32[]{:S(2)}) collective-permute-start(bf16[2,744]{1,0:T(2,128)(2,1)S(1)} %pad_maximum_fusion.3), channel_id=1, source_target_pairs={{0,4},{1,5},{2,6},{3,7},{4,0},{5,1},{6,2},{7,3},{8,12},{9,13},{10,... | collective-permute-start | bytes 8936 | tf_op jit(solution)/shard_map/ppermute | solution.py:1085
  9.7 5.1 %collective-permute-start.2 = (bf16[2,2,744]{2,1,0:T(2,128)(2,1)S(1)}, bf16[2,2,744]{2,1,0:T(2,128)(2,1)S(1)}, u32[]{:S(2)}, u32[]{:S(2)}) collective-permute-start(bf16[2,2,744]{2,1,0:T(2,128)(2,1)S(1)} %pad_maximum_fusion.2), channel_id=1, source_target_pairs={{0,8},{1,9},{2,10},{3,11},{4,12},{5,13},{6,14},{7,15},{8,0},{9,1},... | collective-permute-start | bytes 17864 | tf_op jit(solution)/shard_map/ppermute | solution.py:1085
  11.8 6.3 %collective-permute-start.3 = (bf16[1,48,768]{2,1,0:T(8,128)(2,1)S(1)}, bf16[1,48,768]{2,1,0:T(8,128)(2,1)S(1)}, u32[]{:S(2)}, u32[]{:S(2)}) collective-permute-start(bf16[1,48,768]{2,1,0:T(8,128)(2,1)S(1)} %get-tuple-element.75.first_ref), channel_id=1, source_target_pairs={{0,16},{1,17},{2,18},{3,19},{4,20},{5,21},{6,22},{7,23},{8,24},{9,... | collective-permute-start | bytes 221192 | tf_op jit(solution)/shard_map/ppermute | solution.py:1085
  14.4 6.1 %collective-permute-start.8 = (bf16[1,48,768]{2,1,0:T(8,128)(2,1)S(1)}, bf16[1,48,768]{2,1,0:T(8,128)(2,1)S(1)}, u32[]{:S(2)}, u32[]{:S(2)}) collective-permute-start(bf16[1,48,768]{2,1,0:T(8,128)(2,1)S(1)} %get-tuple-element.84.first_ref), channel_id=1, source_target_pairs={{0,16},{1,17},{2,18},{3,19},{4,20},{5,21},{6,22},{7,23},{8,24},{9,... | collective-permute-start | bytes 221192 | tf_op jit(solution)/shard_map/ppermute | solution.py:1085
  18.2 5.5 %collective-permute-start.5 = (bf16[2,48,768]{2,1,0:T(8,128)(2,1)S(1)}, bf16[2,48,768]{2,1,0:T(8,128)(2,1)S(1)}, u32[]{:S(2)}, u32[]{:S(2)}) collective-permute-start(bf16[2,48,768]{2,1,0:T(8,128)(2,1)S(1)} %shard_map.281.first_ref), channel_id=1, source_target_pairs={{0,8},{1,9},{2,10},{3,11},{4,12},{5,13},{6,14},{7,15},{8,0},{9,1},... | collective-permute-start | bytes 442376 | tf_op jit(solution)/shard_map/ppermute | solution.py:1085
  18.3 4.8 %collective-permute-start.4 = (bf16[2,2,2,744]{3,2,1,0:T(2,128)(2,1)S(1)}, bf16[2,2,2,744]{3,2,1,0:T(2,128)(2,1)S(1)}, u32[]{:S(2)}, u32[]{:S(2)}) collective-permute-start(bf16[2,2,2,744]{3,2,1,0:T(2,128)(2,1)S(1)} %pad_maximum_fusion.1), channel_id=1, source_target_pairs={{0,16},{1,17},{2,18},{3,19},{4,20},{5,21},{6,22},{7,23},{8,24},{9,... | collective-permute-start | bytes 35720 | tf_op jit(solution)/shard_map/ppermute | solution.py:1085
  20.6 5.2 %collective-permute-start.9 = (bf16[2,48,768]{2,1,0:T(8,128)(2,1)S(1)}, bf16[2,48,768]{2,1,0:T(8,128)(2,1)S(1)}, u32[]{:S(2)}, u32[]{:S(2)}) collective-permute-start(bf16[2,48,768]{2,1,0:T(8,128)(2,1)S(1)} %shard_map.285.first_ref), channel_id=1, source_target_pairs={{0,8},{1,9},{2,10},{3,11},{4,12},{5,13},{6,14},{7,15},{8,0},{9,1},... | collective-permute-start | bytes 442376 | tf_op jit(solution)/shard_map/ppermute | solution.py:1085
  23.7 4.6 %copy-start.12 = (s32[16]{0:T(128)S(1)}, s32[16]{0:T(128)}, u32[]{:S(2)}) copy-start(s32[16]{0:T(128)} %partner_ref.1) | copy-start | bytes 196
  23.7 4.6 %copy-start.13 = (f32[16]{0:T(128)S(1)}, f32[16]{0:T(128)}, u32[]{:S(2)}) copy-start(f32[16]{0:T(128)} %weight_ref.1) | copy-start | bytes 196
  23.7 15.4 %collective-permute-start.7 = (bf16[4,48,768]{2,1,0:T(8,128)(2,1)S(1)}, bf16[4,48,768]{2,1,0:T(8,128)(2,1)S(1)}, u32[]{:S(2)}, u32[]{:S(2)}) collective-permute-start(bf16[4,48,768]{2,1,0:T(8,128)(2,1)S(1)} %shard_map.282.first_ref), channel_id=1, source_target_pairs={{0,4},{1,5},{2,6},{3,7},{4,0},{5,1},{6,2},{7,3},{8,12},{9,13},{10,... | collective-permute-start | bytes 884744 | tf_op jit(solution)/shard_map/ppermute | solution.py:1085
  25.2 2.2 %collective-permute-start.6 = (bf16[2,2,2,2,744]{4,3,2,1,0:T(2,128)(2,1)S(1)}, bf16[2,2,2,2,744]{4,3,2,1,0:T(2,128)(2,1)S(1)}, u32[]{:S(2)}, u32[]{:S(2)}) collective-permute-start(bf16[2,2,2,2,744]{4,3,2,1,0:T(2,128)(2,1)S(1)} %pad_maximum_fusion), channel_id=1, source_target_pairs={{0,1},{1,0},{2,3},{3,2},{4,5},{5,4},{6,7},{7,6},{8,9},{9,8},{10,11... | collective-permute-start | bytes 71432 | tf_op jit(solution)/shard_map/ppermute | solution.py:1085
  25.8 11.7 %collective-permute-start.10 = (bf16[4,48,768]{2,1,0:T(8,128)(2,1)S(1)}, bf16[4,48,768]{2,1,0:T(8,128)(2,1)S(1)}, u32[]{:S(2)}, u32[]{:S(2)}) collective-permute-start(bf16[4,48,768]{2,1,0:T(8,128)(2,1)S(1)} %shard_map.286.first_ref), channel_id=1, source_target_pairs={{0,2},{1,3},{2,0},{3,1},{4,6},{5,7},{6,4},{7,5},{8,10},{9,11},{10,... | collective-permute-start | bytes 884744 | tf_op jit(solution)/shard_map/ppermute | solution.py:1085
  37.6 15.1 %collective-permute-start.12 = (bf16[8,48,768]{2,1,0:T(8,128)(2,1)S(1)}, bf16[8,48,768]{2,1,0:T(8,128)(2,1)S(1)}, u32[]{:S(2)}, u32[]{:S(2)}) collective-permute-start(bf16[8,48,768]{2,1,0:T(8,128)(2,1)S(1)} %shard_map.287.refs_6_.first_ref), channel_id=1, source_target_pairs={{0,4},{1,5},{2,6},{3,7},{4,0},{5,1},{6,2},{7,3},{8,12},{9,13},{10,... | collective-permute-start | bytes 1769480 | tf_op jit(solution)/shard_map/ppermute | solution.py:1085
  39.2 13.7 %collective-permute-start.11 = (bf16[8,48,768]{2,1,0:T(8,128)(2,1)S(1)}, bf16[8,48,768]{2,1,0:T(8,128)(2,1)S(1)}, u32[]{:S(2)}, u32[]{:S(2)}) collective-permute-start(bf16[8,48,768]{2,1,0:T(8,128)(2,1)S(1)} %shard_map.284.refs_5_.first_ref), channel_id=1, source_target_pairs={{0,2},{1,3},{2,0},{3,1},{4,6},{5,7},{6,4},{7,5},{8,10},{9,11},{10,... | collective-permute-start | bytes 1769480 | tf_op jit(solution)/shard_map/ppermute | solution.py:1085
  52.7 6.0 %copy-start.1 = (bf16[16,48,768]{2,1,0:T(8,128)(2,1)}, bf16[16,48,768]{2,1,0:T(8,128)(2,1)S(1)}, u32[]{:S(2)}) copy-start(bf16[16,48,768]{2,1,0:T(8,128)(2,1)S(1)} %shard_map.290.refs_6_) | copy-start | bytes 3538948
  52.7 6.0 %collective-permute-start.14 = (bf16[16,48,768]{2,1,0:T(8,128)(2,1)S(1)}, bf16[16,48,768]{2,1,0:T(8,128)(2,1)S(1)}, u32[]{:S(2)}, u32[]{:S(2)}) collective-permute-start(bf16[16,48,768]{2,1,0:T(8,128)(2,1)S(1)} %shard_map.290.refs_6_), channel_id=1, source_target_pairs={{0,1},{1,0},{2,3},{3,2},{4,5},{5,4},{6,7},{7,6},{8,9},{9,8},{10,11... | collective-permute-start | bytes 3538952 | tf_op jit(solution)/shard_map/ppermute | solution.py:1085
  52.9 5.8 %copy-start = (bf16[16,48,768]{2,1,0:T(8,128)(2,1)}, bf16[16,48,768]{2,1,0:T(8,128)(2,1)S(1)}, u32[]{:S(2)}) copy-start(bf16[16,48,768]{2,1,0:T(8,128)(2,1)S(1)} %shard_map.289.refs_5_) | copy-start | bytes 3538948
  52.9 5.8 %collective-permute-start.13 = (bf16[16,48,768]{2,1,0:T(8,128)(2,1)S(1)}, bf16[16,48,768]{2,1,0:T(8,128)(2,1)S(1)}, u32[]{:S(2)}, u32[]{:S(2)}) collective-permute-start(bf16[16,48,768]{2,1,0:T(8,128)(2,1)S(1)} %shard_map.289.refs_5_), channel_id=1, source_target_pairs={{0,1},{1,0},{2,3},{3,2},{4,5},{5,4},{6,7},{7,6},{8,9},{9,8},{10,11... | collective-permute-start | bytes 3538952 | tf_op jit(solution)/shard_map/ppermute | solution.py:1085
  91.7 12.8 %collective-permute-start.15 = (bf16[16,48,768]{2,1,0:T(8,128)(2,1)}, bf16[16,48,768]{2,1,0:T(8,128)(2,1)S(1)}, u32[]{:S(2)}, u32[]{:S(2)}) collective-permute-start(bf16[16,48,768]{2,1,0:T(8,128)(2,1)} %bitcast.58), channel_id=1, source_target_pairs={{0,1},{1,0},{2,3},{3,2},{4,5},{5,4},{6,7},{7,6},{8,9},{9,8},{10,11... | collective-permute-start | bytes 3538952 | tf_op jit(solution)/shard_map/ppermute | solution.py:1085
  92.1 12.5 %copy-start.2 = (bf16[768,768]{1,0:T(8,128)(2,1)S(1)}, bf16[768,768]{1,0:T(8,128)(2,1)}, u32[]{:S(2)}) copy-start(bf16[768,768]{1,0:T(8,128)(2,1)} %get-tuple-element.94) | copy-start | bytes 3538948
  104.2 14.0 %collective-permute-start.16 = (bf16[16,48,768]{2,1,0:T(8,128)(2,1)S(1)}, bf16[16,48,768]{2,1,0:T(8,128)(2,1)S(1)}, u32[]{:S(2)}, u32[]{:S(2)}) collective-permute-start(bf16[16,48,768]{2,1,0:T(8,128)(2,1)S(1)} %bitcast.45), channel_id=1, source_target_pairs={{0,1},{1,0},{2,3},{3,2},{4,5},{5,4},{6,7},{7,6},{8,9},{9,8},{10,11... | collective-permute-start | bytes 3538952 | tf_op jit(solution)/shard_map/ppermute | solution.py:1085
  104.8 15.6 %collective-permute-start.17 = (bf16[8,48,768]{2,1,0:T(8,128)(2,1)S(1)}, bf16[8,48,768]{2,1,0:T(8,128)(2,1)S(1)}, u32[]{:S(2)}, u32[]{:S(2)}) collective-permute-start(bf16[8,48,768]{2,1,0:T(8,128)(2,1)S(1)} %get-tuple-element.97.rest_0_), channel_id=1, source_target_pairs={{0,2},{1,3},{2,0},{3,1},{4,6},{5,7},{6,4},{7,5},{8,10},{9,11},{10,... | collective-permute-start | bytes 1769480 | tf_op jit(solution)/shard_map/ppermute | solution.py:1085
  118.5 15.3 %collective-permute-start.18 = (bf16[8,48,768]{2,1,0:T(8,128)(2,1)S(1)}, bf16[8,48,768]{2,1,0:T(8,128)(2,1)S(1)}, u32[]{:S(2)}, u32[]{:S(2)}) collective-permute-start(bf16[8,48,768]{2,1,0:T(8,128)(2,1)S(1)} %get-tuple-element.105.rest_0_), channel_id=1, source_target_pairs={{0,2},{1,3},{2,0},{3,1},{4,6},{5,7},{6,4},{7,5},{8,10},{9,11},{10,... | collective-permute-start | bytes 1769480 | tf_op jit(solution)/shard_map/ppermute | solution.py:1085
  120.4 30.6 %collective-permute-start.20 = (bf16[4,48,768]{2,1,0:T(8,128)(2,1)S(1)}, bf16[4,48,768]{2,1,0:T(8,128)(2,1)S(1)}, u32[]{:S(2)}, u32[]{:S(2)}) collective-permute-start(bf16[4,48,768]{2,1,0:T(8,128)(2,1)S(1)} %get-tuple-element.107.rest_1_), channel_id=1, source_target_pairs={{0,4},{1,5},{2,6},{3,7},{4,0},{5,1},{6,2},{7,3},{8,12},{9,13},{10,... | collective-permute-start | bytes 884744 | tf_op jit(solution)/shard_map/ppermute | solution.py:1085
  133.8 17.2 %collective-permute-start.19 = (bf16[4,48,768]{2,1,0:T(8,128)(2,1)S(1)}, bf16[4,48,768]{2,1,0:T(8,128)(2,1)S(1)}, u32[]{:S(2)}, u32[]{:S(2)}) collective-permute-start(bf16[4,48,768]{2,1,0:T(8,128)(2,1)S(1)} %get-tuple-element.112.rest_0_), channel_id=1, source_target_pairs={{0,4},{1,5},{2,6},{3,7},{4,0},{5,1},{6,2},{7,3},{8,12},{9,13},{10,... | collective-permute-start | bytes 884744 | tf_op jit(solution)/shard_map/ppermute | solution.py:1085
  151.2 17.7 %collective-permute-start.21 = (bf16[2,48,768]{2,1,0:T(8,128)(2,1)S(1)}, bf16[2,48,768]{2,1,0:T(8,128)(2,1)S(1)}, u32[]{:S(2)}, u32[]{:S(2)}) collective-permute-start(bf16[2,48,768]{2,1,0:T(8,128)(2,1)S(1)} %get-tuple-element.117.rest_0_), channel_id=1, source_target_pairs={{0,16},{1,17},{2,18},{3,19},{4,20},{5,21},{6,22},{7,23},{8,24},{9,... | collective-permute-start | bytes 442376 | tf_op jit(solution)/shard_map/ppermute | solution.py:1085
  153.3 15.6 %collective-permute-start.22 = (bf16[2,48,768]{2,1,0:T(8,128)(2,1)S(1)}, bf16[2,48,768]{2,1,0:T(8,128)(2,1)S(1)}, u32[]{:S(2)}, u32[]{:S(2)}) collective-permute-start(bf16[2,48,768]{2,1,0:T(8,128)(2,1)S(1)} %get-tuple-element.118.rest_1_), channel_id=1, source_target_pairs={{0,8},{1,9},{2,10},{3,11},{4,12},{5,13},{6,14},{7,15},{8,0},{9,1},... | collective-permute-start | bytes 442376 | tf_op jit(solution)/shard_map/ppermute | solution.py:1085
  155.0 13.9 %copy-start.14 = (f32[4,16,384]{2,1,0:T(8,128)S(1)}, f32[4,16,384]{2,1,0:T(8,128)}, u32[]{:S(2)}) copy-start(f32[4,16,384]{2,1,0:T(8,128)} %get-tuple-element.120.sums2_ref) | copy-start | bytes 294916
  155.0 13.9 %copy-start.15 = (f32[16,768]{1,0:T(8,128)S(1)}, f32[16,768]{1,0:T(8,128)}, u32[]{:S(2)}) copy-start(f32[16,768]{1,0:T(8,128)} %get-tuple-element.121.db_ref) | copy-start | bytes 147460
  155.0 13.9 %collective-permute-start.23 = (bf16[2,48,768]{2,1,0:T(8,128)(2,1)S(1)}, bf16[2,48,768]{2,1,0:T(8,128)(2,1)S(1)}, u32[]{:S(2)}, u32[]{:S(2)}) collective-permute-start(bf16[2,48,768]{2,1,0:T(8,128)(2,1)S(1)} %get-tuple-element.119.rest_2_), channel_id=1, source_target_pairs={{0,24},{1,25},{2,26},{3,27},{4,28},{5,29},{6,30},{7,31},{8,16},{9,... | collective-permute-start | bytes 442376 | tf_op jit(solution)/shard_map/ppermute | solution.py:1085
  169.3 17.7 %copy-start.3 = (f32[48,768]{1,0:T(8,128)S(1)}, f32[48,768]{1,0:T(8,128)}, u32[]{:S(2)}) copy-start(f32[48,768]{1,0:T(8,128)} %refs_6_.1) | copy-start | bytes 442372
  169.3 17.7 %copy-start.4 = (f32[48,768]{1,0:T(8,128)S(1)}, f32[48,768]{1,0:T(8,128)}, u32[]{:S(2)}) copy-start(f32[48,768]{1,0:T(8,128)} %refs_7_.1) | copy-start | bytes 442372
  169.4 17.7 %copy-start.5 = (f32[48,768]{1,0:T(8,128)S(1)}, f32[48,768]{1,0:T(8,128)}, u32[]{:S(2)}) copy-start(f32[48,768]{1,0:T(8,128)} %refs_8_.1) | copy-start | bytes 442372
  169.4 17.7 %copy-start.6 = (f32[48,384]{1,0:T(8,128)S(1)}, f32[48,384]{1,0:T(8,128)}, u32[]{:S(2)}) copy-start(f32[48,384]{1,0:T(8,128)} %refs_0_.1) | copy-start | bytes 221188
  169.4 17.7 %copy-start.7 = (f32[48,384]{1,0:T(8,128)S(1)}, f32[48,384]{1,0:T(8,128)}, u32[]{:S(2)}) copy-start(f32[48,384]{1,0:T(8,128)} %refs_3_.3) | copy-start | bytes 221188
  169.4 17.6 %copy-start.8 = (f32[48,384]{1,0:T(8,128)S(1)}, f32[48,384]{1,0:T(8,128)}, u32[]{:S(2)}) copy-start(f32[48,384]{1,0:T(8,128)} %refs_1_.1) | copy-start | bytes 221188
  169.4 17.6 %copy-start.9 = (f32[48,384]{1,0:T(8,128)S(1)}, f32[48,384]{1,0:T(8,128)}, u32[]{:S(2)}) copy-start(f32[48,384]{1,0:T(8,128)} %refs_2_.3) | copy-start | bytes 221188
  169.4 17.6 %copy-start.10 = (f32[48,384]{1,0:T(8,128)S(1)}, f32[48,384]{1,0:T(8,128)}, u32[]{:S(2)}) copy-start(f32[48,384]{1,0:T(8,128)} %refs_4_.1) | copy-start | bytes 221188
  169.4 17.6 %copy-start.11 = (f32[48,384]{1,0:T(8,128)S(1)}, f32[48,384]{1,0:T(8,128)}, u32[]{:S(2)}) copy-start(f32[48,384]{1,0:T(8,128)} %refs_5_.1) | copy-start | bytes 221188
  169.4 4.2 %collective-permute-start.24 = (bf16[64,384]{1,0:T(8,128)(2,1)S(1)}, bf16[64,384]{1,0:T(8,128)(2,1)S(1)}, u32[]{:S(2)}, u32[]{:S(2)}) collective-permute-start(bf16[64,384]{1,0:T(8,128)(2,1)S(1)} %get-tuple-element.123.refs_0_), channel_id=1, source_target_pairs={{0,2},{1,3},{2,0},{3,1},{4,6},{5,7},{6,4},{7,5},{8,10},{9,11},{10,... | collective-permute-start | bytes 147464 | tf_op jit(solution)/shard_map/ppermute | solution.py:1085
  170.5 4.1 %collective-permute-start.25 = (bf16[64,384]{1,0:T(8,128)(2,1)S(1)}, bf16[64,384]{1,0:T(8,128)(2,1)S(1)}, u32[]{:S(2)}, u32[]{:S(2)}) collective-permute-start(bf16[64,384]{1,0:T(8,128)(2,1)S(1)} %get-tuple-element.123.refs_0_), channel_id=1, source_target_pairs={{0,4},{1,5},{2,6},{3,7},{4,0},{5,1},{6,2},{7,3},{8,12},{9,13},{10,... | collective-permute-start | bytes 147464 | tf_op jit(solution)/shard_map/ppermute | solution.py:1085
  171.3 5.0 %collective-permute-start.26 = (bf16[64,384]{1,0:T(8,128)(2,1)S(1)}, bf16[64,384]{1,0:T(8,128)(2,1)S(1)}, u32[]{:S(2)}, u32[]{:S(2)}) collective-permute-start(bf16[64,384]{1,0:T(8,128)(2,1)S(1)} %get-tuple-element.123.refs_0_), channel_id=1, source_target_pairs={{0,6},{1,7},{2,4},{3,5},{4,2},{5,3},{6,0},{7,1},{8,14},{9,15},{10,... | collective-permute-start | bytes 147464 | tf_op jit(solution)/shard_map/ppermute | solution.py:1085
  176.3 4.6 %collective-permute-start.27 = (bf16[64,384]{1,0:T(8,128)(2,1)S(1)}, bf16[64,384]{1,0:T(8,128)(2,1)S(1)}, u32[]{:S(2)}, u32[]{:S(2)}) collective-permute-start(bf16[64,384]{1,0:T(8,128)(2,1)S(1)} %shard_map.304.refs_0_), channel_id=1, source_target_pairs={{0,8},{1,9},{2,10},{3,11},{4,12},{5,13},{6,14},{7,15},{8,0},{9,1},... | collective-permute-start | bytes 147464 | tf_op jit(solution)/shard_map/ppermute | solution.py:1085
  177.4 5.5 %collective-permute-start.28 = (bf16[64,384]{1,0:T(8,128)(2,1)S(1)}, bf16[64,384]{1,0:T(8,128)(2,1)S(1)}, u32[]{:S(2)}, u32[]{:S(2)}) collective-permute-start(bf16[64,384]{1,0:T(8,128)(2,1)S(1)} %shard_map.304.refs_0_), channel_id=1, source_target_pairs={{0,16},{1,17},{2,18},{3,19},{4,20},{5,21},{6,22},{7,23},{8,24},{9,... | collective-permute-start | bytes 147464 | tf_op jit(solution)/shard_map/ppermute | solution.py:1085
  179.7 5.9 %collective-permute-start.29 = (bf16[64,384]{1,0:T(8,128)(2,1)S(1)}, bf16[64,384]{1,0:T(8,128)(2,1)S(1)}, u32[]{:S(2)}, u32[]{:S(2)}) collective-permute-start(bf16[64,384]{1,0:T(8,128)(2,1)S(1)} %shard_map.304.refs_0_), channel_id=1, source_target_pairs={{0,24},{1,25},{2,26},{3,27},{4,28},{5,29},{6,30},{7,31},{8,16},{9,... | collective-permute-start | bytes 147464 | tf_op jit(solution)/shard_map/ppermute | solution.py:1085
  185.7 1.3 collective-permute-start.30
  (4 other events, 6.5 us)
